TPU v7x, 32 devices: a whole 2x2x4 slice. The times are simulated.
32 devices in a mesh: row: 8 (over y, x, core), col: 4 (over z).
Axes of the slice: x: 2, y: 2, z: 4, core: 2. Of those that a mesh axis runs over, the one named last changes fastest.
Arguments:
- high_vectors: float32 [16384, 4096], P('row', 'col'), may hold values from -0.046875 to 0.046875
- high_values: float32 [4096], P('col'), may hold values from 2 to 4
- pool_vectors: float32 [16384, 512], P('row', 'col'), may hold values from -6 to 6
- pool_images: float32 [16384, 512], P('row', 'col'), may hold values from -6 to 6
- pool_values: float32 [512], replicated, may hold values from -2 to 0
- cluster: int32 [256], replicated, may hold values from 0 to 511, as said below
- gap_scale: int32 [256], replicated, may hold values from 1 to 2
Outputs:
- corrected: float32 [16384, 256], P('row', 'col')
Inputs may be any that keep to these rules, and one draw needn't show every extreme that they name: Distinct candidate indices; the first and the last candidate are always in the cluster.
All inputs are finite; a program needn't handle non-finite values.
Results may differ from a plain program's by a relative error of at most 0.000084.
Values sent between devices are 32-bit elements; how exact they have to be, the bound alone decides.
No kernel may reach another device: no remote copies, remote signals or barrier semaphores. Data moves between devices by JAX's collectives and lax.ppermute only.
A program may use at most 64 MiB of HBM per device.

v0:
```python
import functools

import jax
import jax.numpy as jnp
from jax import lax
from jax.experimental import pallas as pl
from jax.experimental.pallas import tpu as pltpu
from jax.sharding import PartitionSpec as P

HIGH = lax.Precision.HIGH
EXACT = lax.Precision.HIGHEST
BF16 = jnp.bfloat16
F32 = jnp.float32


def dot(a, b, dims, precision=None):
    return lax.dot_general(
        a, b, (dims, ((), ())), precision=precision, preferred_element_type=F32
    )


PARTS = 2
VMEM = pl.BlockSpec(memory_space=pltpu.VMEM)
SMEM = pl.BlockSpec(memory_space=pltpu.SMEM)


def split(x, count):
    pieces = []
    for _ in range(count):
        piece = x.astype(BF16)
        x = x - piece.astype(F32)
        pieces.append(piece)
    return pieces


def total(terms):
    return functools.reduce(lambda a, b: a + b, terms)


def steps(x, size, count):
    return total([jnp.where(x >= float(k * size), 1.0, 0.0) for k in range(1, count)])


def plan_kernel(n, parts, room, me_ref, cluster_ref, gap_ref, values_ref, vectors_ref, images_ref, info_ref, own_ref):
    count = cluster_ref.shape[1]
    width = vectors_ref.shape[1]
    pool = values_ref.shape[1]
    share = count // n
    square = (count, count)

    def lanes(row):
        return jnp.broadcast_to(row, square)

    me = me_ref[0]
    across = lax.broadcasted_iota(jnp.int32, square, 1).astype(F32)
    down = lax.broadcasted_iota(jnp.int32, square, 0).astype(F32)
    column = lanes(cluster_ref[...].astype(F32))
    source = steps(column, width, n)
    target = steps(across, share, n)
    source_t, target_t = source.T, target.T
    ahead = jnp.logical_or(
        source_t < source, jnp.logical_and(source_t == source, down < across)
    )
    turn = jnp.sum(
        jnp.where(jnp.logical_and(target_t == target, ahead), 1.0, 0.0), axis=0, keepdims=True
    )
    inner = steps(turn, parts, share // parts)
    row = (turn - parts * inner) * (count // parts) + target[:1] * (share // parts) + inner
    row = lanes(row)
    chosen = down == row

    def pick(values):
        return jnp.sum(jnp.where(chosen, lanes(values.astype(F32)), 0.0), axis=1, keepdims=True)

    spot = pick(cluster_ref[...])
    gap = pick(gap_ref[...])
    every = lax.broadcasted_iota(jnp.int32, (count, pool), 1).astype(F32)
    value = jnp.sum(jnp.where(every == spot, values_ref[...], 0.0), axis=1, keepdims=True)
    spots = lanes(spot)
    spots_t = spots.T
    part = steps(down, count // parts, parts)
    part_t = steps(across, count // parts, parts)
    source = steps(spots, width, n)
    source_t = steps(spots_t, width, n)
    peers = jnp.logical_and(jnp.logical_and(source == source_t, part == part_t), spots_t < spots)
    rank = jnp.sum(jnp.where(peers, 1.0, 0.0), axis=1, keepdims=True)
    wide = info_ref.shape[1]
    lane = lax.broadcasted_iota(jnp.int32, (count, wide), 1)
    info = jnp.zeros((count, wide), F32)
    for k, col in enumerate((spot, rank, value, gap, row.T[:, :1])):
        info = jnp.where(lane == k, col, info)
    info_ref[...] = info

    base = (me * width).astype(F32)
    here = lax.broadcasted_iota(jnp.int32, (count, width), 1).astype(F32) + base == spot
    slots = -(-parts * room // 128) * 128
    slot = lax.broadcasted_iota(jnp.int32, (count, slots), 1).astype(F32)
    filled = jnp.logical_and(slot == part[:, :1] * room + rank, rank < float(room))
    take = dot(
        jnp.where(filled, 1.0, 0.0).T[: parts * room].astype(BF16),
        jnp.where(here, 1.0, 0.0).astype(BF16),
        ((1,), (0,)),
    ).astype(BF16)
    lane = lax.broadcasted_iota(jnp.int32, (pool, width), 0)
    wanted = lane == lax.broadcasted_iota(jnp.int32, (pool, width), 1) + me * width
    values = jnp.sum(jnp.where(wanted, values_ref[...].T, 0.0), axis=0, keepdims=True)
    residual = images_ref[...] - values * vectors_ref[...]
    packed = total([dot(take, piece, ((1,), (1,))) for piece in split(residual, 3)])
    for p in range(parts):
        own_ref[p] = packed[p * room : (p + 1) * room]


def plan(room, me, cluster, gap, pool_values, pool_vectors, pool_images):
    rows = pool_vectors.shape[0]
    count = cluster.shape[0]
    n = lax.axis_size("col")
    return pl.pallas_call(
        functools.partial(plan_kernel, n, PARTS, room),
        out_shape=(
            jax.ShapeDtypeStruct((count, 128), F32),
            jax.ShapeDtypeStruct((PARTS, room, rows), F32),
        ),
        in_specs=[SMEM] + [VMEM] * 5,
        out_specs=(VMEM, VMEM),
        compiler_params=pltpu.CompilerParams(vmem_limit_bytes=24 << 20),
    )(me[None], cluster[None, :], gap[None, :], pool_values[None, :], pool_vectors, pool_images)


def product_kernel(width, n, source_ref, info_ref, *refs):
    *buffers, high_ref, out_ref = refs
    room = buffers[0].shape[0]
    slots = room * len(buffers)
    rows = info_ref.shape[0]
    lane = lax.broadcasted_iota(jnp.int32, (rows, slots), 1)
    owner = jnp.full((rows, slots), -1, jnp.int32)
    for b in range(len(buffers)):
        inside = jnp.logical_and(lane >= b * room, lane < (b + 1) * room)
        owner = jnp.where(inside, source_ref[b], owner)
    slot = lax.broadcasted_iota(jnp.int32, (rows, slots), 1).astype(F32)
    slot = slot - room * steps(slot, room, len(buffers))
    place = jnp.logical_and(
        steps(info_ref[:, 0:1], width, n) == owner.astype(F32), info_ref[:, 1:2] == slot
    )
    place = jnp.where(place, 1.0, 0.0).astype(BF16)
    gathered = jnp.concatenate([b[...] for b in buffers], 0)
    high, low = (dot(place, p, ((1,), (0,))).astype(BF16) for p in split(gathered, 2))
    x_high, x_low = split(high_ref[...], 2)
    term = dot(high, x_high, ((1,), (0,))) + dot(low, x_high, ((1,), (0,)))
    term = term + dot(high, x_low, ((1,), (0,)))

    @pl.when(pl.program_id(0) == 0)
    def _():
        out_ref[...] = term

    @pl.when(pl.program_id(0) > 0)
    def _():
        out_ref[...] += term


def product(part, width, info, buffers, high_vectors):
    n = lax.axis_size("col")
    rows, k = high_vectors.shape
    count = info.shape[0] // PARTS
    room = buffers[0][0].shape[0]
    piece = min(rows, 256)
    sources = jnp.stack([jnp.asarray(src, jnp.int32) for _, src in buffers])
    return pl.pallas_call(
        functools.partial(product_kernel, width, n),
        out_shape=jax.ShapeDtypeStruct((count, k), F32),
        grid=(rows // piece,),
        in_specs=[SMEM, pl.BlockSpec((count, info.shape[1]), lambda i: (part, 0))]
        + [pl.BlockSpec((room, piece), lambda i: (0, i)) for _ in buffers]
        + [pl.BlockSpec((piece, k), lambda i: (i, 0))],
        out_specs=pl.BlockSpec((count, k), lambda i: (0, 0)),
        compiler_params=pltpu.CompilerParams(vmem_limit_bytes=24 << 20),
        cost_estimate=pl.CostEstimate(
            flops=6 * count * rows * k, bytes_accessed=4 * rows * k, transcendentals=0
        ),
    )(sources, info, *[b for b, _ in buffers], high_vectors)


def image_kernel(me_ref, info_ref, sums_ref, mu_ref, vectors_ref, high_ref, out_ref, d_high, d_low):
    @pl.when(pl.program_id(0) == 0)
    def _():
        gaps = info_ref[:, 3:4] * (mu_ref[...] - info_ref[:, 2:3])
        high, low = split(sums_ref[...] / gaps, 2)
        d_high[...] = high
        d_low[...] = low

    width = vectors_ref.shape[1]
    spot = lax.broadcasted_iota(jnp.int32, (info_ref.shape[0], width), 1) + me_ref[0] * width
    mine = jnp.where(spot.astype(F32) == info_ref[:, 0:1], 1.0, 0.0).astype(BF16)
    chosen = total([dot(mine, p, ((1,), (1,))) for p in split(vectors_ref[...], 3)])
    x_high, x_low = split(high_ref[...], 2)
    image = dot(d_high[...], x_high, ((1,), (1,))) + dot(d_low[...], x_high, ((1,), (1,)))
    out_ref[...] = chosen - (image + dot(d_high[...], x_low, ((1,), (1,))))


def image(part, me, info, sums, high_values, pool_vectors, high_vectors):
    rows, k = high_vectors.shape
    count = sums.shape[0]
    piece = min(rows, 256)
    return pl.pallas_call(
        image_kernel,
        out_shape=jax.ShapeDtypeStruct((count, rows), F32),
        grid=(rows // piece,),
        in_specs=[
            SMEM,
            pl.BlockSpec((count, info.shape[1]), lambda i: (part, 0)),
            pl.BlockSpec((count, k), lambda i: (0, 0)),
            pl.BlockSpec((1, k), lambda i: (0, 0)),
            pl.BlockSpec((piece, pool_vectors.shape[1]), lambda i: (i, 0)),
            pl.BlockSpec((piece, k), lambda i: (i, 0)),
        ],
        out_specs=pl.BlockSpec((count, piece), lambda i: (0, i)),
        scratch_shapes=[pltpu.VMEM((count, k), BF16)] * 2,
        compiler_params=pltpu.CompilerParams(vmem_limit_bytes=24 << 20),
        cost_estimate=pl.CostEstimate(
            flops=6 * count * rows * k, bytes_accessed=4 * rows * k, transcendentals=0
        ),
    )(me[None], info, sums, high_values[None, :], pool_vectors, high_vectors)


def finish_kernel(parts, me_ref, info_ref, *refs):
    *terms, out_ref = refs
    share = out_ref.shape[0]
    inner = share // parts
    each = len(terms) // parts
    rows = [total([t[...] for t in terms[p * each : (p + 1) * each]]) for p in range(parts)]
    rows = jnp.concatenate(rows, 0)
    first = me_ref[0] * share
    where = info_ref[pl.ds(pl.multiple_of(first, share), share), :][:, 4:5]
    slot = lax.broadcasted_iota(jnp.int32, (share, share), 1).astype(F32)
    part = steps(slot, inner, parts)
    count = info_ref.shape[0]
    row = part * (count // parts) + (me_ref[0] * inner).astype(F32) + (slot - part * inner)
    order = jnp.where(row == where, 1.0, 0.0).astype(BF16)
    out_ref[...] = total([dot(order, p, ((1,), (0,))) for p in split(rows, 3)])


def finish(me, info, terms):
    n = lax.axis_size("col")
    rows = terms[0].shape[1]
    return pl.pallas_call(
        functools.partial(finish_kernel, PARTS),
        out_shape=jax.ShapeDtypeStruct((info.shape[0] // n, rows), F32),
        in_specs=[SMEM] + [VMEM] * (len(terms) + 1),
        out_specs=VMEM,
        compiler_params=pltpu.CompilerParams(vmem_limit_bytes=24 << 20),
    )(me[None], info, *terms)


def mirrored(n, pairs):
    return pairs + [(n - 1 - a, n - 1 - b) for a, b in pairs]


def gather_line(own, axis):
    n = lax.axis_size(axis)
    me = lax.axis_index(axis)
    buffers = [(own, me)]
    from_left = from_right = own
    for step in range(1, n):
        right = [(i, i + 1) for i in range(step - 1, n - 1)]
        left = [(i, i - 1) for i in range(1, n - step + 1)]
        if 2 * step > n + 1:
            rows = lax.ppermute(from_left, axis, right + left)
        else:
            came_left = lax.ppermute(from_left, axis, right)
            came_right = lax.ppermute(from_right, axis, left)
            if 2 * step < n:
                buffers += [(came_left, me - step), (came_right, me + step)]
                from_left, from_right = came_left, came_right
                continue
            rows = came_left + came_right
        buffers.append((rows, jnp.where(me >= step, me - step, me + step)))
        from_left = from_right = rows
    return [(rows, jnp.where(src < n, src, -1)) for rows, src in buffers]


def scatter_line(blocks, axis):
    n = lax.axis_size(axis)
    me = lax.axis_index(axis)
    half = n // 2
    place = me % half
    base = me - place
    left = me < half

    def block(k):
        return lax.dynamic_index_in_dim(blocks, k, 0, keepdims=False)

    terms = [block(me)]
    for target in range(n - 1, half - 1, -1):
        part = block(jnp.where(left, target, n - 1 - target))
        rows = part
        for hop in range(half - 1):
            rows = part + lax.ppermute(rows, axis, mirrored(n, [(hop, hop + 1)]))
        terms.append(lax.ppermute(rows, axis, mirrored(n, [(half - 1, target)])))
    for step in range(1, half):
        turn = [(g + i, g + (i + step) % half) for g in (0, half) for i in range(half)]
        terms.append(lax.ppermute(block(base + (place + step) % half), axis, turn))
    return terms


def sum_pairs(x, axis):
    n = lax.axis_size(axis)
    me = lax.axis_index(axis)
    half = x.shape[0] // 2
    mine = (me % 2) * half
    pairs = [(i, i ^ 1) for i in range(n)]
    keep = lax.dynamic_slice_in_dim(x, mine, half, 0)
    give = lax.dynamic_slice_in_dim(x, half - mine, half, 0)
    part = keep + lax.ppermute(give, axis, pairs)
    bits = [1 << b for b in range(1, n.bit_length() - 1)]
    cut = -(-half // (8 * len(bits))) * 8
    pieces = [part[i * cut : min(half, (i + 1) * cut)] for i in range(len(bits))]
    for turn in range(len(bits)):
        for i in range(len(bits)):
            bit = bits[(i + turn) % len(bits)]
            pieces[i] = pieces[i] + lax.ppermute(
                pieces[i], axis, [(d, d ^ bit) for d in range(n)]
            )
        pieces = list(lax.optimization_barrier(tuple(pieces)))
    part = jnp.concatenate(pieces, 0)
    other = lax.ppermute(part, axis, pairs)
    first = me % 2 == 0
    return jnp.concatenate(
        [jnp.where(first, part, other), jnp.where(first, other, part)], 0
    )


def correct_parts(room, high_vectors, high_values, pool_vectors, pool_images, pool_values, cluster, gap):
    n = lax.axis_size("col")
    me = lax.axis_index("col")
    count = cluster.shape[0]
    width = pool_vectors.shape[1]
    info, own = plan(room, me, cluster, gap, pool_values, pool_vectors, pool_images)
    gathered = [gather_line(own[p], "col") for p in range(PARTS)]
    sums = [
        sum_pairs(product(p, width, info, gathered[p], high_vectors), "row") for p in range(PARTS)
    ]
    terms = []
    for p in range(PARTS):
        partial = image(p, me, info, sums[p], high_values, pool_vectors, high_vectors)
        terms += scatter_line(partial.reshape(n, count // (n * PARTS), -1), "col")
    return finish(me, info, terms).T, jnp.max(info[:, 1]) + 1.0


def correct_whole(high_vectors, high_values, pool_vectors, pool_images, pool_values, cluster, gap):
    n = lax.axis_size("col")
    me = lax.axis_index("col")
    count = cluster.shape[0]
    width = pool_vectors.shape[1]
    low_vals = jnp.take(pool_values, cluster, axis=0)
    values = lax.dynamic_slice_in_dim(pool_values, me * width, width, 0)
    own = (pool_images - values[None, :] * pool_vectors).T
    sums = jnp.zeros((count, high_vectors.shape[1]), F32)
    for rows, source in gather_line(own, "col"):
        spot = source * width + jnp.arange(width)
        here = jnp.logical_and(cluster[:, None] == spot[None, :], source >= 0).astype(F32)
        rows = dot(here, rows, ((1,), (0,)), EXACT)
        sums = sums + dot(rows, high_vectors, ((1,), (0,)), HIGH)
    sums = sum_pairs(sums, "row")
    coeffs = sums / (gap.astype(F32)[:, None] * (high_values[None, :] - low_vals[:, None]))
    mine = (cluster[:, None] == me * width + jnp.arange(width)[None, :]).astype(F32)
    partial = dot(mine, pool_vectors, ((1,), (1,)), EXACT)
    partial = partial - dot(coeffs, high_vectors, ((1,), (1,)), HIGH)
    return total(scatter_line(partial.reshape(n, count // n, -1), "col")).T


def body(*args):
    width = args[2].shape[1]
    share = args[5].shape[0] // (PARTS * lax.axis_size("col"))
    room = min(width, -(-(share + share // 4) // 8) * 8)
    out, most = correct_parts(room, *args)
    if room == width:
        return out
    return lax.cond(most <= room, lambda *_: out, correct_whole, *args)


def solution(mesh):
    placed = (P("row", "col"), P("col"), P("row", "col"), P("row", "col"), P(), P(), P())
    return jax.shard_map(
        body, mesh=mesh, in_specs=placed, out_specs=P("row", "col"), check_vma=False
    )
```

profile of v0, /device:TPU:0, one launch (start us, length us, event | category | flops | bytes accessed | tf_op | source)
XLA Modules:
  0.0 134.9 jit_solution(16960875662691647040)
XLA Ops:
  0.0 3.1 %shard_map.75 = (f32[256,128]{1,0:T(8,128)S(1)}, f32[2,40,2048]{2,1,0:T(8,128)S(1)}) custom-call(s32[1]{0:T(128)} %bitcast.7.me_ref, s32[1,256]{1,0:T(1,128)} %bitcast.78, s32[1,256]{1,0:T(1,128)} %bitcast.81, f32[1,512]{1,0:T(1,128)} %bitcast.74, f32[2048,128]{1,0:T(8,128)} %vectors_ref.5, f32[2048,128]{1,0:T(8,128)} %images_ref.1), custom_call_target="tpu_custom_call" | custom-call | tf_op jit(solution)/shard_map/pallas_call | solution.py:117
  3.2 4.9 %collective-permute-start.32 = (f32[40,2048]{1,0:T(8,128)S(1)}, f32[40,2048]{1,0:T(8,128)S(1)}, u32[]{:S(2)}, u32[]{:S(2)}) collective-permute-start(f32[40,2048]{1,0:T(8,128)S(1)} %get-tuple-element.72.refs_0_), channel_id=1, source_target_pairs={{0,1},{1,2},{2,3},{4,5},{5,6},{6,7},{8,9},{9,10},{10,11},{12,13},{... | collective-permute-start | bytes 983048 | tf_op jit(solution)/shard_map/ppermute | solution.py:268
  8.1 1.3 collective-permute-start.33
  9.4 4.6 %collective-permute-start.16 = (f32[40,2048]{1,0:T(8,128)S(1)}, f32[40,2048]{1,0:T(8,128)S(1)}, u32[]{:S(2)}, u32[]{:S(2)}) collective-permute-start(f32[40,2048]{1,0:T(8,128)S(1)} %get-tuple-element.73.refs_0_), channel_id=1, source_target_pairs={{0,1},{1,2},{2,3},{4,5},{5,6},{6,7},{8,9},{9,10},{10,11},{12,13},{... | collective-permute-start | bytes 983048 | tf_op jit(solution)/shard_map/ppermute | solution.py:268
  14.0 1.3 collective-permute-start.17
  15.3 0.9 collective-permute-done.32.refs_1_
  16.2 0.7 collective-permute-start.34
  16.9 3.8 %collective-permute-done.33.refs_2_ = f32[40,2048]{1,0:T(8,128)S(1)} collective-permute-done((f32[40,2048]{1,0:T(8,128)S(1)}, f32[40,2048]{1,0:T(8,128)S(1)}, u32[]{:S(2)}, u32[]{:S(2)}) %collective-permute-start.33) | collective-permute-done | bytes 327712 | tf_op jit(solution)/shard_map/ppermute | solution.py:269
  20.7 1.3 collective-permute-start.35
  21.9 0.1 collective-permute-done.16.refs_1_
  22.1 0.7 collective-permute-start.18
  22.8 4.9 %collective-permute-done.17.refs_2_ = f32[40,2048]{1,0:T(8,128)S(1)} collective-permute-done((f32[40,2048]{1,0:T(8,128)S(1)}, f32[40,2048]{1,0:T(8,128)S(1)}, u32[]{:S(2)}, u32[]{:S(2)}) %collective-permute-start.17) | collective-permute-done | bytes 327712 | tf_op jit(solution)/shard_map/ppermute | solution.py:269
  27.7 1.3 collective-permute-start.19
  29.0 5.7 %collective-permute-done.35 = f32[40,2048]{1,0:T(8,128)S(1)} collective-permute-done((f32[40,2048]{1,0:T(8,128)S(1)}, f32[40,2048]{1,0:T(8,128)S(1)}, u32[]{:S(2)}, u32[]{:S(2)}) %collective-permute-start.35) | collective-permute-done | bytes 327712 | tf_op jit(solution)/shard_map/ppermute | solution.py:269
  34.8 1.3 collective-permute-start.36
  36.1 5.7 %collective-permute-done.19 = f32[40,2048]{1,0:T(8,128)S(1)} collective-permute-done((f32[40,2048]{1,0:T(8,128)S(1)}, f32[40,2048]{1,0:T(8,128)S(1)}, u32[]{:S(2)}, u32[]{:S(2)}) %collective-permute-start.19) | collective-permute-done | bytes 327712 | tf_op jit(solution)/shard_map/ppermute | solution.py:269
  41.8 1.3 collective-permute-start.20
  43.1 0.1 stack.29.source_ref
  43.2 5.5 %collective-permute-done.36.refs_4_ = f32[40,2048]{1,0:T(8,128)S(1)} collective-permute-done((f32[40,2048]{1,0:T(8,128)S(1)}, f32[40,2048]{1,0:T(8,128)S(1)}, u32[]{:S(2)}, u32[]{:S(2)}) %collective-permute-start.36) | collective-permute-done | bytes 327712 | tf_op jit(solution)/shard_map/ppermute | solution.py:266
  48.7 8.8 %shard_map.78 = f32[128,1024]{1,0:T(8,128)S(1)} custom-call(s32[5]{0:T(128)S(1)} %stack.29.source_ref, f32[256,128]{1,0:T(8,128)S(1)} %get-tuple-element.44.info_ref, f32[40,2048]{1,0:T(8,128)S(1)} %get-tuple-element.72.refs_0_, f32[40,2048]{1,0:T(8,128)S(1)} %collective-permute-done.32.refs_1_, f32[40,2048]{1,0:T(8,128)S(1)} %collective-permute-done.33.refs_2_, ...), custom_call_target="tpu_custom_call" | custom-call | flops 1610612736 | bytes 8388608 | tf_op jit(solution)/shard_map/pallas_call | solution.py:167
  57.7 5.8 %shard_map.76 = f32[128,1024]{1,0:T(8,128)S(1)} custom-call(s32[5]{0:T(128)S(1)} %stack.29.source_ref, f32[256,128]{1,0:T(8,128)S(1)} %get-tuple-element.44.info_ref, f32[40,2048]{1,0:T(8,128)S(1)} %get-tuple-element.73.refs_0_, f32[40,2048]{1,0:T(8,128)S(1)} %collective-permute-done.16.refs_1_, f32[40,2048]{1,0:T(8,128)S(1)} %collective-permute-done.17.refs_2_, ...), custom_call_target="tpu_custom_call" | custom-call | flops 1610612736 | bytes 8388608 | tf_op jit(solution)/shard_map/pallas_call | solution.py:167
  63.6 0.5 collective-permute-start.21
  64.1 1.6 %collective-permute-start.38 = (f32[32,1024]{1,0:T(8,128)S(1)}, f32[32,1024]{1,0:T(8,128)S(1)}, u32[]{:S(2)}, u32[]{:S(2)}) collective-permute-start(f32[32,1024]{1,0:T(8,128)S(1)} %get-tuple-element.81), channel_id=1, source_target_pairs={{0,8},{4,12},{8,0},{12,4},{16,24},{20,28},{24,16},{28,20},{1,9},{5... | collective-permute-start | bytes 393224 | tf_op jit(solution)/shard_map/ppermute | solution.py:319
  65.7 1.5 %collective-permute-start.39 = (f32[32,1024]{1,0:T(8,128)S(1)}, f32[32,1024]{1,0:T(8,128)S(1)}, u32[]{:S(2)}, u32[]{:S(2)}) collective-permute-start(f32[32,1024]{1,0:T(8,128)S(1)} %get-tuple-element.80), channel_id=1, source_target_pairs={{0,16},{4,20},{8,24},{12,28},{16,0},{20,4},{24,8},{28,12},{1,17},{... | collective-permute-start | bytes 393224 | tf_op jit(solution)/shard_map/ppermute | solution.py:319
  67.2 0.6 collective-permute-start.22
  67.9 0.5 collective-permute-start.23
  68.4 1.5 %collective-permute-done.38 = f32[32,1024]{1,0:T(8,128)S(1)} collective-permute-done((f32[32,1024]{1,0:T(8,128)S(1)}, f32[32,1024]{1,0:T(8,128)S(1)}, u32[]{:S(2)}, u32[]{:S(2)}) %collective-permute-start.38) | collective-permute-done | bytes 131104 | tf_op jit(solution)/shard_map/ppermute | solution.py:319
  69.9 2.2 %collective-permute-done.39 = f32[32,1024]{1,0:T(8,128)S(1)} collective-permute-done((f32[32,1024]{1,0:T(8,128)S(1)}, f32[32,1024]{1,0:T(8,128)S(1)}, u32[]{:S(2)}, u32[]{:S(2)}) %collective-permute-start.39) | collective-permute-done | bytes 131104 | tf_op jit(solution)/shard_map/ppermute | solution.py:319
  72.1 0.1 collective-permute-start.41
  72.2 2.0 %collective-permute-start.40 = (f32[32,1024]{1,0:T(8,128)S(1)}, f32[32,1024]{1,0:T(8,128)S(1)}, u32[]{:S(2)}, u32[]{:S(2)}) collective-permute-start(f32[32,1024]{1,0:T(8,128)S(1)} %get-tuple-element.50), channel_id=1, source_target_pairs={{0,16},{4,20},{8,24},{12,28},{16,0},{20,4},{24,8},{28,12},{1,17},{... | collective-permute-start | bytes 393224 | tf_op jit(solution)/shard_map/ppermute | solution.py:319
  74.2 0.3 collective-permute-done.23
  74.6 1.3 collective-permute-start.25
  75.8 0.6 collective-permute-start.24
  76.4 1.7 %collective-permute-done.41 = f32[32,1024]{1,0:T(8,128)S(1)} collective-permute-done((f32[32,1024]{1,0:T(8,128)S(1)}, f32[32,1024]{1,0:T(8,128)S(1)}, u32[]{:S(2)}, u32[]{:S(2)}) %collective-permute-start.41) | collective-permute-done | bytes 131104 | tf_op jit(solution)/shard_map/ppermute | solution.py:319
  78.1 0.3 collective-permute-done.40
  78.6 1.0 collective-permute-done.25
  79.6 1.2 collective-permute-done.24
  80.8 0.1 collective-permute-start.26
  81.1 9.9 %shard_map.79 = f32[128,2048]{1,0:T(8,128)S(1)} custom-call(s32[1]{0:T(128)} %bitcast.7.me_ref, f32[256,128]{1,0:T(8,128)S(1)} %get-tuple-element.44.info_ref, f32[128,1024]{1,0:T(8,128)S(1)} %pad_maximum_fusion.1.sums_ref, f32[1,1024]{1,0:T(1,128)S(1)} %bitcast.79, f32[2048,128]{1,0:T(8,128)S(1)} %copy-done.2, f32[2048,1024]{1,0:T(8,128)} %high_ref.3), custom_call_target="tpu_custom_call" | custom-call | flops 1610612736 | bytes 8388608 | tf_op jit(solution)/shard_map/pallas_call | solution.py:203
  90.9 0.1 dynamic-slice_bitcast_fusion.3
  91.0 1.4 %collective-permute-start.45 = (f32[32,2048]{1,0:T(8,128)S(1)}, f32[32,2048]{1,0:T(8,128)S(1)}, u32[]{:S(2)}, u32[]{:S(2)}) collective-permute-start(f32[32,2048]{1,0:T(8,128)S(1)} %get-tuple-element.65), channel_id=1, source_target_pairs={{0,1},{3,2},{4,5},{7,6},{8,9},{11,10},{12,13},{15,14},{16,17},{19,... | collective-permute-start | bytes 786440 | tf_op jit(solution)/shard_map/ppermute | solution.py:296
  92.5 1.3 collective-permute-start.43
  93.9 6.2 %shard_map.77 = f32[128,2048]{1,0:T(8,128)S(1)} custom-call(s32[1]{0:T(128)} %bitcast.7.me_ref, f32[256,128]{1,0:T(8,128)S(1)} %get-tuple-element.44.info_ref, f32[128,1024]{1,0:T(8,128)S(1)} %pad_maximum_fusion.sums_ref, f32[1,1024]{1,0:T(1,128)S(1)} %bitcast.80, f32[2048,128]{1,0:T(8,128)S(1)} %copy-done.2, f32[2048,1024]{1,0:T(8,128)S(1)} %bitcast.71), custom_call_target="tpu_custom_call" | custom-call | flops 1610612736 | bytes 8388608 | tf_op jit(solution)/shard_map/pallas_call | solution.py:203
  100.2 0.1 dynamic-slice_bitcast_fusion.7
  100.2 1.3 collective-permute-start.29
  101.6 1.3 collective-permute-start.27
  102.9 0.1 collective-permute-start.47
  103.0 2.0 %collective-permute-start.31 = (f32[32,2048]{1,0:T(8,128)S(1)}, f32[32,2048]{1,0:T(8,128)S(1)}, u32[]{:S(2)}, u32[]{:S(2)}) collective-permute-start(f32[32,2048]{1,0:T(8,128)S(1)} %get-tuple-element.68), channel_id=1, source_target_pairs={{0,1},{1,0},{2,3},{3,2},{4,5},{5,4},{6,7},{7,6},{8,9},{9,8},{10,11... | collective-permute-start | bytes 786440 | tf_op jit(solution)/shard_map/ppermute | solution.py:300
  105.0 0.8 add.302
  105.7 0.7 collective-permute-start.46
  106.4 0.7 add.301
  107.2 3.2 %collective-permute-done.29 = f32[32,2048]{1,0:T(8,128)S(1)} collective-permute-done((f32[32,2048]{1,0:T(8,128)S(1)}, f32[32,2048]{1,0:T(8,128)S(1)}, u32[]{:S(2)}, u32[]{:S(2)}) %collective-permute-start.29) | collective-permute-done | bytes 262176 | tf_op jit(solution)/shard_map/ppermute | solution.py:296
  110.4 1.3 collective-permute-start.44
  111.7 0.8 add.289
  112.4 3.6 %collective-permute-done.27 = f32[32,2048]{1,0:T(8,128)S(1)} collective-permute-done((f32[32,2048]{1,0:T(8,128)S(1)}, f32[32,2048]{1,0:T(8,128)S(1)}, u32[]{:S(2)}, u32[]{:S(2)}) %collective-permute-start.27) | collective-permute-done | bytes 262176 | tf_op jit(solution)/shard_map/ppermute | solution.py:296
  116.0 0.7 collective-permute-start.30
  116.7 0.7 add.288
  117.4 4.2 %collective-permute-done.47.refs_7_ = f32[32,2048]{1,0:T(8,128)S(1)} collective-permute-done((f32[32,2048]{1,0:T(8,128)S(1)}, f32[32,2048]{1,0:T(8,128)S(1)}, u32[]{:S(2)}, u32[]{:S(2)}) %collective-permute-start.47) | collective-permute-done | bytes 262176 | tf_op jit(solution)/shard_map/ppermute | solution.py:300
  121.6 1.3 collective-permute-start.28
  122.9 0.8 slice_reduce_fusion
  124.4 2.5 %collective-permute-done.31.refs_3_ = f32[32,2048]{1,0:T(8,128)S(1)} collective-permute-done((f32[32,2048]{1,0:T(8,128)S(1)}, f32[32,2048]{1,0:T(8,128)S(1)}, u32[]{:S(2)}, u32[]{:S(2)}) %collective-permute-start.31) | collective-permute-done | bytes 262176 | tf_op jit(solution)/shard_map/ppermute | solution.py:300
  126.9 6.4 %collective-permute-done.28.refs_1_ = f32[32,2048]{1,0:T(8,128)S(1)} collective-permute-done((f32[32,2048]{1,0:T(8,128)}, f32[32,2048]{1,0:T(8,128)S(1)}, u32[]{:S(2)}, u32[]{:S(2)}) %collective-permute-start.28) | collective-permute-done | bytes 262176 | tf_op jit(solution)/shard_map/ppermute | solution.py:297
  133.3 1.2 shard_map.80
  134.5 0.2 conditional.1
  (55 shorter events, 0.9 us)
Async XLA Ops:
  3.2 13.0 %collective-permute-start.32 = (f32[40,2048]{1,0:T(8,128)S(1)}, f32[40,2048]{1,0:T(8,128)S(1)}, u32[]{:S(2)}, u32[]{:S(2)}) collective-permute-start(f32[40,2048]{1,0:T(8,128)S(1)} %get-tuple-element.72.refs_0_), channel_id=1, source_target_pairs={{0,1},{1,2},{2,3},{4,5},{5,6},{6,7},{8,9},{9,10},{10,11},{12,13},{... | collective-permute-start | bytes 983048 | tf_op jit(solution)/shard_map/ppermute | solution.py:268
  8.1 12.5 %collective-permute-start.33 = (f32[40,2048]{1,0:T(8,128)S(1)}, f32[40,2048]{1,0:T(8,128)S(1)}, u32[]{:S(2)}, u32[]{:S(2)}) collective-permute-start(f32[40,2048]{1,0:T(8,128)S(1)} %get-tuple-element.72.refs_0_), channel_id=1, source_target_pairs={{1,0},{2,1},{3,2},{5,4},{6,5},{7,6},{9,8},{10,9},{11,10},{13,12},{... | collective-permute-start | bytes 983048 | tf_op jit(solution)/shard_map/ppermute | solution.py:269
  9.4 12.7 %collective-permute-start.16 = (f32[40,2048]{1,0:T(8,128)S(1)}, f32[40,2048]{1,0:T(8,128)S(1)}, u32[]{:S(2)}, u32[]{:S(2)}) collective-permute-start(f32[40,2048]{1,0:T(8,128)S(1)} %get-tuple-element.73.refs_0_), channel_id=1, source_target_pairs={{0,1},{1,2},{2,3},{4,5},{5,6},{6,7},{8,9},{9,10},{10,11},{12,13},{... | collective-permute-start | bytes 983048 | tf_op jit(solution)/shard_map/ppermute | solution.py:268
  14.0 13.7 %collective-permute-start.17 = (f32[40,2048]{1,0:T(8,128)S(1)}, f32[40,2048]{1,0:T(8,128)S(1)}, u32[]{:S(2)}, u32[]{:S(2)}) collective-permute-start(f32[40,2048]{1,0:T(8,128)S(1)} %get-tuple-element.73.refs_0_), channel_id=1, source_target_pairs={{1,0},{2,1},{3,2},{5,4},{6,5},{7,6},{9,8},{10,9},{11,10},{13,12},{... | collective-permute-start | bytes 983048 | tf_op jit(solution)/shard_map/ppermute | solution.py:269
  16.2 12.8 %collective-permute-start.34 = (f32[40,2048]{1,0:T(8,128)S(1)}, f32[40,2048]{1,0:T(8,128)S(1)}, u32[]{:S(2)}, u32[]{:S(2)}) collective-permute-start(f32[40,2048]{1,0:T(8,128)S(1)} %collective-permute-done.32.refs_1_), channel_id=1, source_target_pairs={{1,2},{2,3},{5,6},{6,7},{9,10},{10,11},{13,14},{14,15},{17,18},{18... | collective-permute-start | bytes 983048 | tf_op jit(solution)/shard_map/ppermute | solution.py:268
  20.7 14.0 %collective-permute-start.35 = (f32[40,2048]{1,0:T(8,128)S(1)}, f32[40,2048]{1,0:T(8,128)S(1)}, u32[]{:S(2)}, u32[]{:S(2)}) collective-permute-start(f32[40,2048]{1,0:T(8,128)S(1)} %collective-permute-done.33.refs_2_), channel_id=1, source_target_pairs={{1,0},{2,1},{5,4},{6,5},{9,8},{10,9},{13,12},{14,13},{17,16},{18,1... | collective-permute-start | bytes 983048 | tf_op jit(solution)/shard_map/ppermute | solution.py:269
  22.1 14.0 %collective-permute-start.18 = (f32[40,2048]{1,0:T(8,128)S(1)}, f32[40,2048]{1,0:T(8,128)S(1)}, u32[]{:S(2)}, u32[]{:S(2)}) collective-permute-start(f32[40,2048]{1,0:T(8,128)S(1)} %collective-permute-done.16.refs_1_), channel_id=1, source_target_pairs={{1,2},{2,3},{5,6},{6,7},{9,10},{10,11},{13,14},{14,15},{17,18},{18... | collective-permute-start | bytes 983048 | tf_op jit(solution)/shard_map/ppermute | solution.py:268
  27.7 14.0 %collective-permute-start.19 = (f32[40,2048]{1,0:T(8,128)S(1)}, f32[40,2048]{1,0:T(8,128)S(1)}, u32[]{:S(2)}, u32[]{:S(2)}) collective-permute-start(f32[40,2048]{1,0:T(8,128)S(1)} %collective-permute-done.17.refs_2_), channel_id=1, source_target_pairs={{1,0},{2,1},{5,4},{6,5},{9,8},{10,9},{13,12},{14,13},{17,16},{18,1... | collective-permute-start | bytes 983048 | tf_op jit(solution)/shard_map/ppermute | solution.py:269
  34.8 14.0 %collective-permute-start.36 = (f32[40,2048]{1,0:T(8,128)S(1)}, f32[40,2048]{1,0:T(8,128)S(1)}, u32[]{:S(2)}, u32[]{:S(2)}) collective-permute-start(f32[40,2048]{1,0:T(8,128)S(1)} %add.295.refs_3_), channel_id=1, source_target_pairs={{2,3},{1,0},{6,7},{5,4},{10,11},{9,8},{14,15},{13,12},{18,19},{17,... | collective-permute-start | bytes 983048 | tf_op jit(solution)/shard_map/ppermute | solution.py:266
  41.8 15.9 %collective-permute-start.20 = (f32[40,2048]{1,0:T(8,128)S(1)}, f32[40,2048]{1,0:T(8,128)S(1)}, u32[]{:S(2)}, u32[]{:S(2)}) collective-permute-start(f32[40,2048]{1,0:T(8,128)S(1)} %add.279.refs_3_), channel_id=1, source_target_pairs={{2,3},{1,0},{6,7},{5,4},{10,11},{9,8},{14,15},{13,12},{18,19},{17,... | collective-permute-start | bytes 983048 | tf_op jit(solution)/shard_map/ppermute | solution.py:266
  48.7 9.0 %copy-start = (f32[2048,1024]{1,0:T(8,128)S(1)}, f32[2048,1024]{1,0:T(8,128)}, u32[]{:S(2)}) copy-start(f32[2048,1024]{1,0:T(8,128)} %high_ref.3) | copy-start | bytes 25165828
  57.6 6.4 %collective-permute-start.37 = (f32[64,1024]{1,0:T(8,128)S(1)}, f32[64,1024]{1,0:T(8,128)S(1)}, u32[]{:S(2)}, u32[]{:S(2)}) collective-permute-start(f32[64,1024]{1,0:T(8,128)S(1)} %constant_dynamic-slice_fusion.1), channel_id=1, source_target_pairs={{0,4},{4,0},{8,12},{12,8},{16,20},{20,16},{24,28},{28,24},{1,5},{5... | collective-permute-start | bytes 786440 | tf_op jit(solution)/shard_map/ppermute | solution.py:312
  63.6 3.6 %collective-permute-start.21 = (f32[64,1024]{1,0:T(8,128)S(1)}, f32[64,1024]{1,0:T(8,128)S(1)}, u32[]{:S(2)}, u32[]{:S(2)}) collective-permute-start(f32[64,1024]{1,0:T(8,128)S(1)} %constant_dynamic-slice_fusion.2), channel_id=1, source_target_pairs={{0,4},{4,0},{8,12},{12,8},{16,20},{20,16},{24,28},{28,24},{1,5},{5... | collective-permute-start | bytes 786440 | tf_op jit(solution)/shard_map/ppermute | solution.py:312
  64.1 5.8 %collective-permute-start.38 = (f32[32,1024]{1,0:T(8,128)S(1)}, f32[32,1024]{1,0:T(8,128)S(1)}, u32[]{:S(2)}, u32[]{:S(2)}) collective-permute-start(f32[32,1024]{1,0:T(8,128)S(1)} %get-tuple-element.81), channel_id=1, source_target_pairs={{0,8},{4,12},{8,0},{12,4},{16,24},{20,28},{24,16},{28,20},{1,9},{5... | collective-permute-start | bytes 393224 | tf_op jit(solution)/shard_map/ppermute | solution.py:319
  65.7 6.4 %collective-permute-start.39 = (f32[32,1024]{1,0:T(8,128)S(1)}, f32[32,1024]{1,0:T(8,128)S(1)}, u32[]{:S(2)}, u32[]{:S(2)}) collective-permute-start(f32[32,1024]{1,0:T(8,128)S(1)} %get-tuple-element.80), channel_id=1, source_target_pairs={{0,16},{4,20},{8,24},{12,28},{16,0},{20,4},{24,8},{28,12},{1,17},{... | collective-permute-start | bytes 393224 | tf_op jit(solution)/shard_map/ppermute | solution.py:319
  67.2 7.0 %collective-permute-start.22 = (f32[32,1024]{1,0:T(8,128)S(1)}, f32[32,1024]{1,0:T(8,128)S(1)}, u32[]{:S(2)}, u32[]{:S(2)}) collective-permute-start(f32[32,1024]{1,0:T(8,128)S(1)} %get-tuple-element.85), channel_id=1, source_target_pairs={{0,8},{4,12},{8,0},{12,4},{16,24},{20,28},{24,16},{28,20},{1,9},{5... | collective-permute-start | bytes 393224 | tf_op jit(solution)/shard_map/ppermute | solution.py:319
  67.9 6.6 %collective-permute-start.23 = (f32[32,1024]{1,0:T(8,128)S(1)}, f32[32,1024]{1,0:T(8,128)S(1)}, u32[]{:S(2)}, u32[]{:S(2)}) collective-permute-start(f32[32,1024]{1,0:T(8,128)S(1)} %get-tuple-element.84), channel_id=1, source_target_pairs={{0,16},{4,20},{8,24},{12,28},{16,0},{20,4},{24,8},{28,12},{1,17},{... | collective-permute-start | bytes 393224 | tf_op jit(solution)/shard_map/ppermute | solution.py:319
  72.1 6.0 %collective-permute-start.41 = (f32[32,1024]{1,0:T(8,128)S(1)}, f32[32,1024]{1,0:T(8,128)S(1)}, u32[]{:S(2)}, u32[]{:S(2)}) collective-permute-start(f32[32,1024]{1,0:T(8,128)S(1)} %get-tuple-element.51), channel_id=1, source_target_pairs={{0,8},{4,12},{8,0},{12,4},{16,24},{20,28},{24,16},{28,20},{1,9},{5... | collective-permute-start | bytes 393224 | tf_op jit(solution)/shard_map/ppermute | solution.py:319
  72.2 6.2 %collective-permute-start.40 = (f32[32,1024]{1,0:T(8,128)S(1)}, f32[32,1024]{1,0:T(8,128)S(1)}, u32[]{:S(2)}, u32[]{:S(2)}) collective-permute-start(f32[32,1024]{1,0:T(8,128)S(1)} %get-tuple-element.50), channel_id=1, source_target_pairs={{0,16},{4,20},{8,24},{12,28},{16,0},{20,4},{24,8},{28,12},{1,17},{... | collective-permute-start | bytes 393224 | tf_op jit(solution)/shard_map/ppermute | solution.py:319
  74.6 5.0 %collective-permute-start.25 = (f32[32,1024]{1,0:T(8,128)S(1)}, f32[32,1024]{1,0:T(8,128)S(1)}, u32[]{:S(2)}, u32[]{:S(2)}) collective-permute-start(f32[32,1024]{1,0:T(8,128)S(1)} %get-tuple-element.47), channel_id=1, source_target_pairs={{0,8},{4,12},{8,0},{12,4},{16,24},{20,28},{24,16},{28,20},{1,9},{5... | collective-permute-start | bytes 393224 | tf_op jit(solution)/shard_map/ppermute | solution.py:319
  75.8 5.0 %collective-permute-start.24 = (f32[32,1024]{1,0:T(8,128)S(1)}, f32[32,1024]{1,0:T(8,128)S(1)}, u32[]{:S(2)}, u32[]{:S(2)}) collective-permute-start(f32[32,1024]{1,0:T(8,128)S(1)} %get-tuple-element.46), channel_id=1, source_target_pairs={{0,16},{4,20},{8,24},{12,28},{16,0},{20,4},{24,8},{28,12},{1,17},{... | collective-permute-start | bytes 393224 | tf_op jit(solution)/shard_map/ppermute | solution.py:319
  78.4 2.6 %copy-start.2 = (f32[2048,128]{1,0:T(8,128)S(1)}, f32[2048,128]{1,0:T(8,128)}, u32[]{:S(2)}) copy-start(f32[2048,128]{1,0:T(8,128)} %vectors_ref.5) | copy-start | bytes 3145732
  78.4 2.6 %copy-start.5 = (f32[1024]{0:T(1024)S(1)}, f32[1024]{0:T(1024)}, u32[]{:S(2)}) copy-start(f32[1024]{0:T(1024)} %param.10) | copy-start | bytes 12292
  78.5 2.4 %collective-permute-start.42 = (f32[64,1024]{1,0:T(8,128)S(1)}, f32[64,1024]{1,0:T(8,128)S(1)}, u32[]{:S(2)}, u32[]{:S(2)}) collective-permute-start(f32[64,1024]{1,0:T(8,128)S(1)} %constant_dynamic-update-slice_fusion.4), channel_id=1, source_target_pairs={{0,4},{4,0},{8,12},{12,8},{16,20},{20,16},{24,28},{28,24},{1,5},{5... | collective-permute-start | bytes 786440 | tf_op jit(solution)/shard_map/ppermute | solution.py:324
  80.8 13.0 %collective-permute-start.26 = (f32[64,1024]{1,0:T(8,128)S(1)}, f32[64,1024]{1,0:T(8,128)S(1)}, u32[]{:S(2)}, u32[]{:S(2)}) collective-permute-start(f32[64,1024]{1,0:T(8,128)S(1)} %constant_dynamic-update-slice_fusion.2), channel_id=1, source_target_pairs={{0,4},{4,0},{8,12},{12,8},{16,20},{20,16},{24,28},{28,24},{1,5},{5... | collective-permute-start | bytes 786440 | tf_op jit(solution)/shard_map/ppermute | solution.py:324
  81.0 12.9 %slice-start = ((s8[8388608]{0:T(1024)(128)(4,1)}), s8[4194304]{0:T(1024)(128)(4,1)S(1)}, s32[]{:S(2)}) async-start(s8[8388608]{0:T(1024)(128)(4,1)} %bitcast.70), calls=%async_computation | async-start | bytes 8388608
  81.1 12.9 %slice-start.1 = ((s8[8388608]{0:T(1024)(128)(4,1)}), s8[4194304]{0:T(1024)(128)(4,1)S(1)}, s32[]{:S(2)}) async-start(s8[8388608]{0:T(1024)(128)(4,1)} %bitcast.70), calls=%async_computation.1 | async-start | bytes 8388608
  91.0 11.9 %collective-permute-start.45 = (f32[32,2048]{1,0:T(8,128)S(1)}, f32[32,2048]{1,0:T(8,128)S(1)}, u32[]{:S(2)}, u32[]{:S(2)}) collective-permute-start(f32[32,2048]{1,0:T(8,128)S(1)} %get-tuple-element.65), channel_id=1, source_target_pairs={{0,1},{3,2},{4,5},{7,6},{8,9},{11,10},{12,13},{15,14},{16,17},{19,... | collective-permute-start | bytes 786440 | tf_op jit(solution)/shard_map/ppermute | solution.py:296
  92.5 13.2 %collective-permute-start.43 = (f32[32,2048]{1,0:T(8,128)S(1)}, f32[32,2048]{1,0:T(8,128)S(1)}, u32[]{:S(2)}, u32[]{:S(2)}) collective-permute-start(f32[32,2048]{1,0:T(8,128)S(1)} %get-tuple-element.66), channel_id=1, source_target_pairs={{0,1},{3,2},{4,5},{7,6},{8,9},{11,10},{12,13},{15,14},{16,17},{19,... | collective-permute-start | bytes 786440 | tf_op jit(solution)/shard_map/ppermute | solution.py:296
  100.2 10.1 %collective-permute-start.29 = (f32[32,2048]{1,0:T(8,128)S(1)}, f32[32,2048]{1,0:T(8,128)S(1)}, u32[]{:S(2)}, u32[]{:S(2)}) collective-permute-start(f32[32,2048]{1,0:T(8,128)S(1)} %get-tuple-element.69), channel_id=1, source_target_pairs={{0,1},{3,2},{4,5},{7,6},{8,9},{11,10},{12,13},{15,14},{16,17},{19,... | collective-permute-start | bytes 786440 | tf_op jit(solution)/shard_map/ppermute | solution.py:296
  101.6 14.4 %collective-permute-start.27 = (f32[32,2048]{1,0:T(8,128)S(1)}, f32[32,2048]{1,0:T(8,128)S(1)}, u32[]{:S(2)}, u32[]{:S(2)}) collective-permute-start(f32[32,2048]{1,0:T(8,128)S(1)} %get-tuple-element.70), channel_id=1, source_target_pairs={{0,1},{3,2},{4,5},{7,6},{8,9},{11,10},{12,13},{15,14},{16,17},{19,... | collective-permute-start | bytes 786440 | tf_op jit(solution)/shard_map/ppermute | solution.py:296
  102.9 18.7 %collective-permute-start.47 = (f32[32,2048]{1,0:T(8,128)S(1)}, f32[32,2048]{1,0:T(8,128)S(1)}, u32[]{:S(2)}, u32[]{:S(2)}) collective-permute-start(f32[32,2048]{1,0:T(8,128)S(1)} %get-tuple-element.64), channel_id=1, source_target_pairs={{0,1},{1,0},{2,3},{3,2},{4,5},{5,4},{6,7},{7,6},{8,9},{9,8},{10,11... | collective-permute-start | bytes 786440 | tf_op jit(solution)/shard_map/ppermute | solution.py:300
  103.0 23.9 %collective-permute-start.31 = (f32[32,2048]{1,0:T(8,128)S(1)}, f32[32,2048]{1,0:T(8,128)S(1)}, u32[]{:S(2)}, u32[]{:S(2)}) collective-permute-start(f32[32,2048]{1,0:T(8,128)S(1)} %get-tuple-element.68), channel_id=1, source_target_pairs={{0,1},{1,0},{2,3},{3,2},{4,5},{5,4},{6,7},{7,6},{8,9},{9,8},{10,11... | collective-permute-start | bytes 786440 | tf_op jit(solution)/shard_map/ppermute | solution.py:300
  105.7 21.2 %collective-permute-start.46 = (f32[32,2048]{1,0:T(8,128)}, f32[32,2048]{1,0:T(8,128)S(1)}, u32[]{:S(2)}, u32[]{:S(2)}) collective-permute-start(f32[32,2048]{1,0:T(8,128)} %add.302), channel_id=1, source_target_pairs={{1,2},{2,1},{5,6},{6,5},{9,10},{10,9},{13,14},{14,13},{17,18},{18,... | collective-permute-start | bytes 786440 | tf_op jit(solution)/shard_map/ppermute | solution.py:297
  107.2 27.4 %copy-start.1 = (f32[512]{0:T(512)S(1)}, f32[512]{0:T(512)}, u32[]{:S(2)}) copy-start(f32[512]{0:T(512)} %param.13) | copy-start | bytes 6148
  107.2 27.4 %copy-start.4 = (s32[256]{0:T(256)S(1)}, s32[256]{0:T(256)}, u32[]{:S(2)}) copy-start(s32[256]{0:T(256)} %param.14) | copy-start | bytes 3076
  107.2 27.4 %copy-start.6 = (s32[256]{0:T(256)S(1)}, s32[256]{0:T(256)}, u32[]{:S(2)}) copy-start(s32[256]{0:T(256)} %param.15) | copy-start | bytes 3076
  110.4 16.5 %collective-permute-start.44 = (f32[32,2048]{1,0:T(8,128)}, f32[32,2048]{1,0:T(8,128)S(1)}, u32[]{:S(2)}, u32[]{:S(2)}) collective-permute-start(f32[32,2048]{1,0:T(8,128)} %add.301), channel_id=1, source_target_pairs={{1,3},{2,0},{5,7},{6,4},{9,11},{10,8},{13,15},{14,12},{17,19},{18,... | collective-permute-start | bytes 786440 | tf_op jit(solution)/shard_map/ppermute | solution.py:297
  116.0 10.9 %collective-permute-start.30 = (f32[32,2048]{1,0:T(8,128)}, f32[32,2048]{1,0:T(8,128)S(1)}, u32[]{:S(2)}, u32[]{:S(2)}) collective-permute-start(f32[32,2048]{1,0:T(8,128)} %add.289), channel_id=1, source_target_pairs={{1,2},{2,1},{5,6},{6,5},{9,10},{10,9},{13,14},{14,13},{17,18},{18,... | collective-permute-start | bytes 786440 | tf_op jit(solution)/shard_map/ppermute | solution.py:297
  121.6 11.7 %collective-permute-start.28 = (f32[32,2048]{1,0:T(8,128)}, f32[32,2048]{1,0:T(8,128)S(1)}, u32[]{:S(2)}, u32[]{:S(2)}) collective-permute-start(f32[32,2048]{1,0:T(8,128)} %add.288), channel_id=1, source_target_pairs={{1,3},{2,0},{5,7},{6,4},{9,11},{10,8},{13,15},{14,12},{17,19},{18,... | collective-permute-start | bytes 786440 | tf_op jit(solution)/shard_map/ppermute | solution.py:297
where the time goes:
time: 136 us; the launch traced here: 135 us
  waiting for transfers between devices  54.7 us (40%)
  starting transfers between devices  38.7 us (28%)
  Pallas kernels  35.1 us (26%)
  other arithmetic  4.25 us (3%)
  between operations  1.48 us (1%)
    ppermute x4, waiting for transfers between devices, gather_line(): came_right = lax.ppermute(from_right, axis, left)  20.1 us
    pallas_call x2, Pallas kernels, image(): pl.pallas_call(image_kernel, out_shape=jax.ShapeDtypeStruct((count, rows)...  16.1 us
    pallas_call x2, Pallas kernels, product(): pl.pallas_call(functools.partial(product_kernel, width, n), out_shape=jax...  14.7 us
    ppermute x4, starting transfers between devices, gather_line(): came_left = lax.ppermute(from_left, axis, right)  10.9 us
    ppermute x8, waiting for transfers between devices, sum_pairs(): lax.ppermute(pieces[i], axis, [(d, d ^ bit) for d in range(n)])  8.13 us
    ppermute x8, starting transfers between devices, sum_pairs(): lax.ppermute(pieces[i], axis, [(d, d ^ bit) for d in range(n)])  8.12 us
    ppermute x4, waiting for transfers between devices, scatter_line(): rows = part + lax.ppermute(rows, axis, mirrored(n, [(hop, hop + 1)]))  6.8 us
    ppermute x2, waiting for transfers between devices, scatter_line(): terms.append(lax.ppermute(block(base + (place + step) % half), axis, turn))  6.71 us
  transfers between devices with their start and end apart: 32, of which 19 were waited for; matrix products, arithmetic and copies ran while one was open for 3% of the time, Pallas kernels for 23%

commit v1 on v0

--- a/solution.py
+++ b/solution.py
@@ -84,12 +84,13 @@
     source_t = steps(spots_t, width, n)
     peers = jnp.logical_and(jnp.logical_and(source == source_t, part == part_t), spots_t < spots)
     rank = jnp.sum(jnp.where(peers, 1.0, 0.0), axis=1, keepdims=True)
-    wide = info_ref.shape[1]
+    wide = info_ref.shape[2]
     lane = lax.broadcasted_iota(jnp.int32, (count, wide), 1)
     info = jnp.zeros((count, wide), F32)
     for k, col in enumerate((spot, rank, value, gap, row.T[:, :1])):
         info = jnp.where(lane == k, col, info)
-    info_ref[...] = info
+    for p in range(parts):
+        info_ref[p] = info[p * (count // parts) : (p + 1) * (count // parts)]
 
     base = (me * width).astype(F32)
     here = lax.broadcasted_iota(jnp.int32, (count, width), 1).astype(F32) + base == spot
@@ -117,7 +118,7 @@
     return pl.pallas_call(
         functools.partial(plan_kernel, n, PARTS, room),
         out_shape=(
-            jax.ShapeDtypeStruct((count, 128), F32),
+            jax.ShapeDtypeStruct((PARTS, count // PARTS, 128), F32),
             jax.ShapeDtypeStruct((PARTS, room, rows), F32),
         ),
         in_specs=[SMEM] + [VMEM] * 5,
@@ -136,88 +137,74 @@
     for b in range(len(buffers)):
         inside = jnp.logical_and(lane >= b * room, lane < (b + 1) * room)
         owner = jnp.where(inside, source_ref[b], owner)
-    slot = lax.broadcasted_iota(jnp.int32, (rows, slots), 1).astype(F32)
+    slot = lane.astype(F32)
     slot = slot - room * steps(slot, room, len(buffers))
     place = jnp.logical_and(
         steps(info_ref[:, 0:1], width, n) == owner.astype(F32), info_ref[:, 1:2] == slot
     )
     place = jnp.where(place, 1.0, 0.0).astype(BF16)
-    gathered = jnp.concatenate([b[...] for b in buffers], 0)
-    high, low = (dot(place, p, ((1,), (0,))).astype(BF16) for p in split(gathered, 2))
-    x_high, x_low = split(high_ref[...], 2)
-    term = dot(high, x_high, ((1,), (0,))) + dot(low, x_high, ((1,), (0,)))
-    term = term + dot(high, x_low, ((1,), (0,)))
-
-    @pl.when(pl.program_id(0) == 0)
-    def _():
-        out_ref[...] = term
-
-    @pl.when(pl.program_id(0) > 0)
-    def _():
-        out_ref[...] += term
-
-
-def product(part, width, info, buffers, high_vectors):
-    n = lax.axis_size("col")
+    depth = high_ref.shape[0]
+    piece = min(depth, 512)
+    terms = []
+    for start in range(0, depth, piece):
+        span = slice(start, start + piece)
+        gathered = jnp.concatenate([b[:, span] for b in buffers], 0)
+        high, low = (dot(place, p, ((1,), (0,))).astype(BF16) for p in split(gathered, 2))
+        x_high, x_low = split(high_ref[span], 2)
+        left = jnp.concatenate([high, low, high], 1)
+        terms.append(dot(left, jnp.concatenate([x_high, x_high, x_low], 0), ((1,), (0,))))
+    out_ref[...] = total(terms)
+
+
+def cost(count, high_vectors):
     rows, k = high_vectors.shape
-    count = info.shape[0] // PARTS
-    room = buffers[0][0].shape[0]
-    piece = min(rows, 256)
+    return pl.CostEstimate(
+        flops=6 * count * rows * k, bytes_accessed=4 * rows * k, transcendentals=0
+    )
+
+
+def product(width, info, buffers, high_vectors):
+    n = lax.axis_size("col")
+    count = info.shape[0]
     sources = jnp.stack([jnp.asarray(src, jnp.int32) for _, src in buffers])
     return pl.pallas_call(
         functools.partial(product_kernel, width, n),
-        out_shape=jax.ShapeDtypeStruct((count, k), F32),
-        grid=(rows // piece,),
-        in_specs=[SMEM, pl.BlockSpec((count, info.shape[1]), lambda i: (part, 0))]
-        + [pl.BlockSpec((room, piece), lambda i: (0, i)) for _ in buffers]
-        + [pl.BlockSpec((piece, k), lambda i: (i, 0))],
-        out_specs=pl.BlockSpec((count, k), lambda i: (0, 0)),
-        compiler_params=pltpu.CompilerParams(vmem_limit_bytes=24 << 20),
-        cost_estimate=pl.CostEstimate(
-            flops=6 * count * rows * k, bytes_accessed=4 * rows * k, transcendentals=0
-        ),
+        out_shape=jax.ShapeDtypeStruct((count, high_vectors.shape[1]), F32),
+        in_specs=[SMEM] + [VMEM] * (len(buffers) + 2),
+        out_specs=VMEM,
+        compiler_params=pltpu.CompilerParams(vmem_limit_bytes=40 << 20),
+        cost_estimate=cost(count, high_vectors),
     )(sources, info, *[b for b, _ in buffers], high_vectors)
 
 
-def image_kernel(me_ref, info_ref, sums_ref, mu_ref, vectors_ref, high_ref, out_ref, d_high, d_low):
-    @pl.when(pl.program_id(0) == 0)
-    def _():
-        gaps = info_ref[:, 3:4] * (mu_ref[...] - info_ref[:, 2:3])
-        high, low = split(sums_ref[...] / gaps, 2)
-        d_high[...] = high
-        d_low[...] = low
-
+def image_kernel(me_ref, info_ref, sums_ref, mu_ref, vectors_ref, high_ref, out_ref):
+    count = info_ref.shape[0]
+    gaps = info_ref[:, 3:4] * (mu_ref[...] - info_ref[:, 2:3])
+    d_high, d_low = split(sums_ref[...] / gaps, 2)
+    both = jnp.concatenate([d_high, d_low], 0)
     width = vectors_ref.shape[1]
-    spot = lax.broadcasted_iota(jnp.int32, (info_ref.shape[0], width), 1) + me_ref[0] * width
+    spot = lax.broadcasted_iota(jnp.int32, (count, width), 1) + me_ref[0] * width
     mine = jnp.where(spot.astype(F32) == info_ref[:, 0:1], 1.0, 0.0).astype(BF16)
-    chosen = total([dot(mine, p, ((1,), (1,))) for p in split(vectors_ref[...], 3)])
-    x_high, x_low = split(high_ref[...], 2)
-    image = dot(d_high[...], x_high, ((1,), (1,))) + dot(d_low[...], x_high, ((1,), (1,)))
-    out_ref[...] = chosen - (image + dot(d_high[...], x_low, ((1,), (1,))))
-
-
-def image(part, me, info, sums, high_values, pool_vectors, high_vectors):
-    rows, k = high_vectors.shape
-    count = sums.shape[0]
-    piece = min(rows, 256)
+    depth = high_ref.shape[0]
+    piece = min(depth, 256)
+    for start in range(0, depth, piece):
+        span = slice(start, start + piece)
+        chosen = total([dot(mine, p, ((1,), (1,))) for p in split(vectors_ref[span], 3)])
+        x_high, x_low = split(high_ref[span], 2)
+        image = dot(both, x_high, ((1,), (1,)))
+        image = image[:count] + image[count:] + dot(d_high, x_low, ((1,), (1,)))
+        out_ref[:, span] = chosen - image
+
+
+def image(me, info, sums, high_values, pool_vectors, high_vectors):
+    count = info.shape[0]
     return pl.pallas_call(
         image_kernel,
-        out_shape=jax.ShapeDtypeStruct((count, rows), F32),
-        grid=(rows // piece,),
-        in_specs=[
-            SMEM,
-            pl.BlockSpec((count, info.shape[1]), lambda i: (part, 0)),
-            pl.BlockSpec((count, k), lambda i: (0, 0)),
-            pl.BlockSpec((1, k), lambda i: (0, 0)),
-            pl.BlockSpec((piece, pool_vectors.shape[1]), lambda i: (i, 0)),
-            pl.BlockSpec((piece, k), lambda i: (i, 0)),
-        ],
-        out_specs=pl.BlockSpec((count, piece), lambda i: (0, i)),
-        scratch_shapes=[pltpu.VMEM((count, k), BF16)] * 2,
-        compiler_params=pltpu.CompilerParams(vmem_limit_bytes=24 << 20),
-        cost_estimate=pl.CostEstimate(
-            flops=6 * count * rows * k, bytes_accessed=4 * rows * k, transcendentals=0
-        ),
+        out_shape=jax.ShapeDtypeStruct((count, high_vectors.shape[0]), F32),
+        in_specs=[SMEM] + [VMEM] * 5,
+        out_specs=VMEM,
+        compiler_params=pltpu.CompilerParams(vmem_limit_bytes=40 << 20),
+        cost_estimate=cost(count, high_vectors),
     )(me[None], info, sums, high_values[None, :], pool_vectors, high_vectors)
 
 
@@ -336,13 +323,13 @@
     info, own = plan(room, me, cluster, gap, pool_values, pool_vectors, pool_images)
     gathered = [gather_line(own[p], "col") for p in range(PARTS)]
     sums = [
-        sum_pairs(product(p, width, info, gathered[p], high_vectors), "row") for p in range(PARTS)
+        sum_pairs(product(width, info[p], gathered[p], high_vectors), "row") for p in range(PARTS)
     ]
     terms = []
     for p in range(PARTS):
-        partial = image(p, me, info, sums[p], high_values, pool_vectors, high_vectors)
+        partial = image(me, info[p], sums[p], high_values, pool_vectors, high_vectors)
         terms += scatter_line(partial.reshape(n, count // (n * PARTS), -1), "col")
-    return finish(me, info, terms).T, jnp.max(info[:, 1]) + 1.0
+    return finish(me, info.reshape(count, -1), terms).T, jnp.max(info[:, :, 1]) + 1.0
 
 
 def correct_whole(high_vectors, high_values, pool_vectors, pool_images, pool_values, cluster, gap):

time: 136 us -> 127 us (0.934)
  Pallas kernels: 35.1 us -> 22.9 us
  waiting for transfers between devices: 54.7 us -> 57 us
    pallas_call x2, Pallas kernels: 16.1 us -> 9.61 us  [image(): pl.pallas_call(image_kernel, out_shape=jax.ShapeDtypeStruct((count, high_...]
    pallas_call x2, Pallas kernels: 14.7 us -> 8.98 us  [product(): pl.pallas_call(functools.partial(product_kernel, width, n), out_shape=jax...]
    ppermute x4, waiting for transfers between devices: 6.8 us -> 8.9 us  [scatter_line(): rows = part + lax.ppermute(rows, axis, mirrored(n, [(hop, hop + 1)]))]
  transfers between devices with their start and end apart: 32 -> 32, of which waited for: 19 -> 20; matrix products, arithmetic and copies ran while one was open for 3% -> 4% of each run, Pallas kernels for 23% -> 15%
where the time goes in v1:
time: 127 us; the launch traced here: 126 us
  waiting for transfers between devices  57 us (45%)
  starting transfers between devices  39.1 us (31%)
  Pallas kernels  22.9 us (18%)
  other arithmetic  4.21 us (3%)
  between operations  1.41 us (1%)
    ppermute x4, waiting for transfers between devices, gather_line(): came_right = lax.ppermute(from_right, axis, left)  20.1 us
    ppermute x4, starting transfers between devices, gather_line(): came_left = lax.ppermute(from_left, axis, right)  10.9 us
    pallas_call x2, Pallas kernels, image(): pl.pallas_call(image_kernel, out_shape=jax.ShapeDtypeStruct((count, high_...  9.61 us
    pallas_call x2, Pallas kernels, product(): pl.pallas_call(functools.partial(product_kernel, width, n), out_shape=jax...  8.98 us
    ppermute x4, waiting for transfers between devices, scatter_line(): rows = part + lax.ppermute(rows, axis, mirrored(n, [(hop, hop + 1)]))  8.9 us
    ppermute x8, starting transfers between devices, sum_pairs(): lax.ppermute(pieces[i], axis, [(d, d ^ bit) for d in range(n)])  8.24 us
    ppermute x8, waiting for transfers between devices, sum_pairs(): lax.ppermute(pieces[i], axis, [(d, d ^ bit) for d in range(n)])  8.05 us
    ppermute x2, waiting for transfers between devices, scatter_line(): terms.append(lax.ppermute(block(base + (place + step) % half), axis, turn))  7.02 us
  transfers between devices with their start and end apart: 32, of which 20 were waited for; matrix products, arithmetic and copies ran while one was open for 4% of the time, Pallas kernels for 15%

profile of v1, /device:TPU:0, one launch (start us, length us, event | category | flops | bytes accessed | tf_op | source)
XLA Modules:
  0.0 126.1 jit_solution(4340562898612693571)
XLA Ops:
  0.0 3.1 %shard_map.75 = (f32[2,128,128]{2,1,0:T(8,128)S(1)}, f32[2,40,2048]{2,1,0:T(8,128)S(1)}) custom-call(s32[1]{0:T(128)} %bitcast.7.me_ref, s32[1,256]{1,0:T(1,128)} %bitcast.84, s32[1,256]{1,0:T(1,128)} %bitcast.87, f32[1,512]{1,0:T(1,128)} %bitcast.80, f32[2048,128]{1,0:T(8,128)} %vectors_ref.5, f32[2048,128]{1,0:T(8,128)} %images_ref.1), custom_call_target="tpu_custom_call" | custom-call | tf_op jit(solution)/shard_map/pallas_call | solution.py:118
  3.2 4.9 %collective-permute-start.32 = (f32[40,2048]{1,0:T(8,128)S(1)}, f32[40,2048]{1,0:T(8,128)S(1)}, u32[]{:S(2)}, u32[]{:S(2)}) collective-permute-start(f32[40,2048]{1,0:T(8,128)S(1)} %get-tuple-element.72.refs_0_), channel_id=1, source_target_pairs={{0,1},{1,2},{2,3},{4,5},{5,6},{6,7},{8,9},{9,10},{10,11},{12,13},{... | collective-permute-start | bytes 983048 | tf_op jit(solution)/shard_map/ppermute | solution.py:255
  8.1 1.3 %collective-permute-start.33 = (f32[40,2048]{1,0:T(8,128)S(1)}, f32[40,2048]{1,0:T(8,128)S(1)}, u32[]{:S(2)}, u32[]{:S(2)}) collective-permute-start(f32[40,2048]{1,0:T(8,128)S(1)} %get-tuple-element.72.refs_0_), channel_id=1, source_target_pairs={{1,0},{2,1},{3,2},{5,4},{6,5},{7,6},{9,8},{10,9},{11,10},{13,12},{... | collective-permute-start | bytes 983048 | tf_op jit(solution)/shard_map/ppermute | solution.py:256
  9.4 4.6 %collective-permute-start.16 = (f32[40,2048]{1,0:T(8,128)S(1)}, f32[40,2048]{1,0:T(8,128)S(1)}, u32[]{:S(2)}, u32[]{:S(2)}) collective-permute-start(f32[40,2048]{1,0:T(8,128)S(1)} %get-tuple-element.73.refs_0_), channel_id=1, source_target_pairs={{0,1},{1,2},{2,3},{4,5},{5,6},{6,7},{8,9},{9,10},{10,11},{12,13},{... | collective-permute-start | bytes 983048 | tf_op jit(solution)/shard_map/ppermute | solution.py:255
  14.0 1.3 %collective-permute-start.17 = (f32[40,2048]{1,0:T(8,128)S(1)}, f32[40,2048]{1,0:T(8,128)S(1)}, u32[]{:S(2)}, u32[]{:S(2)}) collective-permute-start(f32[40,2048]{1,0:T(8,128)S(1)} %get-tuple-element.73.refs_0_), channel_id=1, source_target_pairs={{1,0},{2,1},{3,2},{5,4},{6,5},{7,6},{9,8},{10,9},{11,10},{13,12},{... | collective-permute-start | bytes 983048 | tf_op jit(solution)/shard_map/ppermute | solution.py:256
  15.3 0.9 collective-permute-done.32.refs_1_
  16.2 0.7 collective-permute-start.34
  16.9 3.8 %collective-permute-done.33.refs_2_ = f32[40,2048]{1,0:T(8,128)S(1)} collective-permute-done((f32[40,2048]{1,0:T(8,128)S(1)}, f32[40,2048]{1,0:T(8,128)S(1)}, u32[]{:S(2)}, u32[]{:S(2)}) %collective-permute-start.33) | collective-permute-done | bytes 327712 | tf_op jit(solution)/shard_map/ppermute | solution.py:256
  20.7 1.3 %collective-permute-start.35 = (f32[40,2048]{1,0:T(8,128)S(1)}, f32[40,2048]{1,0:T(8,128)S(1)}, u32[]{:S(2)}, u32[]{:S(2)}) collective-permute-start(f32[40,2048]{1,0:T(8,128)S(1)} %collective-permute-done.33.refs_2_), channel_id=1, source_target_pairs={{1,0},{2,1},{5,4},{6,5},{9,8},{10,9},{13,12},{14,13},{17,16},{18,1... | collective-permute-start | bytes 983048 | tf_op jit(solution)/shard_map/ppermute | solution.py:256
  21.9 0.1 collective-permute-done.16.refs_1_
  22.1 0.7 collective-permute-start.18
  22.8 4.9 %collective-permute-done.17.refs_2_ = f32[40,2048]{1,0:T(8,128)S(1)} collective-permute-done((f32[40,2048]{1,0:T(8,128)S(1)}, f32[40,2048]{1,0:T(8,128)S(1)}, u32[]{:S(2)}, u32[]{:S(2)}) %collective-permute-start.17) | collective-permute-done | bytes 327712 | tf_op jit(solution)/shard_map/ppermute | solution.py:256
  27.7 1.3 %collective-permute-start.19 = (f32[40,2048]{1,0:T(8,128)S(1)}, f32[40,2048]{1,0:T(8,128)S(1)}, u32[]{:S(2)}, u32[]{:S(2)}) collective-permute-start(f32[40,2048]{1,0:T(8,128)S(1)} %collective-permute-done.17.refs_2_), channel_id=1, source_target_pairs={{1,0},{2,1},{5,4},{6,5},{9,8},{10,9},{13,12},{14,13},{17,16},{18,1... | collective-permute-start | bytes 983048 | tf_op jit(solution)/shard_map/ppermute | solution.py:256
  29.0 5.7 %collective-permute-done.35 = f32[40,2048]{1,0:T(8,128)S(1)} collective-permute-done((f32[40,2048]{1,0:T(8,128)S(1)}, f32[40,2048]{1,0:T(8,128)S(1)}, u32[]{:S(2)}, u32[]{:S(2)}) %collective-permute-start.35) | collective-permute-done | bytes 327712 | tf_op jit(solution)/shard_map/ppermute | solution.py:256
  34.8 1.3 %collective-permute-start.36 = (f32[40,2048]{1,0:T(8,128)S(1)}, f32[40,2048]{1,0:T(8,128)S(1)}, u32[]{:S(2)}, u32[]{:S(2)}) collective-permute-start(f32[40,2048]{1,0:T(8,128)S(1)} %add.295.refs_3_), channel_id=1, source_target_pairs={{2,3},{1,0},{6,7},{5,4},{10,11},{9,8},{14,15},{13,12},{18,19},{17,... | collective-permute-start | bytes 983048 | tf_op jit(solution)/shard_map/ppermute | solution.py:253
  36.1 5.7 %collective-permute-done.19 = f32[40,2048]{1,0:T(8,128)S(1)} collective-permute-done((f32[40,2048]{1,0:T(8,128)S(1)}, f32[40,2048]{1,0:T(8,128)S(1)}, u32[]{:S(2)}, u32[]{:S(2)}) %collective-permute-start.19) | collective-permute-done | bytes 327712 | tf_op jit(solution)/shard_map/ppermute | solution.py:256
  41.8 1.3 %collective-permute-start.20 = (f32[40,2048]{1,0:T(8,128)S(1)}, f32[40,2048]{1,0:T(8,128)S(1)}, u32[]{:S(2)}, u32[]{:S(2)}) collective-permute-start(f32[40,2048]{1,0:T(8,128)S(1)} %add.279.refs_3_), channel_id=1, source_target_pairs={{2,3},{1,0},{6,7},{5,4},{10,11},{9,8},{14,15},{13,12},{18,19},{17,... | collective-permute-start | bytes 983048 | tf_op jit(solution)/shard_map/ppermute | solution.py:253
  43.1 0.1 stack.29.source_ref
  43.2 5.5 %collective-permute-done.36.refs_4_ = f32[40,2048]{1,0:T(8,128)S(1)} collective-permute-done((f32[40,2048]{1,0:T(8,128)S(1)}, f32[40,2048]{1,0:T(8,128)S(1)}, u32[]{:S(2)}, u32[]{:S(2)}) %collective-permute-start.36) | collective-permute-done | bytes 327712 | tf_op jit(solution)/shard_map/ppermute | solution.py:253
  48.7 6.0 %shard_map.78 = f32[128,1024]{1,0:T(8,128)S(1)} custom-call(s32[5]{0:T(128)S(1)} %stack.29.source_ref, f32[128,128]{1,0:T(8,128)S(1)} %get-tuple-element.86.info_ref, f32[40,2048]{1,0:T(8,128)S(1)} %get-tuple-element.72.refs_0_, f32[40,2048]{1,0:T(8,128)S(1)} %collective-permute-done.32.refs_1_, f32[40,2048]{1,0:T(8,128)S(1)} %collective-permute-done.33.refs_2_, ...), custom_call_target="tpu_custom_call" | custom-call | flops 1610612736 | bytes 8388608 | tf_op jit(solution)/shard_map/pallas_call | solution.py:170
  54.8 0.1 collective-permute-start.37
  54.9 3.0 %shard_map.76 = f32[128,1024]{1,0:T(8,128)S(1)} custom-call(s32[5]{0:T(128)S(1)} %stack.29.source_ref, f32[128,128]{1,0:T(8,128)S(1)} %get-tuple-element.87.info_ref, f32[40,2048]{1,0:T(8,128)S(1)} %get-tuple-element.73.refs_0_, f32[40,2048]{1,0:T(8,128)S(1)} %collective-permute-done.16.refs_1_, f32[40,2048]{1,0:T(8,128)S(1)} %collective-permute-done.17.refs_2_, ...), custom_call_target="tpu_custom_call" | custom-call | flops 1610612736 | bytes 8388608 | tf_op jit(solution)/shard_map/pallas_call | solution.py:170
  57.9 0.6 collective-permute-start.21
  58.5 1.6 %collective-permute-start.38 = (f32[32,1024]{1,0:T(8,128)S(1)}, f32[32,1024]{1,0:T(8,128)S(1)}, u32[]{:S(2)}, u32[]{:S(2)}) collective-permute-start(f32[32,1024]{1,0:T(8,128)S(1)} %get-tuple-element.81), channel_id=1, source_target_pairs={{0,8},{4,12},{8,0},{12,4},{16,24},{20,28},{24,16},{28,20},{1,9},{5... | collective-permute-start | bytes 393224 | tf_op jit(solution)/shard_map/ppermute | solution.py:306
  60.1 1.5 %collective-permute-start.39 = (f32[32,1024]{1,0:T(8,128)S(1)}, f32[32,1024]{1,0:T(8,128)S(1)}, u32[]{:S(2)}, u32[]{:S(2)}) collective-permute-start(f32[32,1024]{1,0:T(8,128)S(1)} %get-tuple-element.80), channel_id=1, source_target_pairs={{0,16},{4,20},{8,24},{12,28},{16,0},{20,4},{24,8},{28,12},{1,17},{... | collective-permute-start | bytes 393224 | tf_op jit(solution)/shard_map/ppermute | solution.py:306
  61.7 0.6 collective-permute-start.22
  62.3 0.5 collective-permute-start.23
  62.8 1.4 %collective-permute-done.38 = f32[32,1024]{1,0:T(8,128)S(1)} collective-permute-done((f32[32,1024]{1,0:T(8,128)S(1)}, f32[32,1024]{1,0:T(8,128)S(1)}, u32[]{:S(2)}, u32[]{:S(2)}) %collective-permute-start.38) | collective-permute-done | bytes 131104 | tf_op jit(solution)/shard_map/ppermute | solution.py:306
  64.2 2.2 %collective-permute-done.39 = f32[32,1024]{1,0:T(8,128)S(1)} collective-permute-done((f32[32,1024]{1,0:T(8,128)S(1)}, f32[32,1024]{1,0:T(8,128)S(1)}, u32[]{:S(2)}, u32[]{:S(2)}) %collective-permute-start.39) | collective-permute-done | bytes 131104 | tf_op jit(solution)/shard_map/ppermute | solution.py:306
  66.4 0.1 collective-permute-start.41
  66.5 2.1 %collective-permute-start.40 = (f32[32,1024]{1,0:T(8,128)S(1)}, f32[32,1024]{1,0:T(8,128)S(1)}, u32[]{:S(2)}, u32[]{:S(2)}) collective-permute-start(f32[32,1024]{1,0:T(8,128)S(1)} %get-tuple-element.50), channel_id=1, source_target_pairs={{0,16},{4,20},{8,24},{12,28},{16,0},{20,4},{24,8},{28,12},{1,17},{... | collective-permute-start | bytes 393224 | tf_op jit(solution)/shard_map/ppermute | solution.py:306
  68.6 0.3 collective-permute-done.23
  68.9 1.3 %collective-permute-start.25 = (f32[32,1024]{1,0:T(8,128)S(1)}, f32[32,1024]{1,0:T(8,128)S(1)}, u32[]{:S(2)}, u32[]{:S(2)}) collective-permute-start(f32[32,1024]{1,0:T(8,128)S(1)} %get-tuple-element.47), channel_id=1, source_target_pairs={{0,8},{4,12},{8,0},{12,4},{16,24},{20,28},{24,16},{28,20},{1,9},{5... | collective-permute-start | bytes 393224 | tf_op jit(solution)/shard_map/ppermute | solution.py:306
  70.2 0.6 collective-permute-start.24
  70.8 1.7 %collective-permute-done.41 = f32[32,1024]{1,0:T(8,128)S(1)} collective-permute-done((f32[32,1024]{1,0:T(8,128)S(1)}, f32[32,1024]{1,0:T(8,128)S(1)}, u32[]{:S(2)}, u32[]{:S(2)}) %collective-permute-start.41) | collective-permute-done | bytes 131104 | tf_op jit(solution)/shard_map/ppermute | solution.py:306
  72.5 0.2 collective-permute-done.40
  72.9 1.0 collective-permute-done.25
  74.0 1.2 collective-permute-done.24
  75.5 6.4 %shard_map.79 = f32[128,2048]{1,0:T(8,128)S(1)} custom-call(s32[1]{0:T(128)} %bitcast.7.me_ref, f32[128,128]{1,0:T(8,128)S(1)} %get-tuple-element.86.info_ref, f32[128,1024]{1,0:T(8,128)S(1)} %pad_maximum_fusion.1.sums_ref, f32[1,1024]{1,0:T(1,128)S(1)} %bitcast.85, f32[2048,128]{1,0:T(8,128)S(1)} %copy-done.2, f32[2048,1024]{1,0:T(8,128)} %high_ref.3), custom_call_target="tpu_custom_call" | custom-call | flops 1610612736 | bytes 8388608 | tf_op jit(solution)/shard_map/pallas_call | solution.py:201
  81.9 0.1 dynamic-slice_bitcast_fusion.3
  82.0 1.5 %collective-permute-start.45 = (f32[32,2048]{1,0:T(8,128)S(1)}, f32[32,2048]{1,0:T(8,128)S(1)}, u32[]{:S(2)}, u32[]{:S(2)}) collective-permute-start(f32[32,2048]{1,0:T(8,128)S(1)} %get-tuple-element.65), channel_id=1, source_target_pairs={{0,1},{3,2},{4,5},{7,6},{8,9},{11,10},{12,13},{15,14},{16,17},{19,... | collective-permute-start | bytes 786440 | tf_op jit(solution)/shard_map/ppermute | solution.py:283
  83.5 1.5 %collective-permute-start.43 = (f32[32,2048]{1,0:T(8,128)S(1)}, f32[32,2048]{1,0:T(8,128)S(1)}, u32[]{:S(2)}, u32[]{:S(2)}) collective-permute-start(f32[32,2048]{1,0:T(8,128)S(1)} %get-tuple-element.66), channel_id=1, source_target_pairs={{0,1},{3,2},{4,5},{7,6},{8,9},{11,10},{12,13},{15,14},{16,17},{19,... | collective-permute-start | bytes 786440 | tf_op jit(solution)/shard_map/ppermute | solution.py:283
  85.1 3.2 %shard_map.77 = f32[128,2048]{1,0:T(8,128)S(1)} custom-call(s32[1]{0:T(128)} %bitcast.7.me_ref, f32[128,128]{1,0:T(8,128)S(1)} %get-tuple-element.87.info_ref, f32[128,1024]{1,0:T(8,128)S(1)} %pad_maximum_fusion.sums_ref, f32[1,1024]{1,0:T(1,128)S(1)} %bitcast.86, f32[2048,128]{1,0:T(8,128)S(1)} %copy-done.2, f32[2048,1024]{1,0:T(8,128)S(1)} %bitcast.77), custom_call_target="tpu_custom_call" | custom-call | flops 1610612736 | bytes 8388608 | tf_op jit(solution)/shard_map/pallas_call | solution.py:201
  88.3 0.8 dynamic-slice_bitcast_fusion.7
  89.1 1.3 %collective-permute-start.29 = (f32[32,2048]{1,0:T(8,128)S(1)}, f32[32,2048]{1,0:T(8,128)S(1)}, u32[]{:S(2)}, u32[]{:S(2)}) collective-permute-start(f32[32,2048]{1,0:T(8,128)S(1)} %get-tuple-element.69), channel_id=1, source_target_pairs={{0,1},{3,2},{4,5},{7,6},{8,9},{11,10},{12,13},{15,14},{16,17},{19,... | collective-permute-start | bytes 786440 | tf_op jit(solution)/shard_map/ppermute | solution.py:283
  90.4 1.3 %collective-permute-start.27 = (f32[32,2048]{1,0:T(8,128)S(1)}, f32[32,2048]{1,0:T(8,128)S(1)}, u32[]{:S(2)}, u32[]{:S(2)}) collective-permute-start(f32[32,2048]{1,0:T(8,128)S(1)} %get-tuple-element.70), channel_id=1, source_target_pairs={{0,1},{3,2},{4,5},{7,6},{8,9},{11,10},{12,13},{15,14},{16,17},{19,... | collective-permute-start | bytes 786440 | tf_op jit(solution)/shard_map/ppermute | solution.py:283
  91.8 2.0 %collective-permute-start.31 = (f32[32,2048]{1,0:T(8,128)}, f32[32,2048]{1,0:T(8,128)S(1)}, u32[]{:S(2)}, u32[]{:S(2)}) collective-permute-start(f32[32,2048]{1,0:T(8,128)} %get-tuple-element.68), channel_id=1, source_target_pairs={{0,1},{1,0},{2,3},{3,2},{4,5},{5,4},{6,7},{7,6},{8,9},{9,8},{10,11... | collective-permute-start | bytes 786440 | tf_op jit(solution)/shard_map/ppermute | solution.py:287
  93.8 0.8 add.302
  94.6 1.1 collective-permute-done.43
  95.7 0.7 collective-permute-start.46
  96.4 0.7 add.301
  97.1 4.2 %collective-permute-done.29 = f32[32,2048]{1,0:T(8,128)S(1)} collective-permute-done((f32[32,2048]{1,0:T(8,128)S(1)}, f32[32,2048]{1,0:T(8,128)S(1)}, u32[]{:S(2)}, u32[]{:S(2)}) %collective-permute-start.29) | collective-permute-done | bytes 262176 | tf_op jit(solution)/shard_map/ppermute | solution.py:283
  101.3 1.3 %collective-permute-start.44 = (f32[32,2048]{1,0:T(8,128)}, f32[32,2048]{1,0:T(8,128)S(1)}, u32[]{:S(2)}, u32[]{:S(2)}) collective-permute-start(f32[32,2048]{1,0:T(8,128)} %add.301), channel_id=1, source_target_pairs={{1,3},{2,0},{5,7},{6,4},{9,11},{10,8},{13,15},{14,12},{17,19},{18,... | collective-permute-start | bytes 786440 | tf_op jit(solution)/shard_map/ppermute | solution.py:284
  102.6 0.7 add.289
  103.3 3.6 %collective-permute-done.27 = f32[32,2048]{1,0:T(8,128)S(1)} collective-permute-done((f32[32,2048]{1,0:T(8,128)S(1)}, f32[32,2048]{1,0:T(8,128)S(1)}, u32[]{:S(2)}, u32[]{:S(2)}) %collective-permute-start.27) | collective-permute-done | bytes 262176 | tf_op jit(solution)/shard_map/ppermute | solution.py:283
  106.9 0.7 collective-permute-start.30
  107.6 0.8 add.288
  108.4 4.2 %collective-permute-done.47.refs_7_ = f32[32,2048]{1,0:T(8,128)S(1)} collective-permute-done((f32[32,2048]{1,0:T(8,128)S(1)}, f32[32,2048]{1,0:T(8,128)S(1)}, u32[]{:S(2)}, u32[]{:S(2)}) %collective-permute-start.47) | collective-permute-done | bytes 262176 | tf_op jit(solution)/shard_map/ppermute | solution.py:287
  112.5 1.3 %collective-permute-start.28 = (f32[32,2048]{1,0:T(8,128)}, f32[32,2048]{1,0:T(8,128)S(1)}, u32[]{:S(2)}, u32[]{:S(2)}) collective-permute-start(f32[32,2048]{1,0:T(8,128)} %add.288), channel_id=1, source_target_pairs={{1,3},{2,0},{5,7},{6,4},{9,11},{10,8},{13,15},{14,12},{17,19},{18,... | collective-permute-start | bytes 786440 | tf_op jit(solution)/shard_map/ppermute | solution.py:284
  113.8 0.7 slice_reduce_fusion
  115.2 2.8 %collective-permute-done.31.refs_3_ = f32[32,2048]{1,0:T(8,128)S(1)} collective-permute-done((f32[32,2048]{1,0:T(8,128)}, f32[32,2048]{1,0:T(8,128)S(1)}, u32[]{:S(2)}, u32[]{:S(2)}) %collective-permute-start.31) | collective-permute-done | bytes 262176 | tf_op jit(solution)/shard_map/ppermute | solution.py:287
  118.0 6.3 %collective-permute-done.28.refs_1_ = f32[32,2048]{1,0:T(8,128)S(1)} collective-permute-done((f32[32,2048]{1,0:T(8,128)}, f32[32,2048]{1,0:T(8,128)S(1)}, u32[]{:S(2)}, u32[]{:S(2)}) %collective-permute-start.28) | collective-permute-done | bytes 262176 | tf_op jit(solution)/shard_map/ppermute | solution.py:284
  124.4 1.2 shard_map.80
  125.6 0.3 conditional.1
  (56 shorter events, 0.9 us)
Async XLA Ops:
  3.2 13.0 %collective-permute-start.32 = (f32[40,2048]{1,0:T(8,128)S(1)}, f32[40,2048]{1,0:T(8,128)S(1)}, u32[]{:S(2)}, u32[]{:S(2)}) collective-permute-start(f32[40,2048]{1,0:T(8,128)S(1)} %get-tuple-element.72.refs_0_), channel_id=1, source_target_pairs={{0,1},{1,2},{2,3},{4,5},{5,6},{6,7},{8,9},{9,10},{10,11},{12,13},{... | collective-permute-start | bytes 983048 | tf_op jit(solution)/shard_map/ppermute | solution.py:255
  8.1 12.5 %collective-permute-start.33 = (f32[40,2048]{1,0:T(8,128)S(1)}, f32[40,2048]{1,0:T(8,128)S(1)}, u32[]{:S(2)}, u32[]{:S(2)}) collective-permute-start(f32[40,2048]{1,0:T(8,128)S(1)} %get-tuple-element.72.refs_0_), channel_id=1, source_target_pairs={{1,0},{2,1},{3,2},{5,4},{6,5},{7,6},{9,8},{10,9},{11,10},{13,12},{... | collective-permute-start | bytes 983048 | tf_op jit(solution)/shard_map/ppermute | solution.py:256
  9.4 12.7 %collective-permute-start.16 = (f32[40,2048]{1,0:T(8,128)S(1)}, f32[40,2048]{1,0:T(8,128)S(1)}, u32[]{:S(2)}, u32[]{:S(2)}) collective-permute-start(f32[40,2048]{1,0:T(8,128)S(1)} %get-tuple-element.73.refs_0_), channel_id=1, source_target_pairs={{0,1},{1,2},{2,3},{4,5},{5,6},{6,7},{8,9},{9,10},{10,11},{12,13},{... | collective-permute-start | bytes 983048 | tf_op jit(solution)/shard_map/ppermute | solution.py:255
  14.0 13.7 %collective-permute-start.17 = (f32[40,2048]{1,0:T(8,128)S(1)}, f32[40,2048]{1,0:T(8,128)S(1)}, u32[]{:S(2)}, u32[]{:S(2)}) collective-permute-start(f32[40,2048]{1,0:T(8,128)S(1)} %get-tuple-element.73.refs_0_), channel_id=1, source_target_pairs={{1,0},{2,1},{3,2},{5,4},{6,5},{7,6},{9,8},{10,9},{11,10},{13,12},{... | collective-permute-start | bytes 983048 | tf_op jit(solution)/shard_map/ppermute | solution.py:256
  16.2 12.8 %collective-permute-start.34 = (f32[40,2048]{1,0:T(8,128)S(1)}, f32[40,2048]{1,0:T(8,128)S(1)}, u32[]{:S(2)}, u32[]{:S(2)}) collective-permute-start(f32[40,2048]{1,0:T(8,128)S(1)} %collective-permute-done.32.refs_1_), channel_id=1, source_target_pairs={{1,2},{2,3},{5,6},{6,7},{9,10},{10,11},{13,14},{14,15},{17,18},{18... | collective-permute-start | bytes 983048 | tf_op jit(solution)/shard_map/ppermute | solution.py:255
  20.7 14.0 %collective-permute-start.35 = (f32[40,2048]{1,0:T(8,128)S(1)}, f32[40,2048]{1,0:T(8,128)S(1)}, u32[]{:S(2)}, u32[]{:S(2)}) collective-permute-start(f32[40,2048]{1,0:T(8,128)S(1)} %collective-permute-done.33.refs_2_), channel_id=1, source_target_pairs={{1,0},{2,1},{5,4},{6,5},{9,8},{10,9},{13,12},{14,13},{17,16},{18,1... | collective-permute-start | bytes 983048 | tf_op jit(solution)/shard_map/ppermute | solution.py:256
  22.1 14.0 %collective-permute-start.18 = (f32[40,2048]{1,0:T(8,128)S(1)}, f32[40,2048]{1,0:T(8,128)S(1)}, u32[]{:S(2)}, u32[]{:S(2)}) collective-permute-start(f32[40,2048]{1,0:T(8,128)S(1)} %collective-permute-done.16.refs_1_), channel_id=1, source_target_pairs={{1,2},{2,3},{5,6},{6,7},{9,10},{10,11},{13,14},{14,15},{17,18},{18... | collective-permute-start | bytes 983048 | tf_op jit(solution)/shard_map/ppermute | solution.py:255
  27.7 14.0 %collective-permute-start.19 = (f32[40,2048]{1,0:T(8,128)S(1)}, f32[40,2048]{1,0:T(8,128)S(1)}, u32[]{:S(2)}, u32[]{:S(2)}) collective-permute-start(f32[40,2048]{1,0:T(8,128)S(1)} %collective-permute-done.17.refs_2_), channel_id=1, source_target_pairs={{1,0},{2,1},{5,4},{6,5},{9,8},{10,9},{13,12},{14,13},{17,16},{18,1... | collective-permute-start | bytes 983048 | tf_op jit(solution)/shard_map/ppermute | solution.py:256
  34.8 14.0 %collective-permute-start.36 = (f32[40,2048]{1,0:T(8,128)S(1)}, f32[40,2048]{1,0:T(8,128)S(1)}, u32[]{:S(2)}, u32[]{:S(2)}) collective-permute-start(f32[40,2048]{1,0:T(8,128)S(1)} %add.295.refs_3_), channel_id=1, source_target_pairs={{2,3},{1,0},{6,7},{5,4},{10,11},{9,8},{14,15},{13,12},{18,19},{17,... | collective-permute-start | bytes 983048 | tf_op jit(solution)/shard_map/ppermute | solution.py:253
  41.8 13.1 %collective-permute-start.20 = (f32[40,2048]{1,0:T(8,128)S(1)}, f32[40,2048]{1,0:T(8,128)S(1)}, u32[]{:S(2)}, u32[]{:S(2)}) collective-permute-start(f32[40,2048]{1,0:T(8,128)S(1)} %add.279.refs_3_), channel_id=1, source_target_pairs={{2,3},{1,0},{6,7},{5,4},{10,11},{9,8},{14,15},{13,12},{18,19},{17,... | collective-permute-start | bytes 983048 | tf_op jit(solution)/shard_map/ppermute | solution.py:253
  48.7 6.1 %copy-start = (f32[2048,1024]{1,0:T(8,128)S(1)}, f32[2048,1024]{1,0:T(8,128)}, u32[]{:S(2)}) copy-start(f32[2048,1024]{1,0:T(8,128)} %high_ref.3) | copy-start | bytes 25165828
  54.8 3.7 %collective-permute-start.37 = (f32[64,1024]{1,0:T(8,128)S(1)}, f32[64,1024]{1,0:T(8,128)S(1)}, u32[]{:S(2)}, u32[]{:S(2)}) collective-permute-start(f32[64,1024]{1,0:T(8,128)S(1)} %constant_dynamic-slice_fusion.1), channel_id=1, source_target_pairs={{0,4},{4,0},{8,12},{12,8},{16,20},{20,16},{24,28},{28,24},{1,5},{5... | collective-permute-start | bytes 786440 | tf_op jit(solution)/shard_map/ppermute | solution.py:299
  57.9 3.7 %collective-permute-start.21 = (f32[64,1024]{1,0:T(8,128)S(1)}, f32[64,1024]{1,0:T(8,128)S(1)}, u32[]{:S(2)}, u32[]{:S(2)}) collective-permute-start(f32[64,1024]{1,0:T(8,128)S(1)} %constant_dynamic-slice_fusion.2), channel_id=1, source_target_pairs={{0,4},{4,0},{8,12},{12,8},{16,20},{20,16},{24,28},{28,24},{1,5},{5... | collective-permute-start | bytes 786440 | tf_op jit(solution)/shard_map/ppermute | solution.py:299
  58.5 5.7 %collective-permute-start.38 = (f32[32,1024]{1,0:T(8,128)S(1)}, f32[32,1024]{1,0:T(8,128)S(1)}, u32[]{:S(2)}, u32[]{:S(2)}) collective-permute-start(f32[32,1024]{1,0:T(8,128)S(1)} %get-tuple-element.81), channel_id=1, source_target_pairs={{0,8},{4,12},{8,0},{12,4},{16,24},{20,28},{24,16},{28,20},{1,9},{5... | collective-permute-start | bytes 393224 | tf_op jit(solution)/shard_map/ppermute | solution.py:306
  60.1 6.3 %collective-permute-start.39 = (f32[32,1024]{1,0:T(8,128)S(1)}, f32[32,1024]{1,0:T(8,128)S(1)}, u32[]{:S(2)}, u32[]{:S(2)}) collective-permute-start(f32[32,1024]{1,0:T(8,128)S(1)} %get-tuple-element.80), channel_id=1, source_target_pairs={{0,16},{4,20},{8,24},{12,28},{16,0},{20,4},{24,8},{28,12},{1,17},{... | collective-permute-start | bytes 393224 | tf_op jit(solution)/shard_map/ppermute | solution.py:306
  61.7 7.0 %collective-permute-start.22 = (f32[32,1024]{1,0:T(8,128)S(1)}, f32[32,1024]{1,0:T(8,128)S(1)}, u32[]{:S(2)}, u32[]{:S(2)}) collective-permute-start(f32[32,1024]{1,0:T(8,128)S(1)} %get-tuple-element.85), channel_id=1, source_target_pairs={{0,8},{4,12},{8,0},{12,4},{16,24},{20,28},{24,16},{28,20},{1,9},{5... | collective-permute-start | bytes 393224 | tf_op jit(solution)/shard_map/ppermute | solution.py:306
  62.3 6.6 %collective-permute-start.23 = (f32[32,1024]{1,0:T(8,128)S(1)}, f32[32,1024]{1,0:T(8,128)S(1)}, u32[]{:S(2)}, u32[]{:S(2)}) collective-permute-start(f32[32,1024]{1,0:T(8,128)S(1)} %get-tuple-element.84), channel_id=1, source_target_pairs={{0,16},{4,20},{8,24},{12,28},{16,0},{20,4},{24,8},{28,12},{1,17},{... | collective-permute-start | bytes 393224 | tf_op jit(solution)/shard_map/ppermute | solution.py:306
  66.4 6.0 %collective-permute-start.41 = (f32[32,1024]{1,0:T(8,128)S(1)}, f32[32,1024]{1,0:T(8,128)S(1)}, u32[]{:S(2)}, u32[]{:S(2)}) collective-permute-start(f32[32,1024]{1,0:T(8,128)S(1)} %get-tuple-element.51), channel_id=1, source_target_pairs={{0,8},{4,12},{8,0},{12,4},{16,24},{20,28},{24,16},{28,20},{1,9},{5... | collective-permute-start | bytes 393224 | tf_op jit(solution)/shard_map/ppermute | solution.py:306
  66.5 6.2 %collective-permute-start.40 = (f32[32,1024]{1,0:T(8,128)S(1)}, f32[32,1024]{1,0:T(8,128)S(1)}, u32[]{:S(2)}, u32[]{:S(2)}) collective-permute-start(f32[32,1024]{1,0:T(8,128)S(1)} %get-tuple-element.50), channel_id=1, source_target_pairs={{0,16},{4,20},{8,24},{12,28},{16,0},{20,4},{24,8},{28,12},{1,17},{... | collective-permute-start | bytes 393224 | tf_op jit(solution)/shard_map/ppermute | solution.py:306
  68.9 5.0 %collective-permute-start.25 = (f32[32,1024]{1,0:T(8,128)S(1)}, f32[32,1024]{1,0:T(8,128)S(1)}, u32[]{:S(2)}, u32[]{:S(2)}) collective-permute-start(f32[32,1024]{1,0:T(8,128)S(1)} %get-tuple-element.47), channel_id=1, source_target_pairs={{0,8},{4,12},{8,0},{12,4},{16,24},{20,28},{24,16},{28,20},{1,9},{5... | collective-permute-start | bytes 393224 | tf_op jit(solution)/shard_map/ppermute | solution.py:306
  70.2 5.0 %collective-permute-start.24 = (f32[32,1024]{1,0:T(8,128)S(1)}, f32[32,1024]{1,0:T(8,128)S(1)}, u32[]{:S(2)}, u32[]{:S(2)}) collective-permute-start(f32[32,1024]{1,0:T(8,128)S(1)} %get-tuple-element.46), channel_id=1, source_target_pairs={{0,16},{4,20},{8,24},{12,28},{16,0},{20,4},{24,8},{28,12},{1,17},{... | collective-permute-start | bytes 393224 | tf_op jit(solution)/shard_map/ppermute | solution.py:306
  72.8 2.7 %copy-start.2 = (f32[2048,128]{1,0:T(8,128)S(1)}, f32[2048,128]{1,0:T(8,128)}, u32[]{:S(2)}) copy-start(f32[2048,128]{1,0:T(8,128)} %vectors_ref.5) | copy-start | bytes 3145732
  72.8 2.7 %copy-start.5 = (f32[1024]{0:T(1024)S(1)}, f32[1024]{0:T(1024)}, u32[]{:S(2)}) copy-start(f32[1024]{0:T(1024)} %param.10) | copy-start | bytes 12292
  72.8 2.5 %collective-permute-start.42 = (f32[64,1024]{1,0:T(8,128)S(1)}, f32[64,1024]{1,0:T(8,128)S(1)}, u32[]{:S(2)}, u32[]{:S(2)}) collective-permute-start(f32[64,1024]{1,0:T(8,128)S(1)} %constant_dynamic-update-slice_fusion.4), channel_id=1, source_target_pairs={{0,4},{4,0},{8,12},{12,8},{16,20},{20,16},{24,28},{28,24},{1,5},{5... | collective-permute-start | bytes 786440 | tf_op jit(solution)/shard_map/ppermute | solution.py:311
  75.3 9.7 %collective-permute-start.26 = (f32[64,1024]{1,0:T(8,128)S(1)}, f32[64,1024]{1,0:T(8,128)S(1)}, u32[]{:S(2)}, u32[]{:S(2)}) collective-permute-start(f32[64,1024]{1,0:T(8,128)S(1)} %constant_dynamic-update-slice_fusion.2), channel_id=1, source_target_pairs={{0,4},{4,0},{8,12},{12,8},{16,20},{20,16},{24,28},{28,24},{1,5},{5... | collective-permute-start | bytes 786440 | tf_op jit(solution)/shard_map/ppermute | solution.py:311
  75.4 9.7 %slice-start = ((s8[8388608]{0:T(1024)(128)(4,1)}), s8[4194304]{0:T(1024)(128)(4,1)S(1)}, s32[]{:S(2)}) async-start(s8[8388608]{0:T(1024)(128)(4,1)} %bitcast.76), calls=%async_computation | async-start | bytes 8388608
  75.5 9.6 %slice-start.1 = ((s8[8388608]{0:T(1024)(128)(4,1)}), s8[4194304]{0:T(1024)(128)(4,1)S(1)}, s32[]{:S(2)}) async-start(s8[8388608]{0:T(1024)(128)(4,1)} %bitcast.76), calls=%async_computation.1 | async-start | bytes 8388608
  82.0 9.7 %collective-permute-start.45 = (f32[32,2048]{1,0:T(8,128)S(1)}, f32[32,2048]{1,0:T(8,128)S(1)}, u32[]{:S(2)}, u32[]{:S(2)}) collective-permute-start(f32[32,2048]{1,0:T(8,128)S(1)} %get-tuple-element.65), channel_id=1, source_target_pairs={{0,1},{3,2},{4,5},{7,6},{8,9},{11,10},{12,13},{15,14},{16,17},{19,... | collective-permute-start | bytes 786440 | tf_op jit(solution)/shard_map/ppermute | solution.py:283
  83.5 12.2 %collective-permute-start.43 = (f32[32,2048]{1,0:T(8,128)S(1)}, f32[32,2048]{1,0:T(8,128)S(1)}, u32[]{:S(2)}, u32[]{:S(2)}) collective-permute-start(f32[32,2048]{1,0:T(8,128)S(1)} %get-tuple-element.66), channel_id=1, source_target_pairs={{0,1},{3,2},{4,5},{7,6},{8,9},{11,10},{12,13},{15,14},{16,17},{19,... | collective-permute-start | bytes 786440 | tf_op jit(solution)/shard_map/ppermute | solution.py:283
  89.1 12.2 %collective-permute-start.29 = (f32[32,2048]{1,0:T(8,128)S(1)}, f32[32,2048]{1,0:T(8,128)S(1)}, u32[]{:S(2)}, u32[]{:S(2)}) collective-permute-start(f32[32,2048]{1,0:T(8,128)S(1)} %get-tuple-element.69), channel_id=1, source_target_pairs={{0,1},{3,2},{4,5},{7,6},{8,9},{11,10},{12,13},{15,14},{16,17},{19,... | collective-permute-start | bytes 786440 | tf_op jit(solution)/shard_map/ppermute | solution.py:283
  90.4 16.5 %collective-permute-start.27 = (f32[32,2048]{1,0:T(8,128)S(1)}, f32[32,2048]{1,0:T(8,128)S(1)}, u32[]{:S(2)}, u32[]{:S(2)}) collective-permute-start(f32[32,2048]{1,0:T(8,128)S(1)} %get-tuple-element.70), channel_id=1, source_target_pairs={{0,1},{3,2},{4,5},{7,6},{8,9},{11,10},{12,13},{15,14},{16,17},{19,... | collective-permute-start | bytes 786440 | tf_op jit(solution)/shard_map/ppermute | solution.py:283
  91.7 20.8 %collective-permute-start.47 = (f32[32,2048]{1,0:T(8,128)S(1)}, f32[32,2048]{1,0:T(8,128)S(1)}, u32[]{:S(2)}, u32[]{:S(2)}) collective-permute-start(f32[32,2048]{1,0:T(8,128)S(1)} %get-tuple-element.64), channel_id=1, source_target_pairs={{0,1},{1,0},{2,3},{3,2},{4,5},{5,4},{6,7},{7,6},{8,9},{9,8},{10,11... | collective-permute-start | bytes 786440 | tf_op jit(solution)/shard_map/ppermute | solution.py:287
  91.8 26.2 %collective-permute-start.31 = (f32[32,2048]{1,0:T(8,128)}, f32[32,2048]{1,0:T(8,128)S(1)}, u32[]{:S(2)}, u32[]{:S(2)}) collective-permute-start(f32[32,2048]{1,0:T(8,128)} %get-tuple-element.68), channel_id=1, source_target_pairs={{0,1},{1,0},{2,3},{3,2},{4,5},{5,4},{6,7},{7,6},{8,9},{9,8},{10,11... | collective-permute-start | bytes 786440 | tf_op jit(solution)/shard_map/ppermute | solution.py:287
  95.7 22.3 %collective-permute-start.46 = (f32[32,2048]{1,0:T(8,128)}, f32[32,2048]{1,0:T(8,128)S(1)}, u32[]{:S(2)}, u32[]{:S(2)}) collective-permute-start(f32[32,2048]{1,0:T(8,128)} %add.302), channel_id=1, source_target_pairs={{1,2},{2,1},{5,6},{6,5},{9,10},{10,9},{13,14},{14,13},{17,18},{18,... | collective-permute-start | bytes 786440 | tf_op jit(solution)/shard_map/ppermute | solution.py:284
  97.1 28.5 %copy-start.1 = (f32[512]{0:T(512)S(1)}, f32[512]{0:T(512)}, u32[]{:S(2)}) copy-start(f32[512]{0:T(512)} %param.13) | copy-start | bytes 6148
  97.1 28.5 %copy-start.4 = (s32[256]{0:T(256)S(1)}, s32[256]{0:T(256)}, u32[]{:S(2)}) copy-start(s32[256]{0:T(256)} %param.14) | copy-start | bytes 3076
  97.1 28.5 %copy-start.6 = (s32[256]{0:T(256)S(1)}, s32[256]{0:T(256)}, u32[]{:S(2)}) copy-start(s32[256]{0:T(256)} %param.15) | copy-start | bytes 3076
  101.3 16.7 %collective-permute-start.44 = (f32[32,2048]{1,0:T(8,128)}, f32[32,2048]{1,0:T(8,128)S(1)}, u32[]{:S(2)}, u32[]{:S(2)}) collective-permute-start(f32[32,2048]{1,0:T(8,128)} %add.301), channel_id=1, source_target_pairs={{1,3},{2,0},{5,7},{6,4},{9,11},{10,8},{13,15},{14,12},{17,19},{18,... | collective-permute-start | bytes 786440 | tf_op jit(solution)/shard_map/ppermute | solution.py:284
  106.9 11.1 %collective-permute-start.30 = (f32[32,2048]{1,0:T(8,128)}, f32[32,2048]{1,0:T(8,128)S(1)}, u32[]{:S(2)}, u32[]{:S(2)}) collective-permute-start(f32[32,2048]{1,0:T(8,128)} %add.289), channel_id=1, source_target_pairs={{1,2},{2,1},{5,6},{6,5},{9,10},{10,9},{13,14},{14,13},{17,18},{18,... | collective-permute-start | bytes 786440 | tf_op jit(solution)/shard_map/ppermute | solution.py:284
  112.5 11.8 %collective-permute-start.28 = (f32[32,2048]{1,0:T(8,128)}, f32[32,2048]{1,0:T(8,128)S(1)}, u32[]{:S(2)}, u32[]{:S(2)}) collective-permute-start(f32[32,2048]{1,0:T(8,128)} %add.288), channel_id=1, source_target_pairs={{1,3},{2,0},{5,7},{6,4},{9,11},{10,8},{13,15},{14,12},{17,19},{18,... | collective-permute-start | bytes 786440 | tf_op jit(solution)/shard_map/ppermute | solution.py:284

commit v2 on v1

--- a/solution.py
+++ b/solution.py
@@ -127,33 +127,44 @@
     )(me[None], cluster[None, :], gap[None, :], pool_values[None, :], pool_vectors, pool_images)
 
 
-def product_kernel(width, n, source_ref, info_ref, *refs):
-    *buffers, high_ref, out_ref = refs
+def pieces_of(x_ref, step):
+    rows = x_ref.shape[0]
+    step = min(rows, step)
+    for start in range(0, rows, step):
+        span = slice(start, start + step)
+        yield span, split(x_ref[span], 2)
+
+
+def product_kernel(width, n, scalar_ref, info_ref, *refs):
+    *buffers, x_ref, keep_ref, give_ref = refs
     room = buffers[0].shape[0]
     slots = room * len(buffers)
     rows = info_ref.shape[0]
+    half = rows // 2
+    mine = pl.multiple_of(scalar_ref[len(buffers)] * half, half)
+    info = jnp.concatenate(
+        [info_ref[pl.ds(mine, half), :], info_ref[pl.ds(half - mine, half), :]], 0
+    )
     lane = lax.broadcasted_iota(jnp.int32, (rows, slots), 1)
     owner = jnp.full((rows, slots), -1, jnp.int32)
     for b in range(len(buffers)):
         inside = jnp.logical_and(lane >= b * room, lane < (b + 1) * room)
-        owner = jnp.where(inside, source_ref[b], owner)
+        owner = jnp.where(inside, scalar_ref[b], owner)
     slot = lane.astype(F32)
     slot = slot - room * steps(slot, room, len(buffers))
     place = jnp.logical_and(
-        steps(info_ref[:, 0:1], width, n) == owner.astype(F32), info_ref[:, 1:2] == slot
+        steps(info[:, 0:1], width, n) == owner.astype(F32), info[:, 1:2] == slot
     )
     place = jnp.where(place, 1.0, 0.0).astype(BF16)
-    depth = high_ref.shape[0]
-    piece = min(depth, 512)
     terms = []
-    for start in range(0, depth, piece):
-        span = slice(start, start + piece)
+    for span, (x_high, x_low) in pieces_of(x_ref, 512):
         gathered = jnp.concatenate([b[:, span] for b in buffers], 0)
         high, low = (dot(place, p, ((1,), (0,))).astype(BF16) for p in split(gathered, 2))
-        x_high, x_low = split(high_ref[span], 2)
         left = jnp.concatenate([high, low, high], 1)
         terms.append(dot(left, jnp.concatenate([x_high, x_high, x_low], 0), ((1,), (0,))))
-    out_ref[...] = total(terms)
+    out = total(terms)
+    keep_ref[...] = out[:half]
+    give_ref[...] = out[half:]
 
 
 def cost(count, high_vectors):
@@ -163,49 +174,67 @@
     )
 
 
-def product(width, info, buffers, high_vectors):
+def product(width, pair, info, buffers, high_vectors):
     n = lax.axis_size("col")
     count = info.shape[0]
-    sources = jnp.stack([jnp.asarray(src, jnp.int32) for _, src in buffers])
+    scalars = jnp.stack([jnp.asarray(src, jnp.int32) for _, src in buffers] + [pair])
     return pl.pallas_call(
         functools.partial(product_kernel, width, n),
-        out_shape=jax.ShapeDtypeStruct((count, high_vectors.shape[1]), F32),
+        out_shape=[jax.ShapeDtypeStruct((count // 2, high_vectors.shape[1]), F32)] * 2,
         in_specs=[SMEM] + [VMEM] * (len(buffers) + 2),
-        out_specs=VMEM,
-        compiler_params=pltpu.CompilerParams(vmem_limit_bytes=40 << 20),
+        out_specs=[VMEM, VMEM],
+        compiler_params=pltpu.CompilerParams(vmem_limit_bytes=24 << 20),
         cost_estimate=cost(count, high_vectors),
-    )(sources, info, *[b for b, _ in buffers], high_vectors)
-
-
-def image_kernel(me_ref, info_ref, sums_ref, mu_ref, vectors_ref, high_ref, out_ref):
+    )(scalars, info, *[b for b, _ in buffers], high_vectors)
+
+
+def image_kernel(pieces, scalar_ref, info_ref, mu_ref, vectors_ref, x_ref, *refs):
+    sums, outs = refs[: 2 * pieces], refs[2 * pieces :]
+    *outs, sums_ref = outs
     count = info_ref.shape[0]
-    gaps = info_ref[:, 3:4] * (mu_ref[...] - info_ref[:, 2:3])
-    d_high, d_low = split(sums_ref[...] / gaps, 2)
+    block = outs[0].shape[0]
+    first = scalar_ref[len(outs) + 1] == 0
+    mine = jnp.concatenate([r[...] for r in sums[:pieces]], 0)
+    pair = jnp.concatenate([r[...] for r in sums[pieces:]], 0)
+    sums_ref[: count // 2] = jnp.where(first, mine, pair)
+    sums_ref[count // 2 :] = jnp.where(first, pair, mine)
+
+    def ordered(ref):
+        spans = [
+            pl.ds(pl.multiple_of(scalar_ref[k] * block, block), block) for k in range(len(outs))
+        ]
+        return jnp.concatenate([ref[span, :] for span in spans], 0)
+
+    info = ordered(info_ref)
+    gaps = info[:, 3:4] * (mu_ref[...] - info[:, 2:3])
+    d_high, d_low = split(ordered(sums_ref) / gaps, 2)
     both = jnp.concatenate([d_high, d_low], 0)
     width = vectors_ref.shape[1]
-    spot = lax.broadcasted_iota(jnp.int32, (count, width), 1) + me_ref[0] * width
-    mine = jnp.where(spot.astype(F32) == info_ref[:, 0:1], 1.0, 0.0).astype(BF16)
-    depth = high_ref.shape[0]
-    piece = min(depth, 256)
-    for start in range(0, depth, piece):
-        span = slice(start, start + piece)
+    spot = lax.broadcasted_iota(jnp.int32, (count, width), 1) + scalar_ref[len(outs)] * width
+    mine = jnp.where(spot.astype(F32) == info[:, 0:1], 1.0, 0.0).astype(BF16)
+    for span, (x_high, x_low) in pieces_of(x_ref, 256):
         chosen = total([dot(mine, p, ((1,), (1,))) for p in split(vectors_ref[span], 3)])
-        x_high, x_low = split(high_ref[span], 2)
         image = dot(both, x_high, ((1,), (1,)))
         image = image[:count] + image[count:] + dot(d_high, x_low, ((1,), (1,)))
-        out_ref[:, span] = chosen - image
-
-
-def image(me, info, sums, high_values, pool_vectors, high_vectors):
+        for k, out in enumerate(outs):
+            rows = slice(k * block, (k + 1) * block)
+            out[:, span] = chosen[rows] - image[rows]
+
+
+def image(order, me, pair, info, sums, high_values, pool_vectors, high_vectors):
     count = info.shape[0]
+    block = count // len(order)
+    depth, k = high_vectors.shape
+    scalars = jnp.stack([jnp.asarray(i, jnp.int32) for i in [*order, me, pair]])
     return pl.pallas_call(
-        image_kernel,
-        out_shape=jax.ShapeDtypeStruct((count, high_vectors.shape[0]), F32),
-        in_specs=[SMEM] + [VMEM] * 5,
-        out_specs=VMEM,
-        compiler_params=pltpu.CompilerParams(vmem_limit_bytes=40 << 20),
+        functools.partial(image_kernel, len(sums) // 2),
+        out_shape=[jax.ShapeDtypeStruct((block, depth), F32)] * len(order),
+        in_specs=[SMEM] + [VMEM] * (len(sums) + 4),
+        out_specs=[VMEM] * len(order),
+        scratch_shapes=[pltpu.VMEM((count, k), F32)],
+        compiler_params=pltpu.CompilerParams(vmem_limit_bytes=24 << 20),
         cost_estimate=cost(count, high_vectors),
-    )(me[None], info, sums, high_values[None, :], pool_vectors, high_vectors)
+    )(scalars, info, high_values[None, :], pool_vectors, high_vectors, *sums)
 
 
 def finish_kernel(parts, me_ref, info_ref, *refs):
@@ -264,38 +293,35 @@
     return [(rows, jnp.where(src < n, src, -1)) for rows, src in buffers]
 
 
-def scatter_line(blocks, axis):
+def scatter_order(axis):
     n = lax.axis_size(axis)
     me = lax.axis_index(axis)
     half = n // 2
     place = me % half
-    base = me - place
-    left = me < half
-
-    def block(k):
-        return lax.dynamic_index_in_dim(blocks, k, 0, keepdims=False)
-
-    terms = [block(me)]
+    near = [me - place + (place + step) % half for step in range(half)]
+    return near + [jnp.where(me < half, k, n - 1 - k) for k in range(n - 1, half - 1, -1)]
+
+
+def scatter_line(blocks, axis):
+    n = lax.axis_size(axis)
+    half = n // 2
+    terms = [blocks[0]]
     for target in range(n - 1, half - 1, -1):
-        part = block(jnp.where(left, target, n - 1 - target))
-        rows = part
+        part = rows = blocks[half + n - 1 - target]
         for hop in range(half - 1):
-            rows = part + lax.ppermute(rows, axis, mirrored(n, [(hop, hop + 1)]))
+            came = lax.ppermute(rows, axis, mirrored(n, [(hop, hop + 1)]))
+            rows = part + came
         terms.append(lax.ppermute(rows, axis, mirrored(n, [(half - 1, target)])))
     for step in range(1, half):
         turn = [(g + i, g + (i + step) % half) for g in (0, half) for i in range(half)]
-        terms.append(lax.ppermute(block(base + (place + step) % half), axis, turn))
+        terms.append(lax.ppermute(blocks[step], axis, turn))
     return terms
 
 
-def sum_pairs(x, axis):
+def sum_pairs(keep, give, axis):
     n = lax.axis_size(axis)
-    me = lax.axis_index(axis)
-    half = x.shape[0] // 2
-    mine = (me % 2) * half
     pairs = [(i, i ^ 1) for i in range(n)]
-    keep = lax.dynamic_slice_in_dim(x, mine, half, 0)
-    give = lax.dynamic_slice_in_dim(x, half - mine, half, 0)
+    half = keep.shape[0]
     part = keep + lax.ppermute(give, axis, pairs)
     bits = [1 << b for b in range(1, n.bit_length() - 1)]
     cut = -(-half // (8 * len(bits))) * 8
@@ -307,34 +333,30 @@
                 pieces[i], axis, [(d, d ^ bit) for d in range(n)]
             )
         pieces = list(lax.optimization_barrier(tuple(pieces)))
-    part = jnp.concatenate(pieces, 0)
-    other = lax.ppermute(part, axis, pairs)
-    first = me % 2 == 0
-    return jnp.concatenate(
-        [jnp.where(first, part, other), jnp.where(first, other, part)], 0
-    )
+    return pieces, [lax.ppermute(p, axis, pairs) for p in pieces]
 
 
 def correct_parts(room, high_vectors, high_values, pool_vectors, pool_images, pool_values, cluster, gap):
-    n = lax.axis_size("col")
     me = lax.axis_index("col")
+    pair = lax.axis_index("row") % 2
     count = cluster.shape[0]
     width = pool_vectors.shape[1]
     info, own = plan(room, me, cluster, gap, pool_values, pool_vectors, pool_images)
-    gathered = [gather_line(own[p], "col") for p in range(PARTS)]
-    sums = [
-        sum_pairs(product(width, info[p], gathered[p], high_vectors), "row") for p in range(PARTS)
-    ]
+    order = scatter_order("col")
     terms = []
     for p in range(PARTS):
-        partial = image(me, info[p], sums[p], high_values, pool_vectors, high_vectors)
-        terms += scatter_line(partial.reshape(n, count // (n * PARTS), -1), "col")
+        gathered = gather_line(own[p], "col")
+        keep, give = product(width, pair, info[p], gathered, high_vectors)
+        mine, other = sum_pairs(keep, give, "row")
+        blocks = image(order, me, pair, info[p], mine + other, high_values, pool_vectors, high_vectors)
+        terms += scatter_line(blocks, "col")
     return finish(me, info.reshape(count, -1), terms).T, jnp.max(info[:, :, 1]) + 1.0
 
 
 def correct_whole(high_vectors, high_values, pool_vectors, pool_images, pool_values, cluster, gap):
     n = lax.axis_size("col")
     me = lax.axis_index("col")
+    pair = lax.axis_index("row") % 2
     count = cluster.shape[0]
     width = pool_vectors.shape[1]
     low_vals = jnp.take(pool_values, cluster, axis=0)
@@ -346,12 +368,19 @@
         here = jnp.logical_and(cluster[:, None] == spot[None, :], source >= 0).astype(F32)
         rows = dot(here, rows, ((1,), (0,)), EXACT)
         sums = sums + dot(rows, high_vectors, ((1,), (0,)), HIGH)
-    sums = sum_pairs(sums, "row")
+    half = count // 2
+    keep = lax.dynamic_slice_in_dim(sums, pair * half, half, 0)
+    give = lax.dynamic_slice_in_dim(sums, half - pair * half, half, 0)
+    mine, other = (jnp.concatenate(p, 0) for p in sum_pairs(keep, give, "row"))
+    first = pair == 0
+    sums = jnp.concatenate([jnp.where(first, mine, other), jnp.where(first, other, mine)], 0)
     coeffs = sums / (gap.astype(F32)[:, None] * (high_values[None, :] - low_vals[:, None]))
     mine = (cluster[:, None] == me * width + jnp.arange(width)[None, :]).astype(F32)
     partial = dot(mine, pool_vectors, ((1,), (1,)), EXACT)
     partial = partial - dot(coeffs, high_vectors, ((1,), (1,)), HIGH)
-    return total(scatter_line(partial.reshape(n, count // n, -1), "col")).T
+    blocks = partial.reshape(n, count // n, -1)
+    blocks = [lax.dynamic_index_in_dim(blocks, k, 0, keepdims=False) for k in scatter_order("col")]
+    return total(scatter_line(blocks, "col")).T
 
 
 def body(*args):

time: 127 us -> 123 us (0.969)
  the two profiles are of different devices: /device:TPU:0 before, /device:TPU:8 now
where the time goes in v2:
time: 123 us
  starting transfers between devices  54.9 us (45%)
  waiting for transfers between devices  37.6 us (31%)
  Pallas kernels  25.9 us (21%)
  other arithmetic  2.57 us (2%)
    ppermute x4, starting transfers between devices, gather_line(): came_left = lax.ppermute(from_left, axis, right)  14.8 us
    pallas_call x2, Pallas kernels, image(): pl.pallas_call(functools.partial(image_kernel, len(sums) // 2), out_shape...  12.6 us
    ppermute x4, starting transfers between devices, gather_line(): came_right = lax.ppermute(from_right, axis, left)  9.5 us
    ppermute x4, waiting for transfers between devices, scatter_line(): came = lax.ppermute(rows, axis, mirrored(n, [(hop, hop + 1)]))  9.24 us
    pallas_call x2, Pallas kernels, product(): pl.pallas_call(functools.partial(product_kernel, width, n), out_shape=[ja...  8.98 us
    ppermute x8, starting transfers between devices, sum_pairs(): lax.ppermute(pieces[i], axis, [(d, d ^ bit) for d in range(n)])  7.98 us
    ppermute x8, waiting for transfers between devices, sum_pairs(): lax.ppermute(pieces[i], axis, [(d, d ^ bit) for d in range(n)])  7.83 us
    ppermute x4, waiting for transfers between devices, gather_line(): came_right = lax.ppermute(from_right, axis, left)  7.6 us
  transfers between devices with their start and end apart: 34, of which 19 were waited for; matrix products, arithmetic and copies ran while one was open for 2% of the time, Pallas kernels for 18%

profile of v2, /device:TPU:8, one launch (start us, length us, event | category | flops | bytes accessed | tf_op | source)
XLA Modules:
  0.0 122.8 jit_solution(1622977610050228309)
XLA Ops:
  0.0 3.1 %shard_map.75 = (f32[2,128,128]{2,1,0:T(8,128)S(1)}, f32[2,40,2048]{2,1,0:T(8,128)S(1)}) custom-call(s32[1]{0:T(128)} %bitcast.7.me_ref, s32[1,256]{1,0:T(1,128)} %bitcast.67, s32[1,256]{1,0:T(1,128)} %bitcast.70, f32[1,512]{1,0:T(1,128)} %bitcast.63, f32[2048,128]{1,0:T(8,128)} %vectors_ref.5, f32[2048,128]{1,0:T(8,128)} %images_ref.1), custom_call_target="tpu_custom_call" | custom-call | tf_op jit(solution)/shard_map/pallas_call | solution.py:118
  3.2 3.5 %collective-permute-start.17 = (f32[40,2048]{1,0:T(8,128)S(1)}, f32[40,2048]{1,0:T(8,128)S(1)}, u32[]{:S(2)}, u32[]{:S(2)}) collective-permute-start(f32[40,2048]{1,0:T(8,128)S(1)} %get-tuple-element.89.refs_0_), channel_id=1, source_target_pairs={{0,1},{1,2},{2,3},{4,5},{5,6},{6,7},{8,9},{9,10},{10,11},{12,13},{... | collective-permute-start | bytes 983048 | tf_op jit(solution)/shard_map/ppermute | solution.py:284
  6.7 2.4 %collective-permute-start.18 = (f32[40,2048]{1,0:T(8,128)S(1)}, f32[40,2048]{1,0:T(8,128)S(1)}, u32[]{:S(2)}, u32[]{:S(2)}) collective-permute-start(f32[40,2048]{1,0:T(8,128)S(1)} %get-tuple-element.89.refs_0_), channel_id=1, source_target_pairs={{1,0},{2,1},{3,2},{5,4},{6,5},{7,6},{9,8},{10,9},{11,10},{13,12},{... | collective-permute-start | bytes 983048 | tf_op jit(solution)/shard_map/ppermute | solution.py:285
  9.0 3.5 %collective-permute-start.34 = (f32[40,2048]{1,0:T(8,128)S(1)}, f32[40,2048]{1,0:T(8,128)S(1)}, u32[]{:S(2)}, u32[]{:S(2)}) collective-permute-start(f32[40,2048]{1,0:T(8,128)S(1)} %get-tuple-element.88.refs_0_), channel_id=1, source_target_pairs={{0,1},{1,2},{2,3},{4,5},{5,6},{6,7},{8,9},{9,10},{10,11},{12,13},{... | collective-permute-start | bytes 983048 | tf_op jit(solution)/shard_map/ppermute | solution.py:284
  12.5 2.4 %collective-permute-start.35 = (f32[40,2048]{1,0:T(8,128)S(1)}, f32[40,2048]{1,0:T(8,128)S(1)}, u32[]{:S(2)}, u32[]{:S(2)}) collective-permute-start(f32[40,2048]{1,0:T(8,128)S(1)} %get-tuple-element.88.refs_0_), channel_id=1, source_target_pairs={{1,0},{2,1},{3,2},{5,4},{6,5},{7,6},{9,8},{10,9},{11,10},{13,12},{... | collective-permute-start | bytes 983048 | tf_op jit(solution)/shard_map/ppermute | solution.py:285
  14.9 0.7 collective-permute-done.17.refs_1_
  15.7 3.5 %collective-permute-start.19 = (f32[40,2048]{1,0:T(8,128)S(1)}, f32[40,2048]{1,0:T(8,128)S(1)}, u32[]{:S(2)}, u32[]{:S(2)}) collective-permute-start(f32[40,2048]{1,0:T(8,128)S(1)} %collective-permute-done.17.refs_1_), channel_id=1, source_target_pairs={{1,2},{2,3},{5,6},{6,7},{9,10},{10,11},{13,14},{14,15},{17,18},{18... | collective-permute-start | bytes 983048 | tf_op jit(solution)/shard_map/ppermute | solution.py:284
  19.2 2.4 %collective-permute-start.20 = (f32[40,2048]{1,0:T(8,128)S(1)}, f32[40,2048]{1,0:T(8,128)S(1)}, u32[]{:S(2)}, u32[]{:S(2)}) collective-permute-start(f32[40,2048]{1,0:T(8,128)S(1)} %collective-permute-done.18.refs_2_), channel_id=1, source_target_pairs={{1,0},{2,1},{5,4},{6,5},{9,8},{10,9},{13,12},{14,13},{17,16},{18,1... | collective-permute-start | bytes 983048 | tf_op jit(solution)/shard_map/ppermute | solution.py:285
  21.6 0.2 collective-permute-done.34.refs_1_
  21.8 4.4 %collective-permute-start.36 = (f32[40,2048]{1,0:T(8,128)S(1)}, f32[40,2048]{1,0:T(8,128)S(1)}, u32[]{:S(2)}, u32[]{:S(2)}) collective-permute-start(f32[40,2048]{1,0:T(8,128)S(1)} %collective-permute-done.34.refs_1_), channel_id=1, source_target_pairs={{1,2},{2,3},{5,6},{6,7},{9,10},{10,11},{13,14},{14,15},{17,18},{18... | collective-permute-start | bytes 983048 | tf_op jit(solution)/shard_map/ppermute | solution.py:284
  26.2 2.4 %collective-permute-start.37 = (f32[40,2048]{1,0:T(8,128)S(1)}, f32[40,2048]{1,0:T(8,128)S(1)}, u32[]{:S(2)}, u32[]{:S(2)}) collective-permute-start(f32[40,2048]{1,0:T(8,128)S(1)} %collective-permute-done.35.refs_2_), channel_id=1, source_target_pairs={{1,0},{2,1},{5,4},{6,5},{9,8},{10,9},{13,12},{14,13},{17,16},{18,1... | collective-permute-start | bytes 983048 | tf_op jit(solution)/shard_map/ppermute | solution.py:285
  28.6 0.2 collective-permute-done.19
  28.8 4.4 %collective-permute-done.20 = f32[40,2048]{1,0:T(8,128)S(1)} collective-permute-done((f32[40,2048]{1,0:T(8,128)S(1)}, f32[40,2048]{1,0:T(8,128)S(1)}, u32[]{:S(2)}, u32[]{:S(2)}) %collective-permute-start.20) | collective-permute-done | bytes 327712 | tf_op jit(solution)/shard_map/ppermute | solution.py:285
  33.3 2.4 %collective-permute-start.21 = (f32[40,2048]{1,0:T(8,128)S(1)}, f32[40,2048]{1,0:T(8,128)S(1)}, u32[]{:S(2)}, u32[]{:S(2)}) collective-permute-start(f32[40,2048]{1,0:T(8,128)S(1)} %add.266.refs_3_), channel_id=1, source_target_pairs={{2,3},{1,0},{6,7},{5,4},{10,11},{9,8},{14,15},{13,12},{18,19},{17,... | collective-permute-start | bytes 983048 | tf_op jit(solution)/shard_map/ppermute | solution.py:282
  35.7 3.1 %collective-permute-done.37 = f32[40,2048]{1,0:T(8,128)S(1)} collective-permute-done((f32[40,2048]{1,0:T(8,128)S(1)}, f32[40,2048]{1,0:T(8,128)S(1)}, u32[]{:S(2)}, u32[]{:S(2)}) %collective-permute-start.37) | collective-permute-done | bytes 327712 | tf_op jit(solution)/shard_map/ppermute | solution.py:285
  38.8 3.9 %collective-permute-start.38 = (f32[40,2048]{1,0:T(8,128)S(1)}, f32[40,2048]{1,0:T(8,128)S(1)}, u32[]{:S(2)}, u32[]{:S(2)}) collective-permute-start(f32[40,2048]{1,0:T(8,128)S(1)} %add.274.refs_3_), channel_id=1, source_target_pairs={{2,3},{1,0},{6,7},{5,4},{10,11},{9,8},{14,15},{13,12},{18,19},{17,... | collective-permute-start | bytes 983048 | tf_op jit(solution)/shard_map/ppermute | solution.py:282
  42.8 0.1 stack.63.scalar_ref
  42.9 2.4 %collective-permute-done.21.refs_4_ = f32[40,2048]{1,0:T(8,128)S(1)} collective-permute-done((f32[40,2048]{1,0:T(8,128)S(1)}, f32[40,2048]{1,0:T(8,128)S(1)}, u32[]{:S(2)}, u32[]{:S(2)}) %collective-permute-start.21) | collective-permute-done | bytes 327712 | tf_op jit(solution)/shard_map/ppermute | solution.py:282
  45.3 6.0 %shard_map.76 = (f32[64,1024]{1,0:T(8,128)S(1)}, f32[64,1024]{1,0:T(8,128)S(1)}) custom-call(s32[6]{0:T(128)S(1)} %stack.63.scalar_ref, f32[128,128]{1,0:T(8,128)S(1)} %get-tuple-element.99.info_ref, f32[40,2048]{1,0:T(8,128)S(1)} %get-tuple-element.89.refs_0_, f32[40,2048]{1,0:T(8,128)S(1)} %collective-permute-done.17.refs_1_, ...), custom_call_target="tpu_custom_call" | custom-call | flops 1610612736 | bytes 8388608 | tf_op jit(solution)/shard_map/pallas_call | solution.py:181
  51.3 0.1 collective-permute-start.22
  51.4 3.0 %shard_map.78 = (f32[64,1024]{1,0:T(8,128)S(1)}, f32[64,1024]{1,0:T(8,128)S(1)}) custom-call(s32[6]{0:T(128)S(1)} %stack.63.scalar_ref, f32[128,128]{1,0:T(8,128)S(1)} %get-tuple-element.98.info_ref, f32[40,2048]{1,0:T(8,128)S(1)} %get-tuple-element.88.refs_0_, f32[40,2048]{1,0:T(8,128)S(1)} %collective-permute-done.34.refs_1_, ...), custom_call_target="tpu_custom_call" | custom-call | flops 1610612736 | bytes 8388608 | tf_op jit(solution)/shard_map/pallas_call | solution.py:181
  54.4 0.6 collective-permute-start.39
  55.0 1.6 %collective-permute-start.24 = (f32[32,1024]{1,0:T(8,128)S(1)}, f32[32,1024]{1,0:T(8,128)S(1)}, u32[]{:S(2)}, u32[]{:S(2)}) collective-permute-start(f32[32,1024]{1,0:T(8,128)S(1)} %get-tuple-element.96), channel_id=1, source_target_pairs={{0,16},{4,20},{8,24},{12,28},{16,0},{20,4},{24,8},{28,12},{1,17},{... | collective-permute-start | bytes 393224 | tf_op jit(solution)/shard_map/ppermute | solution.py:332
  56.6 1.5 %collective-permute-start.23 = (f32[32,1024]{1,0:T(8,128)S(1)}, f32[32,1024]{1,0:T(8,128)S(1)}, u32[]{:S(2)}, u32[]{:S(2)}) collective-permute-start(f32[32,1024]{1,0:T(8,128)S(1)} %get-tuple-element.97), channel_id=1, source_target_pairs={{0,8},{4,12},{8,0},{12,4},{16,24},{20,28},{24,16},{28,20},{1,9},{5... | collective-permute-start | bytes 393224 | tf_op jit(solution)/shard_map/ppermute | solution.py:332
  58.1 0.6 collective-permute-start.41
  58.7 0.6 collective-permute-start.40
  59.2 1.4 %collective-permute-done.24 = f32[32,1024]{1,0:T(8,128)S(1)} collective-permute-done((f32[32,1024]{1,0:T(8,128)S(1)}, f32[32,1024]{1,0:T(8,128)S(1)}, u32[]{:S(2)}, u32[]{:S(2)}) %collective-permute-start.24) | collective-permute-done | bytes 131104 | tf_op jit(solution)/shard_map/ppermute | solution.py:332
  60.6 2.4 %collective-permute-done.23 = f32[32,1024]{1,0:T(8,128)S(1)} collective-permute-done((f32[32,1024]{1,0:T(8,128)S(1)}, f32[32,1024]{1,0:T(8,128)S(1)}, u32[]{:S(2)}, u32[]{:S(2)}) %collective-permute-start.23) | collective-permute-done | bytes 131104 | tf_op jit(solution)/shard_map/ppermute | solution.py:332
  63.1 1.9 %collective-permute-start.26 = (f32[32,1024]{1,0:T(8,128)S(1)}, f32[32,1024]{1,0:T(8,128)S(1)}, u32[]{:S(2)}, u32[]{:S(2)}) collective-permute-start(f32[32,1024]{1,0:T(8,128)S(1)} %get-tuple-element.61), channel_id=1, source_target_pairs={{0,8},{4,12},{8,0},{12,4},{16,24},{20,28},{24,16},{28,20},{1,9},{5... | collective-permute-start | bytes 393224 | tf_op jit(solution)/shard_map/ppermute | solution.py:332
  65.0 0.4 collective-permute-done.40
  65.4 1.3 %collective-permute-start.42 = (f32[32,1024]{1,0:T(8,128)S(1)}, f32[32,1024]{1,0:T(8,128)S(1)}, u32[]{:S(2)}, u32[]{:S(2)}) collective-permute-start(f32[32,1024]{1,0:T(8,128)S(1)} %get-tuple-element.70), channel_id=1, source_target_pairs={{0,16},{4,20},{8,24},{12,28},{16,0},{20,4},{24,8},{28,12},{1,17},{... | collective-permute-start | bytes 393224 | tf_op jit(solution)/shard_map/ppermute | solution.py:332
  66.7 0.6 collective-permute-start.43
  67.3 1.6 %collective-permute-done.25 = f32[32,1024]{1,0:T(8,128)S(1)} collective-permute-done((f32[32,1024]{1,0:T(8,128)S(1)}, f32[32,1024]{1,0:T(8,128)S(1)}, u32[]{:S(2)}, u32[]{:S(2)}) %collective-permute-start.25) | collective-permute-done | bytes 131104 | tf_op jit(solution)/shard_map/ppermute | solution.py:332
  68.9 0.3 collective-permute-done.26
  69.2 0.1 collective-permute-start.27
  69.3 0.5 collective-permute-start.28
  69.8 0.1 stack.57.scalar_ref
  69.9 0.6 collective-permute-done.42
  70.5 1.2 collective-permute-done.43
  71.7 0.1 collective-permute-start.44
  71.8 0.5 collective-permute-start.45
  72.3 6.3 %shard_map.77 = (f32[32,2048]{1,0:T(8,128)S(1)}, f32[32,2048]{1,0:T(8,128)S(1)}, f32[32,2048]{1,0:T(8,128)S(1)}, f32[32,2048]{1,0:T(8,128)S(1)}) custom-call(s32[6]{0:T(128)S(1)} %stack.57.scalar_ref, f32[128,128]{1,0:T(8,128)S(1)} %get-tuple-element.99.info_ref, f32[1,1024]{1,0:T(1,128)S(1)} %bitcast.68, f32[2048,128]{1,0:T(8,128)S(1)} %copy-done.2, ...), custom_call_target="tpu_custom_call" | custom-call | flops 1610612736 | bytes 8388608 | tf_op jit(solution)/shard_map/pallas_call | solution.py:229
  78.6 1.3 %collective-permute-start.29 = (f32[32,2048]{1,0:T(8,128)S(1)}, f32[32,2048]{1,0:T(8,128)S(1)}, u32[]{:S(2)}, u32[]{:S(2)}) collective-permute-start(f32[32,2048]{1,0:T(8,128)S(1)} %get-tuple-element.65), channel_id=1, source_target_pairs={{0,1},{3,2},{4,5},{7,6},{8,9},{11,10},{12,13},{15,14},{16,17},{19,... | collective-permute-start | bytes 786440 | tf_op jit(solution)/shard_map/ppermute | solution.py:312
  79.9 1.5 %collective-permute-start.31 = (f32[32,2048]{1,0:T(8,128)S(1)}, f32[32,2048]{1,0:T(8,128)S(1)}, u32[]{:S(2)}, u32[]{:S(2)}) collective-permute-start(f32[32,2048]{1,0:T(8,128)S(1)} %get-tuple-element.66), channel_id=1, source_target_pairs={{0,1},{3,2},{4,5},{7,6},{8,9},{11,10},{12,13},{15,14},{16,17},{19,... | collective-permute-start | bytes 786440 | tf_op jit(solution)/shard_map/ppermute | solution.py:312
  81.4 6.3 %shard_map.79 = (f32[32,2048]{1,0:T(8,128)S(1)}, f32[32,2048]{1,0:T(8,128)S(1)}, f32[32,2048]{1,0:T(8,128)S(1)}, f32[32,2048]{1,0:T(8,128)S(1)}) custom-call(s32[6]{0:T(128)S(1)} %stack.57.scalar_ref, f32[128,128]{1,0:T(8,128)S(1)} %get-tuple-element.98.info_ref, f32[1,1024]{1,0:T(1,128)S(1)} %bitcast.69, f32[2048,128]{1,0:T(8,128)S(1)} %copy-done.2, ...), custom_call_target="tpu_custom_call" | custom-call | flops 1610612736 | bytes 8388608 | tf_op jit(solution)/shard_map/pallas_call | solution.py:229
  87.8 1.3 %collective-permute-start.46 = (f32[32,2048]{1,0:T(8,128)S(1)}, f32[32,2048]{1,0:T(8,128)S(1)}, u32[]{:S(2)}, u32[]{:S(2)}) collective-permute-start(f32[32,2048]{1,0:T(8,128)S(1)} %get-tuple-element.75), channel_id=1, source_target_pairs={{0,1},{3,2},{4,5},{7,6},{8,9},{11,10},{12,13},{15,14},{16,17},{19,... | collective-permute-start | bytes 786440 | tf_op jit(solution)/shard_map/ppermute | solution.py:312
  89.1 1.3 %collective-permute-start.48 = (f32[32,2048]{1,0:T(8,128)S(1)}, f32[32,2048]{1,0:T(8,128)S(1)}, u32[]{:S(2)}, u32[]{:S(2)}) collective-permute-start(f32[32,2048]{1,0:T(8,128)S(1)} %get-tuple-element.76), channel_id=1, source_target_pairs={{0,1},{3,2},{4,5},{7,6},{8,9},{11,10},{12,13},{15,14},{16,17},{19,... | collective-permute-start | bytes 786440 | tf_op jit(solution)/shard_map/ppermute | solution.py:312
  90.4 2.8 %collective-permute-start.33 = (f32[32,2048]{1,0:T(8,128)S(1)}, f32[32,2048]{1,0:T(8,128)S(1)}, u32[]{:S(2)}, u32[]{:S(2)}) collective-permute-start(f32[32,2048]{1,0:T(8,128)S(1)} %get-tuple-element.67), channel_id=1, source_target_pairs={{0,1},{1,0},{2,3},{3,2},{4,5},{5,4},{6,7},{7,6},{8,9},{9,8},{10,11... | collective-permute-start | bytes 786440 | tf_op jit(solution)/shard_map/ppermute | solution.py:317
  93.1 0.1 collective-permute-start.50
  93.2 2.0 %collective-permute-done.31 = f32[32,2048]{1,0:T(8,128)S(1)} collective-permute-done((f32[32,2048]{1,0:T(8,128)S(1)}, f32[32,2048]{1,0:T(8,128)S(1)}, u32[]{:S(2)}, u32[]{:S(2)}) %collective-permute-start.31) | collective-permute-done | bytes 262176 | tf_op jit(solution)/shard_map/ppermute | solution.py:312
  95.3 1.3 %collective-permute-start.30 = (f32[32,2048]{1,0:T(8,128)S(1)}, f32[32,2048]{1,0:T(8,128)S(1)}, u32[]{:S(2)}, u32[]{:S(2)}) collective-permute-start(f32[32,2048]{1,0:T(8,128)S(1)} %add.272), channel_id=1, source_target_pairs={{1,3},{2,0},{5,7},{6,4},{9,11},{10,8},{13,15},{14,12},{17,19},{18,... | collective-permute-start | bytes 786440 | tf_op jit(solution)/shard_map/ppermute | solution.py:314
  96.7 4.2 %collective-permute-done.46 = f32[32,2048]{1,0:T(8,128)S(1)} collective-permute-done((f32[32,2048]{1,0:T(8,128)S(1)}, f32[32,2048]{1,0:T(8,128)S(1)}, u32[]{:S(2)}, u32[]{:S(2)}) %collective-permute-start.46) | collective-permute-done | bytes 262176 | tf_op jit(solution)/shard_map/ppermute | solution.py:312
  100.9 1.9 %collective-permute-start.32 = (f32[32,2048]{1,0:T(8,128)S(1)}, f32[32,2048]{1,0:T(8,128)S(1)}, u32[]{:S(2)}, u32[]{:S(2)}) collective-permute-start(f32[32,2048]{1,0:T(8,128)S(1)} %add.273), channel_id=1, source_target_pairs={{1,2},{2,1},{5,6},{6,5},{9,10},{10,9},{13,14},{14,13},{17,18},{18,... | collective-permute-start | bytes 786440 | tf_op jit(solution)/shard_map/ppermute | solution.py:314
  102.8 0.7 add.280
  103.5 3.0 %collective-permute-done.48 = f32[32,2048]{1,0:T(8,128)S(1)} collective-permute-done((f32[32,2048]{1,0:T(8,128)S(1)}, f32[32,2048]{1,0:T(8,128)S(1)}, u32[]{:S(2)}, u32[]{:S(2)}) %collective-permute-start.48) | collective-permute-done | bytes 262176 | tf_op jit(solution)/shard_map/ppermute | solution.py:312
  106.5 1.3 %collective-permute-start.47 = (f32[32,2048]{1,0:T(8,128)}, f32[32,2048]{1,0:T(8,128)S(1)}, u32[]{:S(2)}, u32[]{:S(2)}) collective-permute-start(f32[32,2048]{1,0:T(8,128)} %add.280), channel_id=1, source_target_pairs={{1,3},{2,0},{5,7},{6,4},{9,11},{10,8},{13,15},{14,12},{17,19},{18,... | collective-permute-start | bytes 786440 | tf_op jit(solution)/shard_map/ppermute | solution.py:314
  107.8 0.8 add.281
  108.6 3.6 %collective-permute-done.33.refs_3_ = f32[32,2048]{1,0:T(8,128)S(1)} collective-permute-done((f32[32,2048]{1,0:T(8,128)S(1)}, f32[32,2048]{1,0:T(8,128)S(1)}, u32[]{:S(2)}, u32[]{:S(2)}) %collective-permute-start.33) | collective-permute-done | bytes 262176 | tf_op jit(solution)/shard_map/ppermute | solution.py:317
  112.1 1.9 %collective-permute-start.49 = (f32[32,2048]{1,0:T(8,128)}, f32[32,2048]{1,0:T(8,128)S(1)}, u32[]{:S(2)}, u32[]{:S(2)}) collective-permute-start(f32[32,2048]{1,0:T(8,128)} %add.281), channel_id=1, source_target_pairs={{1,2},{2,1},{5,6},{6,5},{9,10},{10,9},{13,14},{14,13},{17,18},{18,... | collective-permute-start | bytes 786440 | tf_op jit(solution)/shard_map/ppermute | solution.py:314
  114.0 0.7 slice_reduce_fusion
  115.3 1.7 %collective-permute-done.50.refs_7_ = f32[32,2048]{1,0:T(8,128)S(1)} collective-permute-done((f32[32,2048]{1,0:T(8,128)S(1)}, f32[32,2048]{1,0:T(8,128)S(1)}, u32[]{:S(2)}, u32[]{:S(2)}) %collective-permute-start.50) | collective-permute-done | bytes 262176 | tf_op jit(solution)/shard_map/ppermute | solution.py:317
  117.0 4.0 %collective-permute-done.49.refs_6_ = f32[32,2048]{1,0:T(8,128)S(1)} collective-permute-done((f32[32,2048]{1,0:T(8,128)}, f32[32,2048]{1,0:T(8,128)S(1)}, u32[]{:S(2)}, u32[]{:S(2)}) %collective-permute-start.49) | collective-permute-done | bytes 262176 | tf_op jit(solution)/shard_map/ppermute | solution.py:314
  121.1 1.2 shard_map.80
  122.3 0.3 conditional.1
  (44 shorter events, 0.7 us)
Async XLA Ops:
  3.2 12.5 %collective-permute-start.17 = (f32[40,2048]{1,0:T(8,128)S(1)}, f32[40,2048]{1,0:T(8,128)S(1)}, u32[]{:S(2)}, u32[]{:S(2)}) collective-permute-start(f32[40,2048]{1,0:T(8,128)S(1)} %get-tuple-element.89.refs_0_), channel_id=1, source_target_pairs={{0,1},{1,2},{2,3},{4,5},{5,6},{6,7},{8,9},{9,10},{10,11},{12,13},{... | collective-permute-start | bytes 983048 | tf_op jit(solution)/shard_map/ppermute | solution.py:284
  6.7 12.5 %collective-permute-start.18 = (f32[40,2048]{1,0:T(8,128)S(1)}, f32[40,2048]{1,0:T(8,128)S(1)}, u32[]{:S(2)}, u32[]{:S(2)}) collective-permute-start(f32[40,2048]{1,0:T(8,128)S(1)} %get-tuple-element.89.refs_0_), channel_id=1, source_target_pairs={{1,0},{2,1},{3,2},{5,4},{6,5},{7,6},{9,8},{10,9},{11,10},{13,12},{... | collective-permute-start | bytes 983048 | tf_op jit(solution)/shard_map/ppermute | solution.py:285
  9.0 12.7 %collective-permute-start.34 = (f32[40,2048]{1,0:T(8,128)S(1)}, f32[40,2048]{1,0:T(8,128)S(1)}, u32[]{:S(2)}, u32[]{:S(2)}) collective-permute-start(f32[40,2048]{1,0:T(8,128)S(1)} %get-tuple-element.88.refs_0_), channel_id=1, source_target_pairs={{0,1},{1,2},{2,3},{4,5},{5,6},{6,7},{8,9},{9,10},{10,11},{12,13},{... | collective-permute-start | bytes 983048 | tf_op jit(solution)/shard_map/ppermute | solution.py:284
  12.5 13.7 %collective-permute-start.35 = (f32[40,2048]{1,0:T(8,128)S(1)}, f32[40,2048]{1,0:T(8,128)S(1)}, u32[]{:S(2)}, u32[]{:S(2)}) collective-permute-start(f32[40,2048]{1,0:T(8,128)S(1)} %get-tuple-element.88.refs_0_), channel_id=1, source_target_pairs={{1,0},{2,1},{3,2},{5,4},{6,5},{7,6},{9,8},{10,9},{11,10},{13,12},{... | collective-permute-start | bytes 983048 | tf_op jit(solution)/shard_map/ppermute | solution.py:285
  15.7 13.1 %collective-permute-start.19 = (f32[40,2048]{1,0:T(8,128)S(1)}, f32[40,2048]{1,0:T(8,128)S(1)}, u32[]{:S(2)}, u32[]{:S(2)}) collective-permute-start(f32[40,2048]{1,0:T(8,128)S(1)} %collective-permute-done.17.refs_1_), channel_id=1, source_target_pairs={{1,2},{2,3},{5,6},{6,7},{9,10},{10,11},{13,14},{14,15},{17,18},{18... | collective-permute-start | bytes 983048 | tf_op jit(solution)/shard_map/ppermute | solution.py:284
  19.2 14.0 %collective-permute-start.20 = (f32[40,2048]{1,0:T(8,128)S(1)}, f32[40,2048]{1,0:T(8,128)S(1)}, u32[]{:S(2)}, u32[]{:S(2)}) collective-permute-start(f32[40,2048]{1,0:T(8,128)S(1)} %collective-permute-done.18.refs_2_), channel_id=1, source_target_pairs={{1,0},{2,1},{5,4},{6,5},{9,8},{10,9},{13,12},{14,13},{17,16},{18,1... | collective-permute-start | bytes 983048 | tf_op jit(solution)/shard_map/ppermute | solution.py:285
  21.8 13.9 %collective-permute-start.36 = (f32[40,2048]{1,0:T(8,128)S(1)}, f32[40,2048]{1,0:T(8,128)S(1)}, u32[]{:S(2)}, u32[]{:S(2)}) collective-permute-start(f32[40,2048]{1,0:T(8,128)S(1)} %collective-permute-done.34.refs_1_), channel_id=1, source_target_pairs={{1,2},{2,3},{5,6},{6,7},{9,10},{10,11},{13,14},{14,15},{17,18},{18... | collective-permute-start | bytes 983048 | tf_op jit(solution)/shard_map/ppermute | solution.py:284
  26.2 12.6 %collective-permute-start.37 = (f32[40,2048]{1,0:T(8,128)S(1)}, f32[40,2048]{1,0:T(8,128)S(1)}, u32[]{:S(2)}, u32[]{:S(2)}) collective-permute-start(f32[40,2048]{1,0:T(8,128)S(1)} %collective-permute-done.35.refs_2_), channel_id=1, source_target_pairs={{1,0},{2,1},{5,4},{6,5},{9,8},{10,9},{13,12},{14,13},{17,16},{18,1... | collective-permute-start | bytes 983048 | tf_op jit(solution)/shard_map/ppermute | solution.py:285
  33.3 12.0 %collective-permute-start.21 = (f32[40,2048]{1,0:T(8,128)S(1)}, f32[40,2048]{1,0:T(8,128)S(1)}, u32[]{:S(2)}, u32[]{:S(2)}) collective-permute-start(f32[40,2048]{1,0:T(8,128)S(1)} %add.266.refs_3_), channel_id=1, source_target_pairs={{2,3},{1,0},{6,7},{5,4},{10,11},{9,8},{14,15},{13,12},{18,19},{17,... | collective-permute-start | bytes 983048 | tf_op jit(solution)/shard_map/ppermute | solution.py:282
  38.8 12.5 %collective-permute-start.38 = (f32[40,2048]{1,0:T(8,128)S(1)}, f32[40,2048]{1,0:T(8,128)S(1)}, u32[]{:S(2)}, u32[]{:S(2)}) collective-permute-start(f32[40,2048]{1,0:T(8,128)S(1)} %add.274.refs_3_), channel_id=1, source_target_pairs={{2,3},{1,0},{6,7},{5,4},{10,11},{9,8},{14,15},{13,12},{18,19},{17,... | collective-permute-start | bytes 983048 | tf_op jit(solution)/shard_map/ppermute | solution.py:282
  45.3 6.1 %copy-start = (f32[2048,1024]{1,0:T(8,128)S(1)}, f32[2048,1024]{1,0:T(8,128)}, u32[]{:S(2)}) copy-start(f32[2048,1024]{1,0:T(8,128)} %x_ref.3) | copy-start | bytes 25165828
  51.3 3.7 %collective-permute-start.22 = (f32[64,1024]{1,0:T(8,128)S(1)}, f32[64,1024]{1,0:T(8,128)S(1)}, u32[]{:S(2)}, u32[]{:S(2)}) collective-permute-start(f32[64,1024]{1,0:T(8,128)S(1)} %get-tuple-element.59), channel_id=1, source_target_pairs={{0,4},{4,0},{8,12},{12,8},{16,20},{20,16},{24,28},{28,24},{1,5},{5... | collective-permute-start | bytes 786440 | tf_op jit(solution)/shard_map/ppermute | solution.py:325
  54.4 3.7 %collective-permute-start.39 = (f32[64,1024]{1,0:T(8,128)S(1)}, f32[64,1024]{1,0:T(8,128)S(1)}, u32[]{:S(2)}, u32[]{:S(2)}) collective-permute-start(f32[64,1024]{1,0:T(8,128)S(1)} %get-tuple-element.69), channel_id=1, source_target_pairs={{0,4},{4,0},{8,12},{12,8},{16,20},{20,16},{24,28},{28,24},{1,5},{5... | collective-permute-start | bytes 786440 | tf_op jit(solution)/shard_map/ppermute | solution.py:325
  55.0 5.6 %collective-permute-start.24 = (f32[32,1024]{1,0:T(8,128)S(1)}, f32[32,1024]{1,0:T(8,128)S(1)}, u32[]{:S(2)}, u32[]{:S(2)}) collective-permute-start(f32[32,1024]{1,0:T(8,128)S(1)} %get-tuple-element.96), channel_id=1, source_target_pairs={{0,16},{4,20},{8,24},{12,28},{16,0},{20,4},{24,8},{28,12},{1,17},{... | collective-permute-start | bytes 393224 | tf_op jit(solution)/shard_map/ppermute | solution.py:332
  56.6 6.4 %collective-permute-start.23 = (f32[32,1024]{1,0:T(8,128)S(1)}, f32[32,1024]{1,0:T(8,128)S(1)}, u32[]{:S(2)}, u32[]{:S(2)}) collective-permute-start(f32[32,1024]{1,0:T(8,128)S(1)} %get-tuple-element.97), channel_id=1, source_target_pairs={{0,8},{4,12},{8,0},{12,4},{16,24},{20,28},{24,16},{28,20},{1,9},{5... | collective-permute-start | bytes 393224 | tf_op jit(solution)/shard_map/ppermute | solution.py:332
  58.1 14.2 %copy-start.2 = (f32[2048,128]{1,0:T(8,128)S(1)}, f32[2048,128]{1,0:T(8,128)}, u32[]{:S(2)}) copy-start(f32[2048,128]{1,0:T(8,128)} %vectors_ref.5) | copy-start | bytes 3145732
  58.1 14.2 %copy-start.6 = (f32[1024]{0:T(1024)S(1)}, f32[1024]{0:T(1024)}, u32[]{:S(2)}) copy-start(f32[1024]{0:T(1024)} %param.10) | copy-start | bytes 12292
  58.1 6.8 %collective-permute-start.41 = (f32[32,1024]{1,0:T(8,128)S(1)}, f32[32,1024]{1,0:T(8,128)S(1)}, u32[]{:S(2)}, u32[]{:S(2)}) collective-permute-start(f32[32,1024]{1,0:T(8,128)S(1)} %get-tuple-element.92), channel_id=1, source_target_pairs={{0,16},{4,20},{8,24},{12,28},{16,0},{20,4},{24,8},{28,12},{1,17},{... | collective-permute-start | bytes 393224 | tf_op jit(solution)/shard_map/ppermute | solution.py:332
  58.7 6.7 %collective-permute-start.40 = (f32[32,1024]{1,0:T(8,128)S(1)}, f32[32,1024]{1,0:T(8,128)S(1)}, u32[]{:S(2)}, u32[]{:S(2)}) collective-permute-start(f32[32,1024]{1,0:T(8,128)S(1)} %get-tuple-element.93), channel_id=1, source_target_pairs={{0,8},{4,12},{8,0},{12,4},{16,24},{20,28},{24,16},{28,20},{1,9},{5... | collective-permute-start | bytes 393224 | tf_op jit(solution)/shard_map/ppermute | solution.py:332
  63.0 5.9 %collective-permute-start.25 = (f32[32,1024]{1,0:T(8,128)S(1)}, f32[32,1024]{1,0:T(8,128)S(1)}, u32[]{:S(2)}, u32[]{:S(2)}) collective-permute-start(f32[32,1024]{1,0:T(8,128)S(1)} %get-tuple-element.60), channel_id=1, source_target_pairs={{0,16},{4,20},{8,24},{12,28},{16,0},{20,4},{24,8},{28,12},{1,17},{... | collective-permute-start | bytes 393224 | tf_op jit(solution)/shard_map/ppermute | solution.py:332
  63.1 6.1 %collective-permute-start.26 = (f32[32,1024]{1,0:T(8,128)S(1)}, f32[32,1024]{1,0:T(8,128)S(1)}, u32[]{:S(2)}, u32[]{:S(2)}) collective-permute-start(f32[32,1024]{1,0:T(8,128)S(1)} %get-tuple-element.61), channel_id=1, source_target_pairs={{0,8},{4,12},{8,0},{12,4},{16,24},{20,28},{24,16},{28,20},{1,9},{5... | collective-permute-start | bytes 393224 | tf_op jit(solution)/shard_map/ppermute | solution.py:332
  65.4 5.0 %collective-permute-start.42 = (f32[32,1024]{1,0:T(8,128)S(1)}, f32[32,1024]{1,0:T(8,128)S(1)}, u32[]{:S(2)}, u32[]{:S(2)}) collective-permute-start(f32[32,1024]{1,0:T(8,128)S(1)} %get-tuple-element.70), channel_id=1, source_target_pairs={{0,16},{4,20},{8,24},{12,28},{16,0},{20,4},{24,8},{28,12},{1,17},{... | collective-permute-start | bytes 393224 | tf_op jit(solution)/shard_map/ppermute | solution.py:332
  66.7 5.0 %collective-permute-start.43 = (f32[32,1024]{1,0:T(8,128)S(1)}, f32[32,1024]{1,0:T(8,128)S(1)}, u32[]{:S(2)}, u32[]{:S(2)}) collective-permute-start(f32[32,1024]{1,0:T(8,128)S(1)} %get-tuple-element.71), channel_id=1, source_target_pairs={{0,8},{4,12},{8,0},{12,4},{16,24},{20,28},{24,16},{28,20},{1,9},{5... | collective-permute-start | bytes 393224 | tf_op jit(solution)/shard_map/ppermute | solution.py:332
  69.2 3.0 %collective-permute-start.27 = (f32[32,1024]{1,0:T(8,128)S(1)}, f32[32,1024]{1,0:T(8,128)S(1)}, u32[]{:S(2)}, u32[]{:S(2)}) collective-permute-start(f32[32,1024]{1,0:T(8,128)S(1)} %add.270.refs_0_), channel_id=1, source_target_pairs={{0,4},{4,0},{8,12},{12,8},{16,20},{20,16},{24,28},{28,24},{1,5},{5... | collective-permute-start | bytes 393224 | tf_op jit(solution)/shard_map/ppermute | solution.py:336
  69.3 3.0 %collective-permute-start.28 = (f32[32,1024]{1,0:T(8,128)S(1)}, f32[32,1024]{1,0:T(8,128)S(1)}, u32[]{:S(2)}, u32[]{:S(2)}) collective-permute-start(f32[32,1024]{1,0:T(8,128)S(1)} %add.271.refs_1_), channel_id=1, source_target_pairs={{0,4},{4,0},{8,12},{12,8},{16,20},{20,16},{24,28},{28,24},{1,5},{5... | collective-permute-start | bytes 393224 | tf_op jit(solution)/shard_map/ppermute | solution.py:336
  71.7 9.7 %collective-permute-start.44 = (f32[32,1024]{1,0:T(8,128)S(1)}, f32[32,1024]{1,0:T(8,128)S(1)}, u32[]{:S(2)}, u32[]{:S(2)}) collective-permute-start(f32[32,1024]{1,0:T(8,128)S(1)} %add.278.refs_0_), channel_id=1, source_target_pairs={{0,4},{4,0},{8,12},{12,8},{16,20},{20,16},{24,28},{28,24},{1,5},{5... | collective-permute-start | bytes 393224 | tf_op jit(solution)/shard_map/ppermute | solution.py:336
  71.8 9.6 %collective-permute-start.45 = (f32[32,1024]{1,0:T(8,128)S(1)}, f32[32,1024]{1,0:T(8,128)S(1)}, u32[]{:S(2)}, u32[]{:S(2)}) collective-permute-start(f32[32,1024]{1,0:T(8,128)S(1)} %add.279.refs_1_), channel_id=1, source_target_pairs={{0,4},{4,0},{8,12},{12,8},{16,20},{20,16},{24,28},{28,24},{1,5},{5... | collective-permute-start | bytes 393224 | tf_op jit(solution)/shard_map/ppermute | solution.py:336
  78.6 14.5 %collective-permute-start.29 = (f32[32,2048]{1,0:T(8,128)S(1)}, f32[32,2048]{1,0:T(8,128)S(1)}, u32[]{:S(2)}, u32[]{:S(2)}) collective-permute-start(f32[32,2048]{1,0:T(8,128)S(1)} %get-tuple-element.65), channel_id=1, source_target_pairs={{0,1},{3,2},{4,5},{7,6},{8,9},{11,10},{12,13},{15,14},{16,17},{19,... | collective-permute-start | bytes 786440 | tf_op jit(solution)/shard_map/ppermute | solution.py:312
  79.9 15.4 %collective-permute-start.31 = (f32[32,2048]{1,0:T(8,128)S(1)}, f32[32,2048]{1,0:T(8,128)S(1)}, u32[]{:S(2)}, u32[]{:S(2)}) collective-permute-start(f32[32,2048]{1,0:T(8,128)S(1)} %get-tuple-element.66), channel_id=1, source_target_pairs={{0,1},{3,2},{4,5},{7,6},{8,9},{11,10},{12,13},{15,14},{16,17},{19,... | collective-permute-start | bytes 786440 | tf_op jit(solution)/shard_map/ppermute | solution.py:312
  87.8 13.1 %collective-permute-start.46 = (f32[32,2048]{1,0:T(8,128)S(1)}, f32[32,2048]{1,0:T(8,128)S(1)}, u32[]{:S(2)}, u32[]{:S(2)}) collective-permute-start(f32[32,2048]{1,0:T(8,128)S(1)} %get-tuple-element.75), channel_id=1, source_target_pairs={{0,1},{3,2},{4,5},{7,6},{8,9},{11,10},{12,13},{15,14},{16,17},{19,... | collective-permute-start | bytes 786440 | tf_op jit(solution)/shard_map/ppermute | solution.py:312
  89.1 17.5 %collective-permute-start.48 = (f32[32,2048]{1,0:T(8,128)S(1)}, f32[32,2048]{1,0:T(8,128)S(1)}, u32[]{:S(2)}, u32[]{:S(2)}) collective-permute-start(f32[32,2048]{1,0:T(8,128)S(1)} %get-tuple-element.76), channel_id=1, source_target_pairs={{0,1},{3,2},{4,5},{7,6},{8,9},{11,10},{12,13},{15,14},{16,17},{19,... | collective-permute-start | bytes 786440 | tf_op jit(solution)/shard_map/ppermute | solution.py:312
  90.4 21.8 %collective-permute-start.33 = (f32[32,2048]{1,0:T(8,128)S(1)}, f32[32,2048]{1,0:T(8,128)S(1)}, u32[]{:S(2)}, u32[]{:S(2)}) collective-permute-start(f32[32,2048]{1,0:T(8,128)S(1)} %get-tuple-element.67), channel_id=1, source_target_pairs={{0,1},{1,0},{2,3},{3,2},{4,5},{5,4},{6,7},{7,6},{8,9},{9,8},{10,11... | collective-permute-start | bytes 786440 | tf_op jit(solution)/shard_map/ppermute | solution.py:317
  93.1 23.9 %collective-permute-start.50 = (f32[32,2048]{1,0:T(8,128)S(1)}, f32[32,2048]{1,0:T(8,128)S(1)}, u32[]{:S(2)}, u32[]{:S(2)}) collective-permute-start(f32[32,2048]{1,0:T(8,128)S(1)} %get-tuple-element.77), channel_id=1, source_target_pairs={{0,1},{1,0},{2,3},{3,2},{4,5},{5,4},{6,7},{7,6},{8,9},{9,8},{10,11... | collective-permute-start | bytes 786440 | tf_op jit(solution)/shard_map/ppermute | solution.py:317
  95.3 21.7 %collective-permute-start.30 = (f32[32,2048]{1,0:T(8,128)S(1)}, f32[32,2048]{1,0:T(8,128)S(1)}, u32[]{:S(2)}, u32[]{:S(2)}) collective-permute-start(f32[32,2048]{1,0:T(8,128)S(1)} %add.272), channel_id=1, source_target_pairs={{1,3},{2,0},{5,7},{6,4},{9,11},{10,8},{13,15},{14,12},{17,19},{18,... | collective-permute-start | bytes 786440 | tf_op jit(solution)/shard_map/ppermute | solution.py:314
  96.6 25.7 %copy-start.1 = (f32[512]{0:T(512)S(1)}, f32[512]{0:T(512)}, u32[]{:S(2)}) copy-start(f32[512]{0:T(512)} %param.13) | copy-start | bytes 6148
  96.6 25.7 %copy-start.5 = (s32[256]{0:T(256)S(1)}, s32[256]{0:T(256)}, u32[]{:S(2)}) copy-start(s32[256]{0:T(256)} %param.14) | copy-start | bytes 3076
  96.6 25.6 %copy-start.7 = (s32[256]{0:T(256)S(1)}, s32[256]{0:T(256)}, u32[]{:S(2)}) copy-start(s32[256]{0:T(256)} %param.15) | copy-start | bytes 3076
  100.9 16.1 %collective-permute-start.32 = (f32[32,2048]{1,0:T(8,128)S(1)}, f32[32,2048]{1,0:T(8,128)S(1)}, u32[]{:S(2)}, u32[]{:S(2)}) collective-permute-start(f32[32,2048]{1,0:T(8,128)S(1)} %add.273), channel_id=1, source_target_pairs={{1,2},{2,1},{5,6},{6,5},{9,10},{10,9},{13,14},{14,13},{17,18},{18,... | collective-permute-start | bytes 786440 | tf_op jit(solution)/shard_map/ppermute | solution.py:314
  106.5 10.5 %collective-permute-start.47 = (f32[32,2048]{1,0:T(8,128)}, f32[32,2048]{1,0:T(8,128)S(1)}, u32[]{:S(2)}, u32[]{:S(2)}) collective-permute-start(f32[32,2048]{1,0:T(8,128)} %add.280), channel_id=1, source_target_pairs={{1,3},{2,0},{5,7},{6,4},{9,11},{10,8},{13,15},{14,12},{17,19},{18,... | collective-permute-start | bytes 786440 | tf_op jit(solution)/shard_map/ppermute | solution.py:314
  112.1 8.9 %collective-permute-start.49 = (f32[32,2048]{1,0:T(8,128)}, f32[32,2048]{1,0:T(8,128)S(1)}, u32[]{:S(2)}, u32[]{:S(2)}) collective-permute-start(f32[32,2048]{1,0:T(8,128)} %add.281), channel_id=1, source_target_pairs={{1,2},{2,1},{5,6},{6,5},{9,10},{10,9},{13,14},{14,13},{17,18},{18,... | collective-permute-start | bytes 786440 | tf_op jit(solution)/shard_map/ppermute | solution.py:314

commit v3 on v2

--- a/solution.py
+++ b/solution.py
@@ -22,6 +22,7 @@
 PARTS = 2
 VMEM = pl.BlockSpec(memory_space=pltpu.VMEM)
 SMEM = pl.BlockSpec(memory_space=pltpu.SMEM)
+HBM = pl.BlockSpec(memory_space=pltpu.HBM)
 
 
 def split(x, count):
@@ -188,9 +189,24 @@
     )(scalars, info, *[b for b, _ in buffers], high_vectors)
 
 
+def copies_of(x_ref, held_ref, sems):
+    rows = x_ref.shape[0] // sems.shape[0]
+    spans = [slice(i * rows, (i + 1) * rows) for i in range(sems.shape[0])]
+    copies = [
+        pltpu.make_async_copy(
+            x_ref.at[pl.ds(i * rows, rows)], held_ref.at[pl.ds(i * rows, rows)], sems.at[i]
+        )
+        for i in range(len(spans))
+    ]
+    return list(zip(copies, spans))
+
+
 def image_kernel(pieces, scalar_ref, info_ref, mu_ref, vectors_ref, x_ref, *refs):
     sums, outs = refs[: 2 * pieces], refs[2 * pieces :]
-    *outs, sums_ref = outs
+    *outs, sums_ref, held_ref, sems = outs
+    copies = copies_of(x_ref, held_ref, sems)
+    for copy, _ in copies:
+        copy.start()
     count = info_ref.shape[0]
     block = outs[0].shape[0]
     first = scalar_ref[len(outs) + 1] == 0
@@ -212,7 +228,9 @@
     width = vectors_ref.shape[1]
     spot = lax.broadcasted_iota(jnp.int32, (count, width), 1) + scalar_ref[len(outs)] * width
     mine = jnp.where(spot.astype(F32) == info[:, 0:1], 1.0, 0.0).astype(BF16)
-    for span, (x_high, x_low) in pieces_of(x_ref, 256):
+    for copy, span in copies:
+        copy.wait()
+        x_high, x_low = split(held_ref[span], 2)
         chosen = total([dot(mine, p, ((1,), (1,))) for p in split(vectors_ref[span], 3)])
         image = dot(both, x_high, ((1,), (1,)))
         image = image[:count] + image[count:] + dot(d_high, x_low, ((1,), (1,)))
@@ -229,9 +247,13 @@
     return pl.pallas_call(
         functools.partial(image_kernel, len(sums) // 2),
         out_shape=[jax.ShapeDtypeStruct((block, depth), F32)] * len(order),
-        in_specs=[SMEM] + [VMEM] * (len(sums) + 4),
+        in_specs=[SMEM] + [VMEM] * 3 + [HBM] + [VMEM] * len(sums),
         out_specs=[VMEM] * len(order),
-        scratch_shapes=[pltpu.VMEM((count, k), F32)],
+        scratch_shapes=[
+            pltpu.VMEM((count, k), F32),
+            pltpu.VMEM((depth, k), F32),
+            pltpu.SemaphoreType.DMA((4,)),
+        ],
         compiler_params=pltpu.CompilerParams(vmem_limit_bytes=24 << 20),
         cost_estimate=cost(count, high_vectors),
     )(scalars, info, high_values[None, :], pool_vectors, high_vectors, *sums)

time: 123 us -> 123 us (level)
  transfers between devices with their start and end apart: 34 -> 34, of which waited for: 19 -> 19; matrix products, arithmetic and copies ran while one was open for 2% -> 2% of each run, Pallas kernels for 18% -> 17%
where the time goes in v3:
time: 123 us; the launch traced here: 122 us
  starting transfers between devices  54.9 us (45%)
  waiting for transfers between devices  38.1 us (31%)
  Pallas kernels  24.8 us (20%)
  other arithmetic  2.57 us (2%)
    ppermute x4, starting transfers between devices, gather_line(): came_left = lax.ppermute(from_left, axis, right)  14.8 us
    pallas_call x2, Pallas kernels, image(): pl.pallas_call(functools.partial(image_kernel, len(sums) // 2), out_shape...  11.5 us
    ppermute x4, waiting for transfers between devices, scatter_line(): came = lax.ppermute(rows, axis, mirrored(n, [(hop, hop + 1)]))  9.81 us
    ppermute x4, starting transfers between devices, gather_line(): came_right = lax.ppermute(from_right, axis, left)  9.5 us
    pallas_call x2, Pallas kernels, product(): pl.pallas_call(functools.partial(product_kernel, width, n), out_shape=[ja...  8.98 us
    ppermute x8, starting transfers between devices, sum_pairs(): lax.ppermute(pieces[i], axis, [(d, d ^ bit) for d in range(n)])  7.98 us
    ppermute x8, waiting for transfers between devices, sum_pairs(): lax.ppermute(pieces[i], axis, [(d, d ^ bit) for d in range(n)])  7.83 us
    ppermute x4, waiting for transfers between devices, gather_line(): came_right = lax.ppermute(from_right, axis, left)  7.6 us
  transfers between devices with their start and end apart: 34, of which 19 were waited for; matrix products, arithmetic and copies ran while one was open for 2% of the time, Pallas kernels for 17%

profile of v3, /device:TPU:8, one launch (start us, length us, event | category | flops | bytes accessed | tf_op | source)
XLA Modules:
  0.0 122.2 jit_solution(6052764576257469489)
XLA Ops:
  0.0 3.1 %shard_map.75 = (f32[2,128,128]{2,1,0:T(8,128)S(1)}, f32[2,40,2048]{2,1,0:T(8,128)S(1)}) custom-call(s32[1]{0:T(128)} %bitcast.7.me_ref, s32[1,256]{1,0:T(1,128)} %bitcast.67, s32[1,256]{1,0:T(1,128)} %bitcast.70, f32[1,512]{1,0:T(1,128)} %bitcast.63, f32[2048,128]{1,0:T(8,128)} %vectors_ref.5, f32[2048,128]{1,0:T(8,128)} %images_ref.1), custom_call_target="tpu_custom_call" | custom-call | tf_op jit(solution)/shard_map/pallas_call | solution.py:119
  3.2 3.5 %collective-permute-start.17 = (f32[40,2048]{1,0:T(8,128)S(1)}, f32[40,2048]{1,0:T(8,128)S(1)}, u32[]{:S(2)}, u32[]{:S(2)}) collective-permute-start(f32[40,2048]{1,0:T(8,128)S(1)} %get-tuple-element.89.refs_0_), channel_id=1, source_target_pairs={{0,1},{1,2},{2,3},{4,5},{5,6},{6,7},{8,9},{9,10},{10,11},{12,13},{... | collective-permute-start | bytes 983048 | tf_op jit(solution)/shard_map/ppermute | solution.py:306
  6.7 2.4 %collective-permute-start.18 = (f32[40,2048]{1,0:T(8,128)S(1)}, f32[40,2048]{1,0:T(8,128)S(1)}, u32[]{:S(2)}, u32[]{:S(2)}) collective-permute-start(f32[40,2048]{1,0:T(8,128)S(1)} %get-tuple-element.89.refs_0_), channel_id=1, source_target_pairs={{1,0},{2,1},{3,2},{5,4},{6,5},{7,6},{9,8},{10,9},{11,10},{13,12},{... | collective-permute-start | bytes 983048 | tf_op jit(solution)/shard_map/ppermute | solution.py:307
  9.0 3.5 %collective-permute-start.34 = (f32[40,2048]{1,0:T(8,128)S(1)}, f32[40,2048]{1,0:T(8,128)S(1)}, u32[]{:S(2)}, u32[]{:S(2)}) collective-permute-start(f32[40,2048]{1,0:T(8,128)S(1)} %get-tuple-element.88.refs_0_), channel_id=1, source_target_pairs={{0,1},{1,2},{2,3},{4,5},{5,6},{6,7},{8,9},{9,10},{10,11},{12,13},{... | collective-permute-start | bytes 983048 | tf_op jit(solution)/shard_map/ppermute | solution.py:306
  12.5 2.4 %collective-permute-start.35 = (f32[40,2048]{1,0:T(8,128)S(1)}, f32[40,2048]{1,0:T(8,128)S(1)}, u32[]{:S(2)}, u32[]{:S(2)}) collective-permute-start(f32[40,2048]{1,0:T(8,128)S(1)} %get-tuple-element.88.refs_0_), channel_id=1, source_target_pairs={{1,0},{2,1},{3,2},{5,4},{6,5},{7,6},{9,8},{10,9},{11,10},{13,12},{... | collective-permute-start | bytes 983048 | tf_op jit(solution)/shard_map/ppermute | solution.py:307
  14.9 0.7 collective-permute-done.17.refs_1_
  15.7 3.5 %collective-permute-start.19 = (f32[40,2048]{1,0:T(8,128)S(1)}, f32[40,2048]{1,0:T(8,128)S(1)}, u32[]{:S(2)}, u32[]{:S(2)}) collective-permute-start(f32[40,2048]{1,0:T(8,128)S(1)} %collective-permute-done.17.refs_1_), channel_id=1, source_target_pairs={{1,2},{2,3},{5,6},{6,7},{9,10},{10,11},{13,14},{14,15},{17,18},{18... | collective-permute-start | bytes 983048 | tf_op jit(solution)/shard_map/ppermute | solution.py:306
  19.2 2.4 %collective-permute-start.20 = (f32[40,2048]{1,0:T(8,128)S(1)}, f32[40,2048]{1,0:T(8,128)S(1)}, u32[]{:S(2)}, u32[]{:S(2)}) collective-permute-start(f32[40,2048]{1,0:T(8,128)S(1)} %collective-permute-done.18.refs_2_), channel_id=1, source_target_pairs={{1,0},{2,1},{5,4},{6,5},{9,8},{10,9},{13,12},{14,13},{17,16},{18,1... | collective-permute-start | bytes 983048 | tf_op jit(solution)/shard_map/ppermute | solution.py:307
  21.6 0.2 collective-permute-done.34.refs_1_
  21.8 4.4 %collective-permute-start.36 = (f32[40,2048]{1,0:T(8,128)S(1)}, f32[40,2048]{1,0:T(8,128)S(1)}, u32[]{:S(2)}, u32[]{:S(2)}) collective-permute-start(f32[40,2048]{1,0:T(8,128)S(1)} %collective-permute-done.34.refs_1_), channel_id=1, source_target_pairs={{1,2},{2,3},{5,6},{6,7},{9,10},{10,11},{13,14},{14,15},{17,18},{18... | collective-permute-start | bytes 983048 | tf_op jit(solution)/shard_map/ppermute | solution.py:306
  26.2 2.4 %collective-permute-start.37 = (f32[40,2048]{1,0:T(8,128)S(1)}, f32[40,2048]{1,0:T(8,128)S(1)}, u32[]{:S(2)}, u32[]{:S(2)}) collective-permute-start(f32[40,2048]{1,0:T(8,128)S(1)} %collective-permute-done.35.refs_2_), channel_id=1, source_target_pairs={{1,0},{2,1},{5,4},{6,5},{9,8},{10,9},{13,12},{14,13},{17,16},{18,1... | collective-permute-start | bytes 983048 | tf_op jit(solution)/shard_map/ppermute | solution.py:307
  28.6 0.2 collective-permute-done.19
  28.8 4.4 %collective-permute-done.20 = f32[40,2048]{1,0:T(8,128)S(1)} collective-permute-done((f32[40,2048]{1,0:T(8,128)S(1)}, f32[40,2048]{1,0:T(8,128)S(1)}, u32[]{:S(2)}, u32[]{:S(2)}) %collective-permute-start.20) | collective-permute-done | bytes 327712 | tf_op jit(solution)/shard_map/ppermute | solution.py:307
  33.3 2.4 %collective-permute-start.21 = (f32[40,2048]{1,0:T(8,128)S(1)}, f32[40,2048]{1,0:T(8,128)S(1)}, u32[]{:S(2)}, u32[]{:S(2)}) collective-permute-start(f32[40,2048]{1,0:T(8,128)S(1)} %add.266.refs_3_), channel_id=1, source_target_pairs={{2,3},{1,0},{6,7},{5,4},{10,11},{9,8},{14,15},{13,12},{18,19},{17,... | collective-permute-start | bytes 983048 | tf_op jit(solution)/shard_map/ppermute | solution.py:304
  35.7 3.1 %collective-permute-done.37 = f32[40,2048]{1,0:T(8,128)S(1)} collective-permute-done((f32[40,2048]{1,0:T(8,128)S(1)}, f32[40,2048]{1,0:T(8,128)S(1)}, u32[]{:S(2)}, u32[]{:S(2)}) %collective-permute-start.37) | collective-permute-done | bytes 327712 | tf_op jit(solution)/shard_map/ppermute | solution.py:307
  38.8 3.9 %collective-permute-start.38 = (f32[40,2048]{1,0:T(8,128)S(1)}, f32[40,2048]{1,0:T(8,128)S(1)}, u32[]{:S(2)}, u32[]{:S(2)}) collective-permute-start(f32[40,2048]{1,0:T(8,128)S(1)} %add.274.refs_3_), channel_id=1, source_target_pairs={{2,3},{1,0},{6,7},{5,4},{10,11},{9,8},{14,15},{13,12},{18,19},{17,... | collective-permute-start | bytes 983048 | tf_op jit(solution)/shard_map/ppermute | solution.py:304
  42.8 0.1 stack.63.scalar_ref
  42.9 2.4 %collective-permute-done.21.refs_4_ = f32[40,2048]{1,0:T(8,128)S(1)} collective-permute-done((f32[40,2048]{1,0:T(8,128)S(1)}, f32[40,2048]{1,0:T(8,128)S(1)}, u32[]{:S(2)}, u32[]{:S(2)}) %collective-permute-start.21) | collective-permute-done | bytes 327712 | tf_op jit(solution)/shard_map/ppermute | solution.py:304
  45.3 6.0 %shard_map.76 = (f32[64,1024]{1,0:T(8,128)S(1)}, f32[64,1024]{1,0:T(8,128)S(1)}) custom-call(s32[6]{0:T(128)S(1)} %stack.63.scalar_ref, f32[128,128]{1,0:T(8,128)S(1)} %get-tuple-element.99.info_ref, f32[40,2048]{1,0:T(8,128)S(1)} %get-tuple-element.89.refs_0_, f32[40,2048]{1,0:T(8,128)S(1)} %collective-permute-done.17.refs_1_, ...), custom_call_target="tpu_custom_call" | custom-call | flops 1610612736 | bytes 8388608 | tf_op jit(solution)/shard_map/pallas_call | solution.py:182
  51.3 0.1 collective-permute-start.22
  51.4 3.0 %shard_map.78 = (f32[64,1024]{1,0:T(8,128)S(1)}, f32[64,1024]{1,0:T(8,128)S(1)}) custom-call(s32[6]{0:T(128)S(1)} %stack.63.scalar_ref, f32[128,128]{1,0:T(8,128)S(1)} %get-tuple-element.98.info_ref, f32[40,2048]{1,0:T(8,128)S(1)} %get-tuple-element.88.refs_0_, f32[40,2048]{1,0:T(8,128)S(1)} %collective-permute-done.34.refs_1_, ...), custom_call_target="tpu_custom_call" | custom-call | flops 1610612736 | bytes 8388608 | tf_op jit(solution)/shard_map/pallas_call | solution.py:182
  54.4 0.6 collective-permute-start.39
  55.0 1.6 %collective-permute-start.24 = (f32[32,1024]{1,0:T(8,128)S(1)}, f32[32,1024]{1,0:T(8,128)S(1)}, u32[]{:S(2)}, u32[]{:S(2)}) collective-permute-start(f32[32,1024]{1,0:T(8,128)S(1)} %get-tuple-element.96), channel_id=1, source_target_pairs={{0,16},{4,20},{8,24},{12,28},{16,0},{20,4},{24,8},{28,12},{1,17},{... | collective-permute-start | bytes 393224 | tf_op jit(solution)/shard_map/ppermute | solution.py:354
  56.6 1.5 %collective-permute-start.23 = (f32[32,1024]{1,0:T(8,128)S(1)}, f32[32,1024]{1,0:T(8,128)S(1)}, u32[]{:S(2)}, u32[]{:S(2)}) collective-permute-start(f32[32,1024]{1,0:T(8,128)S(1)} %get-tuple-element.97), channel_id=1, source_target_pairs={{0,8},{4,12},{8,0},{12,4},{16,24},{20,28},{24,16},{28,20},{1,9},{5... | collective-permute-start | bytes 393224 | tf_op jit(solution)/shard_map/ppermute | solution.py:354
  58.1 0.6 collective-permute-start.41
  58.7 0.6 collective-permute-start.40
  59.2 1.4 %collective-permute-done.24 = f32[32,1024]{1,0:T(8,128)S(1)} collective-permute-done((f32[32,1024]{1,0:T(8,128)S(1)}, f32[32,1024]{1,0:T(8,128)S(1)}, u32[]{:S(2)}, u32[]{:S(2)}) %collective-permute-start.24) | collective-permute-done | bytes 131104 | tf_op jit(solution)/shard_map/ppermute | solution.py:354
  60.6 2.4 %collective-permute-done.23 = f32[32,1024]{1,0:T(8,128)S(1)} collective-permute-done((f32[32,1024]{1,0:T(8,128)S(1)}, f32[32,1024]{1,0:T(8,128)S(1)}, u32[]{:S(2)}, u32[]{:S(2)}) %collective-permute-start.23) | collective-permute-done | bytes 131104 | tf_op jit(solution)/shard_map/ppermute | solution.py:354
  63.1 1.9 %collective-permute-start.26 = (f32[32,1024]{1,0:T(8,128)S(1)}, f32[32,1024]{1,0:T(8,128)S(1)}, u32[]{:S(2)}, u32[]{:S(2)}) collective-permute-start(f32[32,1024]{1,0:T(8,128)S(1)} %get-tuple-element.61), channel_id=1, source_target_pairs={{0,8},{4,12},{8,0},{12,4},{16,24},{20,28},{24,16},{28,20},{1,9},{5... | collective-permute-start | bytes 393224 | tf_op jit(solution)/shard_map/ppermute | solution.py:354
  65.0 0.4 collective-permute-done.40
  65.4 1.3 %collective-permute-start.42 = (f32[32,1024]{1,0:T(8,128)S(1)}, f32[32,1024]{1,0:T(8,128)S(1)}, u32[]{:S(2)}, u32[]{:S(2)}) collective-permute-start(f32[32,1024]{1,0:T(8,128)S(1)} %get-tuple-element.70), channel_id=1, source_target_pairs={{0,16},{4,20},{8,24},{12,28},{16,0},{20,4},{24,8},{28,12},{1,17},{... | collective-permute-start | bytes 393224 | tf_op jit(solution)/shard_map/ppermute | solution.py:354
  66.7 0.6 collective-permute-start.43
  67.3 1.6 %collective-permute-done.25 = f32[32,1024]{1,0:T(8,128)S(1)} collective-permute-done((f32[32,1024]{1,0:T(8,128)S(1)}, f32[32,1024]{1,0:T(8,128)S(1)}, u32[]{:S(2)}, u32[]{:S(2)}) %collective-permute-start.25) | collective-permute-done | bytes 131104 | tf_op jit(solution)/shard_map/ppermute | solution.py:354
  68.9 0.3 collective-permute-done.26
  69.2 0.1 collective-permute-start.27
  69.3 0.5 collective-permute-start.28
  69.8 0.1 stack.57.scalar_ref
  69.9 0.6 collective-permute-done.42
  70.5 1.2 collective-permute-done.43
  71.7 0.1 collective-permute-start.44
  71.8 0.5 collective-permute-start.45
  72.3 5.8 %shard_map.77 = (f32[32,2048]{1,0:T(8,128)S(1)}, f32[32,2048]{1,0:T(8,128)S(1)}, f32[32,2048]{1,0:T(8,128)S(1)}, f32[32,2048]{1,0:T(8,128)S(1)}) custom-call(s32[6]{0:T(128)S(1)} %stack.57.scalar_ref, f32[128,128]{1,0:T(8,128)S(1)} %get-tuple-element.99.info_ref, f32[1,1024]{1,0:T(1,128)S(1)} %bitcast.68, f32[2048,128]{1,0:T(8,128)S(1)} %copy-done.2, ...), custom_call_target="tpu_custom_call" | custom-call | flops 1610612736 | bytes 8388608 | tf_op jit(solution)/shard_map/pallas_call | solution.py:247
  78.0 1.3 %collective-permute-start.29 = (f32[32,2048]{1,0:T(8,128)S(1)}, f32[32,2048]{1,0:T(8,128)S(1)}, u32[]{:S(2)}, u32[]{:S(2)}) collective-permute-start(f32[32,2048]{1,0:T(8,128)S(1)} %get-tuple-element.65), channel_id=1, source_target_pairs={{0,1},{3,2},{4,5},{7,6},{8,9},{11,10},{12,13},{15,14},{16,17},{19,... | collective-permute-start | bytes 786440 | tf_op jit(solution)/shard_map/ppermute | solution.py:334
  79.3 1.5 %collective-permute-start.31 = (f32[32,2048]{1,0:T(8,128)S(1)}, f32[32,2048]{1,0:T(8,128)S(1)}, u32[]{:S(2)}, u32[]{:S(2)}) collective-permute-start(f32[32,2048]{1,0:T(8,128)S(1)} %get-tuple-element.66), channel_id=1, source_target_pairs={{0,1},{3,2},{4,5},{7,6},{8,9},{11,10},{12,13},{15,14},{16,17},{19,... | collective-permute-start | bytes 786440 | tf_op jit(solution)/shard_map/ppermute | solution.py:334
  80.9 5.8 %shard_map.79 = (f32[32,2048]{1,0:T(8,128)S(1)}, f32[32,2048]{1,0:T(8,128)S(1)}, f32[32,2048]{1,0:T(8,128)S(1)}, f32[32,2048]{1,0:T(8,128)S(1)}) custom-call(s32[6]{0:T(128)S(1)} %stack.57.scalar_ref, f32[128,128]{1,0:T(8,128)S(1)} %get-tuple-element.98.info_ref, f32[1,1024]{1,0:T(1,128)S(1)} %bitcast.69, f32[2048,128]{1,0:T(8,128)S(1)} %copy-done.2, ...), custom_call_target="tpu_custom_call" | custom-call | flops 1610612736 | bytes 8388608 | tf_op jit(solution)/shard_map/pallas_call | solution.py:247
  86.6 1.3 %collective-permute-start.46 = (f32[32,2048]{1,0:T(8,128)S(1)}, f32[32,2048]{1,0:T(8,128)S(1)}, u32[]{:S(2)}, u32[]{:S(2)}) collective-permute-start(f32[32,2048]{1,0:T(8,128)S(1)} %get-tuple-element.75), channel_id=1, source_target_pairs={{0,1},{3,2},{4,5},{7,6},{8,9},{11,10},{12,13},{15,14},{16,17},{19,... | collective-permute-start | bytes 786440 | tf_op jit(solution)/shard_map/ppermute | solution.py:334
  87.9 1.3 %collective-permute-start.48 = (f32[32,2048]{1,0:T(8,128)S(1)}, f32[32,2048]{1,0:T(8,128)S(1)}, u32[]{:S(2)}, u32[]{:S(2)}) collective-permute-start(f32[32,2048]{1,0:T(8,128)S(1)} %get-tuple-element.76), channel_id=1, source_target_pairs={{0,1},{3,2},{4,5},{7,6},{8,9},{11,10},{12,13},{15,14},{16,17},{19,... | collective-permute-start | bytes 786440 | tf_op jit(solution)/shard_map/ppermute | solution.py:334
  89.2 2.8 %collective-permute-start.33 = (f32[32,2048]{1,0:T(8,128)S(1)}, f32[32,2048]{1,0:T(8,128)S(1)}, u32[]{:S(2)}, u32[]{:S(2)}) collective-permute-start(f32[32,2048]{1,0:T(8,128)S(1)} %get-tuple-element.67), channel_id=1, source_target_pairs={{0,1},{1,0},{2,3},{3,2},{4,5},{5,4},{6,7},{7,6},{8,9},{9,8},{10,11... | collective-permute-start | bytes 786440 | tf_op jit(solution)/shard_map/ppermute | solution.py:339
  92.0 0.1 collective-permute-start.50
  92.1 2.6 %collective-permute-done.31 = f32[32,2048]{1,0:T(8,128)S(1)} collective-permute-done((f32[32,2048]{1,0:T(8,128)S(1)}, f32[32,2048]{1,0:T(8,128)S(1)}, u32[]{:S(2)}, u32[]{:S(2)}) %collective-permute-start.31) | collective-permute-done | bytes 262176 | tf_op jit(solution)/shard_map/ppermute | solution.py:334
  94.7 1.3 %collective-permute-start.30 = (f32[32,2048]{1,0:T(8,128)S(1)}, f32[32,2048]{1,0:T(8,128)S(1)}, u32[]{:S(2)}, u32[]{:S(2)}) collective-permute-start(f32[32,2048]{1,0:T(8,128)S(1)} %add.272), channel_id=1, source_target_pairs={{1,3},{2,0},{5,7},{6,4},{9,11},{10,8},{13,15},{14,12},{17,19},{18,... | collective-permute-start | bytes 786440 | tf_op jit(solution)/shard_map/ppermute | solution.py:336
  96.1 4.2 %collective-permute-done.46 = f32[32,2048]{1,0:T(8,128)S(1)} collective-permute-done((f32[32,2048]{1,0:T(8,128)S(1)}, f32[32,2048]{1,0:T(8,128)S(1)}, u32[]{:S(2)}, u32[]{:S(2)}) %collective-permute-start.46) | collective-permute-done | bytes 262176 | tf_op jit(solution)/shard_map/ppermute | solution.py:334
  100.3 1.9 %collective-permute-start.32 = (f32[32,2048]{1,0:T(8,128)S(1)}, f32[32,2048]{1,0:T(8,128)S(1)}, u32[]{:S(2)}, u32[]{:S(2)}) collective-permute-start(f32[32,2048]{1,0:T(8,128)S(1)} %add.273), channel_id=1, source_target_pairs={{1,2},{2,1},{5,6},{6,5},{9,10},{10,9},{13,14},{14,13},{17,18},{18,... | collective-permute-start | bytes 786440 | tf_op jit(solution)/shard_map/ppermute | solution.py:336
  102.2 0.7 add.280
  103.0 3.0 %collective-permute-done.48 = f32[32,2048]{1,0:T(8,128)S(1)} collective-permute-done((f32[32,2048]{1,0:T(8,128)S(1)}, f32[32,2048]{1,0:T(8,128)S(1)}, u32[]{:S(2)}, u32[]{:S(2)}) %collective-permute-start.48) | collective-permute-done | bytes 262176 | tf_op jit(solution)/shard_map/ppermute | solution.py:334
  105.9 1.3 %collective-permute-start.47 = (f32[32,2048]{1,0:T(8,128)}, f32[32,2048]{1,0:T(8,128)S(1)}, u32[]{:S(2)}, u32[]{:S(2)}) collective-permute-start(f32[32,2048]{1,0:T(8,128)} %add.280), channel_id=1, source_target_pairs={{1,3},{2,0},{5,7},{6,4},{9,11},{10,8},{13,15},{14,12},{17,19},{18,... | collective-permute-start | bytes 786440 | tf_op jit(solution)/shard_map/ppermute | solution.py:336
  107.2 0.8 add.281
  108.0 3.6 %collective-permute-done.33.refs_3_ = f32[32,2048]{1,0:T(8,128)S(1)} collective-permute-done((f32[32,2048]{1,0:T(8,128)S(1)}, f32[32,2048]{1,0:T(8,128)S(1)}, u32[]{:S(2)}, u32[]{:S(2)}) %collective-permute-start.33) | collective-permute-done | bytes 262176 | tf_op jit(solution)/shard_map/ppermute | solution.py:339
  111.6 1.9 %collective-permute-start.49 = (f32[32,2048]{1,0:T(8,128)}, f32[32,2048]{1,0:T(8,128)S(1)}, u32[]{:S(2)}, u32[]{:S(2)}) collective-permute-start(f32[32,2048]{1,0:T(8,128)} %add.281), channel_id=1, source_target_pairs={{1,2},{2,1},{5,6},{6,5},{9,10},{10,9},{13,14},{14,13},{17,18},{18,... | collective-permute-start | bytes 786440 | tf_op jit(solution)/shard_map/ppermute | solution.py:336
  113.5 0.7 slice_reduce_fusion
  114.7 1.7 %collective-permute-done.50.refs_7_ = f32[32,2048]{1,0:T(8,128)S(1)} collective-permute-done((f32[32,2048]{1,0:T(8,128)S(1)}, f32[32,2048]{1,0:T(8,128)S(1)}, u32[]{:S(2)}, u32[]{:S(2)}) %collective-permute-start.50) | collective-permute-done | bytes 262176 | tf_op jit(solution)/shard_map/ppermute | solution.py:339
  116.4 4.0 %collective-permute-done.49.refs_6_ = f32[32,2048]{1,0:T(8,128)S(1)} collective-permute-done((f32[32,2048]{1,0:T(8,128)}, f32[32,2048]{1,0:T(8,128)S(1)}, u32[]{:S(2)}, u32[]{:S(2)}) %collective-permute-start.49) | collective-permute-done | bytes 262176 | tf_op jit(solution)/shard_map/ppermute | solution.py:336
  120.5 1.2 shard_map.80
  121.7 0.3 conditional.1
  (44 shorter events, 0.7 us)
Async XLA Ops:
  3.2 12.5 %collective-permute-start.17 = (f32[40,2048]{1,0:T(8,128)S(1)}, f32[40,2048]{1,0:T(8,128)S(1)}, u32[]{:S(2)}, u32[]{:S(2)}) collective-permute-start(f32[40,2048]{1,0:T(8,128)S(1)} %get-tuple-element.89.refs_0_), channel_id=1, source_target_pairs={{0,1},{1,2},{2,3},{4,5},{5,6},{6,7},{8,9},{9,10},{10,11},{12,13},{... | collective-permute-start | bytes 983048 | tf_op jit(solution)/shard_map/ppermute | solution.py:306
  6.7 12.5 %collective-permute-start.18 = (f32[40,2048]{1,0:T(8,128)S(1)}, f32[40,2048]{1,0:T(8,128)S(1)}, u32[]{:S(2)}, u32[]{:S(2)}) collective-permute-start(f32[40,2048]{1,0:T(8,128)S(1)} %get-tuple-element.89.refs_0_), channel_id=1, source_target_pairs={{1,0},{2,1},{3,2},{5,4},{6,5},{7,6},{9,8},{10,9},{11,10},{13,12},{... | collective-permute-start | bytes 983048 | tf_op jit(solution)/shard_map/ppermute | solution.py:307
  9.0 12.7 %collective-permute-start.34 = (f32[40,2048]{1,0:T(8,128)S(1)}, f32[40,2048]{1,0:T(8,128)S(1)}, u32[]{:S(2)}, u32[]{:S(2)}) collective-permute-start(f32[40,2048]{1,0:T(8,128)S(1)} %get-tuple-element.88.refs_0_), channel_id=1, source_target_pairs={{0,1},{1,2},{2,3},{4,5},{5,6},{6,7},{8,9},{9,10},{10,11},{12,13},{... | collective-permute-start | bytes 983048 | tf_op jit(solution)/shard_map/ppermute | solution.py:306
  12.5 13.7 %collective-permute-start.35 = (f32[40,2048]{1,0:T(8,128)S(1)}, f32[40,2048]{1,0:T(8,128)S(1)}, u32[]{:S(2)}, u32[]{:S(2)}) collective-permute-start(f32[40,2048]{1,0:T(8,128)S(1)} %get-tuple-element.88.refs_0_), channel_id=1, source_target_pairs={{1,0},{2,1},{3,2},{5,4},{6,5},{7,6},{9,8},{10,9},{11,10},{13,12},{... | collective-permute-start | bytes 983048 | tf_op jit(solution)/shard_map/ppermute | solution.py:307
  15.7 13.1 %collective-permute-start.19 = (f32[40,2048]{1,0:T(8,128)S(1)}, f32[40,2048]{1,0:T(8,128)S(1)}, u32[]{:S(2)}, u32[]{:S(2)}) collective-permute-start(f32[40,2048]{1,0:T(8,128)S(1)} %collective-permute-done.17.refs_1_), channel_id=1, source_target_pairs={{1,2},{2,3},{5,6},{6,7},{9,10},{10,11},{13,14},{14,15},{17,18},{18... | collective-permute-start | bytes 983048 | tf_op jit(solution)/shard_map/ppermute | solution.py:306
  19.2 14.0 %collective-permute-start.20 = (f32[40,2048]{1,0:T(8,128)S(1)}, f32[40,2048]{1,0:T(8,128)S(1)}, u32[]{:S(2)}, u32[]{:S(2)}) collective-permute-start(f32[40,2048]{1,0:T(8,128)S(1)} %collective-permute-done.18.refs_2_), channel_id=1, source_target_pairs={{1,0},{2,1},{5,4},{6,5},{9,8},{10,9},{13,12},{14,13},{17,16},{18,1... | collective-permute-start | bytes 983048 | tf_op jit(solution)/shard_map/ppermute | solution.py:307
  21.8 13.9 %collective-permute-start.36 = (f32[40,2048]{1,0:T(8,128)S(1)}, f32[40,2048]{1,0:T(8,128)S(1)}, u32[]{:S(2)}, u32[]{:S(2)}) collective-permute-start(f32[40,2048]{1,0:T(8,128)S(1)} %collective-permute-done.34.refs_1_), channel_id=1, source_target_pairs={{1,2},{2,3},{5,6},{6,7},{9,10},{10,11},{13,14},{14,15},{17,18},{18... | collective-permute-start | bytes 983048 | tf_op jit(solution)/shard_map/ppermute | solution.py:306
  26.2 12.6 %collective-permute-start.37 = (f32[40,2048]{1,0:T(8,128)S(1)}, f32[40,2048]{1,0:T(8,128)S(1)}, u32[]{:S(2)}, u32[]{:S(2)}) collective-permute-start(f32[40,2048]{1,0:T(8,128)S(1)} %collective-permute-done.35.refs_2_), channel_id=1, source_target_pairs={{1,0},{2,1},{5,4},{6,5},{9,8},{10,9},{13,12},{14,13},{17,16},{18,1... | collective-permute-start | bytes 983048 | tf_op jit(solution)/shard_map/ppermute | solution.py:307
  33.3 12.0 %collective-permute-start.21 = (f32[40,2048]{1,0:T(8,128)S(1)}, f32[40,2048]{1,0:T(8,128)S(1)}, u32[]{:S(2)}, u32[]{:S(2)}) collective-permute-start(f32[40,2048]{1,0:T(8,128)S(1)} %add.266.refs_3_), channel_id=1, source_target_pairs={{2,3},{1,0},{6,7},{5,4},{10,11},{9,8},{14,15},{13,12},{18,19},{17,... | collective-permute-start | bytes 983048 | tf_op jit(solution)/shard_map/ppermute | solution.py:304
  38.8 12.5 %collective-permute-start.38 = (f32[40,2048]{1,0:T(8,128)S(1)}, f32[40,2048]{1,0:T(8,128)S(1)}, u32[]{:S(2)}, u32[]{:S(2)}) collective-permute-start(f32[40,2048]{1,0:T(8,128)S(1)} %add.274.refs_3_), channel_id=1, source_target_pairs={{2,3},{1,0},{6,7},{5,4},{10,11},{9,8},{14,15},{13,12},{18,19},{17,... | collective-permute-start | bytes 983048 | tf_op jit(solution)/shard_map/ppermute | solution.py:304
  45.3 6.1 %copy-start = (f32[2048,1024]{1,0:T(8,128)S(1)}, f32[2048,1024]{1,0:T(8,128)}, u32[]{:S(2)}) copy-start(f32[2048,1024]{1,0:T(8,128)} %x_ref.3) | copy-start | bytes 25165828
  51.3 3.7 %collective-permute-start.22 = (f32[64,1024]{1,0:T(8,128)S(1)}, f32[64,1024]{1,0:T(8,128)S(1)}, u32[]{:S(2)}, u32[]{:S(2)}) collective-permute-start(f32[64,1024]{1,0:T(8,128)S(1)} %get-tuple-element.59), channel_id=1, source_target_pairs={{0,4},{4,0},{8,12},{12,8},{16,20},{20,16},{24,28},{28,24},{1,5},{5... | collective-permute-start | bytes 786440 | tf_op jit(solution)/shard_map/ppermute | solution.py:347
  54.4 3.7 %collective-permute-start.39 = (f32[64,1024]{1,0:T(8,128)S(1)}, f32[64,1024]{1,0:T(8,128)S(1)}, u32[]{:S(2)}, u32[]{:S(2)}) collective-permute-start(f32[64,1024]{1,0:T(8,128)S(1)} %get-tuple-element.69), channel_id=1, source_target_pairs={{0,4},{4,0},{8,12},{12,8},{16,20},{20,16},{24,28},{28,24},{1,5},{5... | collective-permute-start | bytes 786440 | tf_op jit(solution)/shard_map/ppermute | solution.py:347
  55.0 5.6 %collective-permute-start.24 = (f32[32,1024]{1,0:T(8,128)S(1)}, f32[32,1024]{1,0:T(8,128)S(1)}, u32[]{:S(2)}, u32[]{:S(2)}) collective-permute-start(f32[32,1024]{1,0:T(8,128)S(1)} %get-tuple-element.96), channel_id=1, source_target_pairs={{0,16},{4,20},{8,24},{12,28},{16,0},{20,4},{24,8},{28,12},{1,17},{... | collective-permute-start | bytes 393224 | tf_op jit(solution)/shard_map/ppermute | solution.py:354
  56.6 6.4 %collective-permute-start.23 = (f32[32,1024]{1,0:T(8,128)S(1)}, f32[32,1024]{1,0:T(8,128)S(1)}, u32[]{:S(2)}, u32[]{:S(2)}) collective-permute-start(f32[32,1024]{1,0:T(8,128)S(1)} %get-tuple-element.97), channel_id=1, source_target_pairs={{0,8},{4,12},{8,0},{12,4},{16,24},{20,28},{24,16},{28,20},{1,9},{5... | collective-permute-start | bytes 393224 | tf_op jit(solution)/shard_map/ppermute | solution.py:354
  58.1 14.2 %copy-start.2 = (f32[2048,128]{1,0:T(8,128)S(1)}, f32[2048,128]{1,0:T(8,128)}, u32[]{:S(2)}) copy-start(f32[2048,128]{1,0:T(8,128)} %vectors_ref.5) | copy-start | bytes 3145732
  58.1 14.2 %copy-start.6 = (f32[1024]{0:T(1024)S(1)}, f32[1024]{0:T(1024)}, u32[]{:S(2)}) copy-start(f32[1024]{0:T(1024)} %param.10) | copy-start | bytes 12292
  58.1 6.8 %collective-permute-start.41 = (f32[32,1024]{1,0:T(8,128)S(1)}, f32[32,1024]{1,0:T(8,128)S(1)}, u32[]{:S(2)}, u32[]{:S(2)}) collective-permute-start(f32[32,1024]{1,0:T(8,128)S(1)} %get-tuple-element.92), channel_id=1, source_target_pairs={{0,16},{4,20},{8,24},{12,28},{16,0},{20,4},{24,8},{28,12},{1,17},{... | collective-permute-start | bytes 393224 | tf_op jit(solution)/shard_map/ppermute | solution.py:354
  58.7 6.7 %collective-permute-start.40 = (f32[32,1024]{1,0:T(8,128)S(1)}, f32[32,1024]{1,0:T(8,128)S(1)}, u32[]{:S(2)}, u32[]{:S(2)}) collective-permute-start(f32[32,1024]{1,0:T(8,128)S(1)} %get-tuple-element.93), channel_id=1, source_target_pairs={{0,8},{4,12},{8,0},{12,4},{16,24},{20,28},{24,16},{28,20},{1,9},{5... | collective-permute-start | bytes 393224 | tf_op jit(solution)/shard_map/ppermute | solution.py:354
  63.0 5.9 %collective-permute-start.25 = (f32[32,1024]{1,0:T(8,128)S(1)}, f32[32,1024]{1,0:T(8,128)S(1)}, u32[]{:S(2)}, u32[]{:S(2)}) collective-permute-start(f32[32,1024]{1,0:T(8,128)S(1)} %get-tuple-element.60), channel_id=1, source_target_pairs={{0,16},{4,20},{8,24},{12,28},{16,0},{20,4},{24,8},{28,12},{1,17},{... | collective-permute-start | bytes 393224 | tf_op jit(solution)/shard_map/ppermute | solution.py:354
  63.1 6.1 %collective-permute-start.26 = (f32[32,1024]{1,0:T(8,128)S(1)}, f32[32,1024]{1,0:T(8,128)S(1)}, u32[]{:S(2)}, u32[]{:S(2)}) collective-permute-start(f32[32,1024]{1,0:T(8,128)S(1)} %get-tuple-element.61), channel_id=1, source_target_pairs={{0,8},{4,12},{8,0},{12,4},{16,24},{20,28},{24,16},{28,20},{1,9},{5... | collective-permute-start | bytes 393224 | tf_op jit(solution)/shard_map/ppermute | solution.py:354
  65.4 5.0 %collective-permute-start.42 = (f32[32,1024]{1,0:T(8,128)S(1)}, f32[32,1024]{1,0:T(8,128)S(1)}, u32[]{:S(2)}, u32[]{:S(2)}) collective-permute-start(f32[32,1024]{1,0:T(8,128)S(1)} %get-tuple-element.70), channel_id=1, source_target_pairs={{0,16},{4,20},{8,24},{12,28},{16,0},{20,4},{24,8},{28,12},{1,17},{... | collective-permute-start | bytes 393224 | tf_op jit(solution)/shard_map/ppermute | solution.py:354
  66.7 5.0 %collective-permute-start.43 = (f32[32,1024]{1,0:T(8,128)S(1)}, f32[32,1024]{1,0:T(8,128)S(1)}, u32[]{:S(2)}, u32[]{:S(2)}) collective-permute-start(f32[32,1024]{1,0:T(8,128)S(1)} %get-tuple-element.71), channel_id=1, source_target_pairs={{0,8},{4,12},{8,0},{12,4},{16,24},{20,28},{24,16},{28,20},{1,9},{5... | collective-permute-start | bytes 393224 | tf_op jit(solution)/shard_map/ppermute | solution.py:354
  69.2 3.0 %collective-permute-start.27 = (f32[32,1024]{1,0:T(8,128)S(1)}, f32[32,1024]{1,0:T(8,128)S(1)}, u32[]{:S(2)}, u32[]{:S(2)}) collective-permute-start(f32[32,1024]{1,0:T(8,128)S(1)} %add.270.refs_0_), channel_id=1, source_target_pairs={{0,4},{4,0},{8,12},{12,8},{16,20},{20,16},{24,28},{28,24},{1,5},{5... | collective-permute-start | bytes 393224 | tf_op jit(solution)/shard_map/ppermute | solution.py:358
  69.3 3.0 %collective-permute-start.28 = (f32[32,1024]{1,0:T(8,128)S(1)}, f32[32,1024]{1,0:T(8,128)S(1)}, u32[]{:S(2)}, u32[]{:S(2)}) collective-permute-start(f32[32,1024]{1,0:T(8,128)S(1)} %add.271.refs_1_), channel_id=1, source_target_pairs={{0,4},{4,0},{8,12},{12,8},{16,20},{20,16},{24,28},{28,24},{1,5},{5... | collective-permute-start | bytes 393224 | tf_op jit(solution)/shard_map/ppermute | solution.py:358
  71.7 9.1 %collective-permute-start.44 = (f32[32,1024]{1,0:T(8,128)S(1)}, f32[32,1024]{1,0:T(8,128)S(1)}, u32[]{:S(2)}, u32[]{:S(2)}) collective-permute-start(f32[32,1024]{1,0:T(8,128)S(1)} %add.278.refs_0_), channel_id=1, source_target_pairs={{0,4},{4,0},{8,12},{12,8},{16,20},{20,16},{24,28},{28,24},{1,5},{5... | collective-permute-start | bytes 393224 | tf_op jit(solution)/shard_map/ppermute | solution.py:358
  71.8 9.1 %collective-permute-start.45 = (f32[32,1024]{1,0:T(8,128)S(1)}, f32[32,1024]{1,0:T(8,128)S(1)}, u32[]{:S(2)}, u32[]{:S(2)}) collective-permute-start(f32[32,1024]{1,0:T(8,128)S(1)} %add.279.refs_1_), channel_id=1, source_target_pairs={{0,4},{4,0},{8,12},{12,8},{16,20},{20,16},{24,28},{28,24},{1,5},{5... | collective-permute-start | bytes 393224 | tf_op jit(solution)/shard_map/ppermute | solution.py:358
  78.0 13.9 %collective-permute-start.29 = (f32[32,2048]{1,0:T(8,128)S(1)}, f32[32,2048]{1,0:T(8,128)S(1)}, u32[]{:S(2)}, u32[]{:S(2)}) collective-permute-start(f32[32,2048]{1,0:T(8,128)S(1)} %get-tuple-element.65), channel_id=1, source_target_pairs={{0,1},{3,2},{4,5},{7,6},{8,9},{11,10},{12,13},{15,14},{16,17},{19,... | collective-permute-start | bytes 786440 | tf_op jit(solution)/shard_map/ppermute | solution.py:334
  79.3 15.4 %collective-permute-start.31 = (f32[32,2048]{1,0:T(8,128)S(1)}, f32[32,2048]{1,0:T(8,128)S(1)}, u32[]{:S(2)}, u32[]{:S(2)}) collective-permute-start(f32[32,2048]{1,0:T(8,128)S(1)} %get-tuple-element.66), channel_id=1, source_target_pairs={{0,1},{3,2},{4,5},{7,6},{8,9},{11,10},{12,13},{15,14},{16,17},{19,... | collective-permute-start | bytes 786440 | tf_op jit(solution)/shard_map/ppermute | solution.py:334
  86.6 13.7 %collective-permute-start.46 = (f32[32,2048]{1,0:T(8,128)S(1)}, f32[32,2048]{1,0:T(8,128)S(1)}, u32[]{:S(2)}, u32[]{:S(2)}) collective-permute-start(f32[32,2048]{1,0:T(8,128)S(1)} %get-tuple-element.75), channel_id=1, source_target_pairs={{0,1},{3,2},{4,5},{7,6},{8,9},{11,10},{12,13},{15,14},{16,17},{19,... | collective-permute-start | bytes 786440 | tf_op jit(solution)/shard_map/ppermute | solution.py:334
  87.9 18.0 %collective-permute-start.48 = (f32[32,2048]{1,0:T(8,128)S(1)}, f32[32,2048]{1,0:T(8,128)S(1)}, u32[]{:S(2)}, u32[]{:S(2)}) collective-permute-start(f32[32,2048]{1,0:T(8,128)S(1)} %get-tuple-element.76), channel_id=1, source_target_pairs={{0,1},{3,2},{4,5},{7,6},{8,9},{11,10},{12,13},{15,14},{16,17},{19,... | collective-permute-start | bytes 786440 | tf_op jit(solution)/shard_map/ppermute | solution.py:334
  89.2 22.3 %collective-permute-start.33 = (f32[32,2048]{1,0:T(8,128)S(1)}, f32[32,2048]{1,0:T(8,128)S(1)}, u32[]{:S(2)}, u32[]{:S(2)}) collective-permute-start(f32[32,2048]{1,0:T(8,128)S(1)} %get-tuple-element.67), channel_id=1, source_target_pairs={{0,1},{1,0},{2,3},{3,2},{4,5},{5,4},{6,7},{7,6},{8,9},{9,8},{10,11... | collective-permute-start | bytes 786440 | tf_op jit(solution)/shard_map/ppermute | solution.py:339
  92.0 24.5 %collective-permute-start.50 = (f32[32,2048]{1,0:T(8,128)S(1)}, f32[32,2048]{1,0:T(8,128)S(1)}, u32[]{:S(2)}, u32[]{:S(2)}) collective-permute-start(f32[32,2048]{1,0:T(8,128)S(1)} %get-tuple-element.77), channel_id=1, source_target_pairs={{0,1},{1,0},{2,3},{3,2},{4,5},{5,4},{6,7},{7,6},{8,9},{9,8},{10,11... | collective-permute-start | bytes 786440 | tf_op jit(solution)/shard_map/ppermute | solution.py:339
  94.7 21.7 %collective-permute-start.30 = (f32[32,2048]{1,0:T(8,128)S(1)}, f32[32,2048]{1,0:T(8,128)S(1)}, u32[]{:S(2)}, u32[]{:S(2)}) collective-permute-start(f32[32,2048]{1,0:T(8,128)S(1)} %add.272), channel_id=1, source_target_pairs={{1,3},{2,0},{5,7},{6,4},{9,11},{10,8},{13,15},{14,12},{17,19},{18,... | collective-permute-start | bytes 786440 | tf_op jit(solution)/shard_map/ppermute | solution.py:336
  96.1 25.6 %copy-start.1 = (f32[512]{0:T(512)S(1)}, f32[512]{0:T(512)}, u32[]{:S(2)}) copy-start(f32[512]{0:T(512)} %param.13) | copy-start | bytes 6148
  96.1 25.6 %copy-start.5 = (s32[256]{0:T(256)S(1)}, s32[256]{0:T(256)}, u32[]{:S(2)}) copy-start(s32[256]{0:T(256)} %param.14) | copy-start | bytes 3076
  96.1 25.6 %copy-start.7 = (s32[256]{0:T(256)S(1)}, s32[256]{0:T(256)}, u32[]{:S(2)}) copy-start(s32[256]{0:T(256)} %param.15) | copy-start | bytes 3076
  100.3 16.1 %collective-permute-start.32 = (f32[32,2048]{1,0:T(8,128)S(1)}, f32[32,2048]{1,0:T(8,128)S(1)}, u32[]{:S(2)}, u32[]{:S(2)}) collective-permute-start(f32[32,2048]{1,0:T(8,128)S(1)} %add.273), channel_id=1, source_target_pairs={{1,2},{2,1},{5,6},{6,5},{9,10},{10,9},{13,14},{14,13},{17,18},{18,... | collective-permute-start | bytes 786440 | tf_op jit(solution)/shard_map/ppermute | solution.py:336
  105.9 10.5 %collective-permute-start.47 = (f32[32,2048]{1,0:T(8,128)}, f32[32,2048]{1,0:T(8,128)S(1)}, u32[]{:S(2)}, u32[]{:S(2)}) collective-permute-start(f32[32,2048]{1,0:T(8,128)} %add.280), channel_id=1, source_target_pairs={{1,3},{2,0},{5,7},{6,4},{9,11},{10,8},{13,15},{14,12},{17,19},{18,... | collective-permute-start | bytes 786440 | tf_op jit(solution)/shard_map/ppermute | solution.py:336
  111.6 8.9 %collective-permute-start.49 = (f32[32,2048]{1,0:T(8,128)}, f32[32,2048]{1,0:T(8,128)S(1)}, u32[]{:S(2)}, u32[]{:S(2)}) collective-permute-start(f32[32,2048]{1,0:T(8,128)} %add.281), channel_id=1, source_target_pairs={{1,2},{2,1},{5,6},{6,5},{9,10},{10,9},{13,14},{14,13},{17,18},{18,... | collective-permute-start | bytes 786440 | tf_op jit(solution)/shard_map/ppermute | solution.py:336
